TPU v7x, 128 devices: a whole 4x4x4 slice. The times are simulated.
128 devices in a mesh: station: 32 (over z, y_hi, x), tm: 4 (over y_lo, core).
Axes of the slice: x: 4, y: 4 (y_hi: 2, y_lo: 2; y = y_hi * 2 + y_lo), z: 4, core: 2. Of those that a mesh axis runs over, the one named last changes fastest.
Arguments:
- spectra: bfloat16 [4, 48, 2048, 1024], P('tm', None, 'station'), may hold values from -80 to 80
- counts: int32 [4, 2048], P('tm', 'station'), may hold values from 1 to 48, as said below
- block_ids: int32 [2], replicated, may hold values from 0 to 31
Outputs:
- correlations: bfloat16 [2, 64, 2048, 512], P(None, 'tm', 'station')
Inputs may be any that keep to these rules, and one draw needn't show every extreme that they name: Subwindow s of channel c in window w is live when s < counts[w, c]; later subwindows are gaps. `block_ids`: block b holds channels b * 64 to (b + 1) * 64 - 1.
All inputs are finite; a program needn't handle non-finite values.
Results may differ from a plain program's by a relative error of at most 0.0056.
Values may be sent and summed in bfloat16 or wider, within the bound.
No kernel may reach another device: no remote copies, remote signals or barrier semaphores. Data moves between devices by JAX's collectives and lax.ppermute only.
A program may use at most 320 MiB of HBM per device.

v0:
```python
import math

import jax
import jax.numpy as jnp
from jax import lax
from jax.sharding import PartitionSpec as P

NFFT = 2048
BINS = 512
LAGS = 512
BLOCK = 64
STEPS = 2


eps_value = 1e-06


def from_root(block, axis, owner):
    block = jnp.where(lax.axis_index(axis) == owner, block, jnp.zeros_like(block))
    return lax.psum(block, axis)


def whiten(spectra, counts):
    values = spectra.astype(jnp.float32)
    mean_power = jnp.mean(values * values, axis=-1, keepdims=True)
    subwin_pos = lax.broadcasted_iota(jnp.int32, (spectra.shape[0], spectra.shape[1]), 0)
    valid_mask = (subwin_pos < counts[None, :]).astype(jnp.float32)
    return (values * lax.rsqrt(mean_power + eps_value) * valid_mask[..., None]).astype(jnp.bfloat16)


def lag_table(bin_count, lag_count, length):
    bin_index = lax.broadcasted_iota(jnp.int32, (bin_count, lag_count), 0) + 1
    lag_index = lax.broadcasted_iota(jnp.int32, (bin_count, lag_count), 1) - lag_count // 2
    phase_angle = jnp.mod(bin_index * lag_index, length).astype(jnp.float32) * (
        2.0 * math.pi / length
    )
    norm_scale = 1.0 / math.sqrt(bin_count)
    return jnp.concatenate(
        [jnp.cos(phase_angle) * norm_scale, -jnp.sin(phase_angle) * norm_scale], axis=0
    )


def inverse(cross_spec, lag_rows):
    flat_rows = cross_spec.reshape(-1, cross_spec.shape[-1])
    result = jnp.dot(
        flat_rows, lag_rows, precision=lax.Precision.HIGHEST, preferred_element_type=jnp.float32
    )
    return result.reshape(cross_spec.shape[:-1] + (lag_rows.shape[1],))


def body(spectra, counts, block_ids):
    own_counts = counts[0]
    normed = whiten(spectra[0], own_counts)
    count_marks = own_counts.astype(jnp.bfloat16)
    per_device = normed.shape[1] // BLOCK
    lag_rows = lag_table(BINS, LAGS, NFFT)
    normed_all = normed[None]
    marks_all = count_marks[None]
    receiver_pairs = jnp.stack([normed_all[..., :BINS], normed_all[..., BINS:]])
    receiver_swapped = jnp.stack([normed_all[..., BINS:], normed_all[..., :BINS]])
    receiver_counts = marks_all.astype(jnp.float32)
    sources = []
    for position in range(STEPS):
        block_index = block_ids[position]
        block_spec = normed_all
        block_counts = marks_all
        block_spec, block_counts = (block_spec, block_counts)
        sources.append(
            (
                from_root(block_spec, "station", block_index // per_device),
                from_root(block_counts, "station", block_index // per_device),
            )
        )
    results = []
    for position in range(STEPS):
        block_spec, block_counts = sources[position]
        src_real = block_spec[..., :BINS]
        src_imag = block_spec[..., BINS:]
        real_pairs = jnp.stack([src_real, src_imag])
        imag_pairs = jnp.stack([src_real, -src_imag])
        real_part = jnp.einsum(
            "pwsjk,pwsrk->wjrk", real_pairs, receiver_pairs, preferred_element_type=jnp.float32
        )
        imag_part = jnp.einsum(
            "pwsjk,pwsrk->wjrk", imag_pairs, receiver_swapped, preferred_element_type=jnp.float32
        )
        pair_count = jnp.minimum(
            block_counts.astype(jnp.float32)[:, :, None], receiver_counts[:, None, :]
        )
        cross_all = jnp.concatenate(
            [real_part / pair_count[..., None], imag_part / pair_count[..., None]], axis=-1
        )
        cross_spec = cross_all[0]
        stacked = lax.psum_scatter(
            inverse(cross_spec, lag_rows), "tm", scatter_dimension=0, tiled=True
        )
        results.append(stacked.astype(jnp.bfloat16))
    return jnp.stack(results)


def solution(mesh):
    placed = (P("tm", None, "station", None), P("tm", "station"), P())
    return jax.shard_map(
        body, mesh=mesh, in_specs=placed, out_specs=P(None, "tm", "station", None), check_vma=False
    )
```

profile of v0, /device:TPU:1, one launch (start us, length us, event | category | flops | bytes accessed | tf_op | source)
XLA Modules:
  0.0 945.5 jit_solution(14842765232830361575)
XLA Ops:
  6.5 1.4 fusion.37
  9.3 15.7 %copy.4 = bf16[1,48,64,1024]{2,1,3,0:T(8,128)(2,1)} copy(bf16[1,48,64,1024]{3,2,1,0:T(8,128)(2,1)} %param.3) | data formatting | bytes 12582912 | tf_op args[0]
  25.0 7.9 fusion
  32.9 12.6 %broadcast_select_fusion.1 = (bf16[1,48,64,1024]{2,1,3,0:T(8,128)(2,1)}, bf16[1,48,64,1024]{2,1,3,0:T(8,128)(2,1)S(1)}) fusion(pred[]{:T(512)S(6)} %eq.10, f32[48,64]{1,0:T(8,128)S(1)} %fusion.27, f32[48,64]{1,0:T(8,128)S(1)} %add_rsqrt_fusion, bf16[1,48,64,1024]{2,1,3,0:T(8,128)(2,1)} %copy.4), kind=kLoop, calls=%fused_computation.29 | loop fusion | flops 15728640 | bytes 18898944 | tf_op jit(solution)/shard_map/jit(_where)/select_n | solution.py:19
  45.5 6.9 broadcast_select_fusion
  52.4 1.5 copy-done
  53.9 0.0 all-reduce.4.cloned.1.call-update
  53.9 0.0 reduce-scatter.3.cloned.1.call-start
  54.0 91.9 %all-reduce = (bf16[64]{0:T(256)(128)(2,1)S(1)}, bf16[64]{0:T(256)(128)(2,1)S(1)}) all-reduce(bf16[64]{0:T(256)(128)(2,1)S(1)} %get-tuple-element.25, bf16[64]{0:T(256)(128)(2,1)S(1)} %get-tuple-element.24), channel_id=1, replica_groups=mesh['station'=32,'tm'=4] {'station'}, use_global_device_ids=true, to_apply=%region_5.6 | all-reduce | flops 128 | bytes 512 | tf_op jit(solution)/shard_map/psum | solution.py:20
  145.9 0.1 broadcast_minimum_fusion.1
  146.0 4.2 cosine_multiply_fusion
  150.2 11.3 %slice_bitcast_fusion.1 = (bf16[1,1,48,64,512]{3,2,4,1,0:T(8,128)(2,1)}, bf16[1,1,48,64,512]{3,2,4,1,0:T(8,128)(2,1)}) fusion(bf16[1,48,64,1024]{2,1,3,0:T(8,128)(2,1)} %copy-done), kind=kLoop, calls=%fused_computation.31 | loop fusion | bytes 12582912 | tf_op jit(solution)/shard_map/stack | solution.py:59
  161.5 453.4 %all-reduce.4.cloned.1.call-done = (bf16[1,48,64,1024]{2,1,3,0:T(8,128)(2,1)}, bf16[1,48,64,1024]{2,1,3,0:T(8,128)(2,1)}) async-done(((bf16[1,48,64,1024]{2,1,3,0:T(8,128)(2,1)}, bf16[1,48,64,1024]{2,1,3,0:T(8,128)(2,1)}), (bf16[1,48,64,1024]{2,1,3,0:T(8,128)(2,1)}, bf16[1,48,64,1024]{2,1,3,0:T(8,128)(2,1)})) %all-reduce.4.cloned.1.call-update) | async-done | bytes 12582928 | tf_op jit(solution)/shard_map/psum | solution.py:20
  614.9 12.8 %slice_bitcast_fusion.5 = (bf16[1,1,48,64,512]{3,2,0,4,1:T(8,128)(2,1)}, bf16[1,1,48,64,512]{3,2,4,1,0:T(8,128)(2,1)}, bf16[1,1,48,64,512]{3,2,0,4,1:T(8,128)(2,1)}, bf16[1,1,48,64,512]{3,2,4,1,0:T(8,128)(2,1)}) fusion(bf16[1,48,64,1024]{2,1,3,0:T(8,128)(2,1)} %get-tuple-element.8), kind=kLoop, calls=%fused_computation.37 | loop fusion | flops 1572864 | bytes 18874368 | tf_op jit(solution)/shard_map/stack | solution.py:79
  627.7 15.0 %bitcast_divide_fusion.3 = f32[1,64,64,512]{1,2,3,0:T(8,128)} fusion(f32[64,64]{0,1:T(8,128)S(1)} %get-tuple-element.22, bf16[1,1,48,64,512]{3,2,4,1,0:T(8,128)(2,1)} %get-tuple-element.18, bf16[1,1,48,64,512]{3,2,4,1,0:T(8,128)(2,1)} %get-tuple-element.19, bf16[1,1,48,64,512]{3,2,0,4,1:T(8,128)(2,1)} %get-tuple-element.13, ...), kind=kOutput, calls=%fused_computation.10 | convolution fusion | flops 411041792 | bytes 20987904 | tf_op jit(solution)/shard_map/pwsjk,pwsrk->wjrk/dot_general | solution.py:81
  642.7 15.4 %bitcast_divide_fusion.2 = f32[1,64,64,512]{1,2,3,0:T(8,128)} fusion(f32[64,64]{0,1:T(8,128)S(1)} %get-tuple-element.22, bf16[1,1,48,64,512]{3,2,4,1,0:T(8,128)(2,1)} %get-tuple-element.12, bf16[1,1,48,64,512]{3,2,4,1,0:T(8,128)(2,1)} %get-tuple-element.14, bf16[1,1,48,64,512]{3,2,4,1,0:T(8,128)(2,1)} %get-tuple-element.19, ...), kind=kOutput, calls=%fused_computation.9 | convolution fusion | flops 411041792 | bytes 20987904 | tf_op jit(solution)/shard_map/pwsjk,pwsrk->wjrk/dot_general | solution.py:84
  658.2 22.7 %maximum_bitcast_fusion = f32[64,64,1024]{0,1,2:T(8,128)} fusion(f32[1,64,64,512]{1,2,3,0:T(8,128)} %bitcast_divide_fusion.2, f32[1,64,64,512]{1,2,3,0:T(8,128)} %bitcast_divide_fusion.3), kind=kLoop, calls=%fused_computation | loop fusion | flops 4194304 | bytes 33554432 | tf_op jit(solution)/shard_map/dot_general | solution.py:45
  680.8 26.2 %copy.9 = f32[64,64,1024]{2,1,0:T(8,128)} copy(f32[64,64,1024]{0,1,2:T(8,128)} %maximum_bitcast_fusion) | data formatting | bytes 33554432 | tf_op jit(solution)/shard_map/dot_general | solution.py:45
  707.0 30.4 %fusion.23 = f32[64,64,512]{2,1,0:T(8,128)} fusion(f32[64,64,1024]{2,1,0:T(8,128)} %copy.9, f32[512,512]{1,0:T(8,128)S(1)} %get-tuple-element.21, f32[512,512]{1,0:T(8,128)S(1)} %get-tuple-element.20), kind=kOutput, calls=%fused_computation.45 | convolution fusion | flops 25770328064 | bytes 27262976 | tf_op jit(solution)/shard_map/dot_general | solution.py:45
  737.4 0.0 reduce-scatter.3.cloned.1.call-update
  737.5 0.0 reduce-scatter.5.cloned.1.call-start
  737.5 12.0 %slice_bitcast_fusion.3 = (bf16[1,1,48,64,512]{3,2,4,1,0:T(8,128)(2,1)}, bf16[1,1,48,64,512]{3,2,4,1,0:T(8,128)(2,1)}, bf16[1,1,48,64,512]{3,2,4,1,0:T(8,128)(2,1)}) fusion(bf16[1,48,64,1024]{2,1,3,0:T(8,128)(2,1)} %get-tuple-element.7), kind=kLoop, calls=%fused_computation.35 | loop fusion | flops 1572864 | bytes 15728640 | tf_op jit(solution)/shard_map/stack | solution.py:79
  749.5 15.4 %bitcast_divide_fusion.1 = f32[1,64,64,512]{1,2,3,0:T(8,128)} fusion(f32[64,64]{0,1:T(8,128)S(1)} %get-tuple-element.23, bf16[1,1,48,64,512]{3,2,4,1,0:T(8,128)(2,1)} %get-tuple-element.17, bf16[1,1,48,64,512]{3,2,4,1,0:T(8,128)(2,1)} %get-tuple-element.15, bf16[1,1,48,64,512]{3,2,4,1,0:T(8,128)(2,1)} %get-tuple-element.18, ...), kind=kOutput, calls=%fused_computation.8 | convolution fusion | flops 411041792 | bytes 20987904 | tf_op jit(solution)/shard_map/pwsjk,pwsrk->wjrk/dot_general | solution.py:81
  765.0 15.4 %bitcast_divide_fusion = f32[1,64,64,512]{1,2,3,0:T(8,128)} fusion(f32[64,64]{0,1:T(8,128)S(1)} %get-tuple-element.23, bf16[1,1,48,64,512]{3,2,4,1,0:T(8,128)(2,1)} %get-tuple-element.17, bf16[1,1,48,64,512]{3,2,4,1,0:T(8,128)(2,1)} %get-tuple-element.16, bf16[1,1,48,64,512]{3,2,4,1,0:T(8,128)(2,1)} %get-tuple-element.19, ...), kind=kOutput, calls=%fused_computation.7 | convolution fusion | flops 411041792 | bytes 20987904 | tf_op jit(solution)/shard_map/pwsjk,pwsrk->wjrk/dot_general | solution.py:84
  780.4 22.8 %maximum_bitcast_fusion.1 = f32[64,64,1024]{0,1,2:T(8,128)} fusion(f32[1,64,64,512]{1,2,3,0:T(8,128)} %bitcast_divide_fusion, f32[1,64,64,512]{1,2,3,0:T(8,128)} %bitcast_divide_fusion.1), kind=kLoop, calls=%fused_computation.1 | loop fusion | flops 4194304 | bytes 33554432 | tf_op jit(solution)/shard_map/dot_general | solution.py:45
  803.2 26.5 %copy.14 = f32[64,64,1024]{2,1,0:T(8,128)} copy(f32[64,64,1024]{0,1,2:T(8,128)} %maximum_bitcast_fusion.1) | data formatting | bytes 33554432 | tf_op jit(solution)/shard_map/dot_general | solution.py:45
  829.7 30.7 %fusion.22 = f32[64,64,512]{2,1,0:T(8,128)} fusion(f32[64,64,1024]{2,1,0:T(8,128)} %copy.14, f32[512,512]{1,0:T(8,128)S(1)} %get-tuple-element.21, f32[512,512]{1,0:T(8,128)S(1)} %get-tuple-element.20), kind=kOutput, calls=%fused_computation.44 | convolution fusion | flops 25770328064 | bytes 27262976 | tf_op jit(solution)/shard_map/dot_general | solution.py:45
  860.4 0.0 reduce-scatter.3.cloned.1.call-done
  860.4 1.7 convert_bitcast_fusion.1
  862.2 73.3 %reduce-scatter.5.cloned.1.call-done = f32[16,64,512]{2,1,0:T(8,128)} async-done(((f32[64,64,512]{2,1,0:T(8,128)}), f32[16,64,512]{2,1,0:T(8,128)}) %reduce-scatter.5.cloned.1.call-update) | async-done | bytes 2097168 | tf_op jit(solution)/shard_map/reduce_scatter | solution.py:94
  935.5 1.7 convert_bitcast_fusion
  937.2 1.5 pad_maximum_fusion.2
  (12 shorter events, 0.1 us)
Async XLA Ops:
  6.5 608.4 %all-reduce.4.cloned.1.call-start = ((), (), s32[]{:S(2)}) async-start(), calls=%async_computation.4 | async-start | bytes 50331648 | tf_op jit(solution)/shard_map/psum | solution.py:20
  9.3 23.6 %copy-start.1 = (s32[1,64]{1,0:T(1,128)S(1)}, s32[1,64]{1,0:T(1,128)}, u32[]{:S(2)}) copy-start(s32[1,64]{1,0:T(1,128)} %param.4) | copy-start | bytes 772
  45.5 8.4 copy-start
  53.9 806.5 %reduce-scatter.3.cloned.1.call-start = ((), (), s32[]{:S(2)}) async-start(), calls=%async_computation.2 | async-start | bytes 10485760 | tf_op jit(solution)/shard_map/reduce_scatter | solution.py:94
  737.5 198.0 %reduce-scatter.5.cloned.1.call-start = ((), (), s32[]{:S(2)}) async-start(), calls=%async_computation.3 | async-start | bytes 10485760 | tf_op jit(solution)/shard_map/reduce_scatter | solution.py:94
Sparse Core Ops, SparseCore 0:
  54.0 560.8 all-reduce.3
  737.6 75.0 reduce-scatter.2
  860.5 74.9 reduce-scatter.4
where the time goes:
time: 951 us; the launch traced here: 946 us
  waiting for transfers between devices  527 us (55%)
  matrix products  122 us (13%)
  other arithmetic  107 us (11%)
  blocking collectives  91.9 us (10%)
  local copies, waits for them, and re-layouts  82.6 us (9%)
  between operations  14.8 us (2%)
    psum x1, waiting for transfers between devices, from_root(): return lax.psum(block, axis)  453 us
    psum x1, blocking collectives, from_root(): return lax.psum(block, axis)  91.9 us
    reduce_scatter x2, waiting for transfers between devices, body(): lax.psum_scatter(inverse(cross_spec, lag_rows), 'tm', scatter_dimension=0...  73.4 us
    dot_general x2, matrix products, inverse(): jnp.dot(flat_rows, lag_rows, precision=lax.Precision.HIGHEST, preferred_e...  61.1 us
    dot_general x2, local copies, waits for them, and re-layouts, inverse(): jnp.dot(flat_rows, lag_rows, precision=lax.Precision.HIGHEST, preferred_e...  52.7 us
    dot_general x2, other arithmetic, inverse(): jnp.dot(flat_rows, lag_rows, precision=lax.Precision.HIGHEST, preferred_e...  45.5 us
    dot_general x2, matrix products, body(): jnp.einsum('pwsjk,pwsrk->wjrk', imag_pairs, receiver_swapped, preferred_e...  30.9 us
    dot_general x2, matrix products, body(): jnp.einsum('pwsjk,pwsrk->wjrk', real_pairs, receiver_pairs, preferred_ele...  30.4 us
  transfers between devices with their start and end apart: 3, of which 2 were waited for; matrix products, arithmetic and copies ran while one was open for 15% of the time, Pallas kernels for 0%

commit v1 on v0

v1 whole, which is shorter than its diff:
```python
import functools, math
import jax
import jax.numpy as jnp
import numpy as np
from jax import lax
from jax.experimental import pallas as pl
from jax.experimental.pallas import tpu as pltpu

NFFT, BINS, LAGS, BLOCK, STEPS, SUB = 2048, 512, 512, 64, 2, 48
EPS = 1e-6
F32, BF = jnp.float32, jnp.bfloat16
VMEM = pltpu.CompilerParams(vmem_limit_bytes=56 * 2**20)
SB = 16


def whiten_kernel(spec, counts, own, rot, work):
    base = pl.program_id(0) * SB
    live = counts[...]

    def one(s, _):
        v = spec[s].astype(F32)
        power = jnp.mean(v * v, axis=-1, keepdims=True)
        mask = (base + s < live).astype(F32)
        n = v * lax.rsqrt(power + EPS) * mask
        m = jnp.concatenate([n[:, :BINS], n[:, BINS:]], axis=0)
        work[:, s, :] = m.T
        return 0

    for s in range(SB):
        one(s, 0)
    whole = work[...]
    own[...] = whole.astype(BF)
    lane = lax.broadcasted_iota(jnp.int32, (1, 1, 128), 2)
    turned = pltpu.roll(whole, 64, 2)
    rot[...] = jnp.where(lane < 64, turned, -turned).astype(BF)


def whiten(spectra, counts):
    return pl.pallas_call(
        whiten_kernel,
        grid=(SUB // SB,),
        in_specs=[
            pl.BlockSpec((SB, BLOCK, 2 * BINS), lambda i: (i, 0, 0)),
            pl.BlockSpec((BLOCK, 1), lambda i: (0, 0)),
        ],
        out_specs=[pl.BlockSpec((BINS, SB, 128), lambda i: (0, i, 0))] * 2,
        out_shape=[jax.ShapeDtypeStruct((BINS, SUB, 128), BF)] * 2,
        scratch_shapes=[pltpu.VMEM((BINS, SB, 128), F32)],
        compiler_params=VMEM,
        name="whiten",
    )(spectra, counts[:, None])


KC = 32


def corr_kernel(src, own, rot, inv, table, out, cross, rows):
    step = pl.program_id(0)
    for k in range(KC):
        x = src[k].T
        h = jnp.dot(x[:BLOCK], own[k], preferred_element_type=F32)
        h += jnp.dot(x[BLOCK:], rot[k], preferred_element_type=F32)
        cross[k] = h
    for j in range(BLOCK):
        rows[j, pl.ds(pl.multiple_of(step * KC, KC), KC), :] = cross[:, j, :].astype(BF)

    @pl.when(step == BINS // KC - 1)
    def _():
        def quad(q, _):
            a = [rows[4 * q + i] for i in range(4)]
            rhs = jnp.concatenate(
                [
                    jnp.concatenate([v[:, :BLOCK] for v in a], axis=1),
                    jnp.concatenate([v[:, BLOCK:] for v in a], axis=1),
                ],
                axis=0,
            )
            y = jnp.dot(table[...], rhs, preferred_element_type=F32)
            col = pl.multiple_of((q % 4) * 256, 256)
            out[q // 4, :, pl.ds(col, 256)] = (y * inv[q // 4, :, pl.ds(col, 256)]).astype(BF)
            return 0

        lax.fori_loop(0, BLOCK // 4, quad, 0)


def corr(src, own, rot, inv, table):
    blk = pl.BlockSpec((KC, SUB, 128), lambda i: (i, 0, 0))
    return pl.pallas_call(
        corr_kernel,
        grid=(BINS // KC,),
        in_specs=[
            blk,
            blk,
            blk,
            pl.BlockSpec((4, 1, 1024), lambda i: (0, 0, 0)),
            pl.BlockSpec((LAGS, 2 * BINS), lambda i: (0, 0)),
        ],
        out_specs=pl.BlockSpec((4, LAGS, 1024), lambda i: (0, 0, 0)),
        out_shape=jax.ShapeDtypeStruct((4, LAGS, 1024), BF),
        scratch_shapes=[
            pltpu.VMEM((KC, BLOCK, 128), F32),
            pltpu.VMEM((BLOCK, BINS, 128), BF),
        ],
        compiler_params=VMEM,
        name="corr",
    )(src, own, rot, inv, table)


def finish_kernel(a, b, out):
    out[0] = (a[0].astype(F32) + b[0].astype(F32)).T.astype(BF)


def finish(a, b):
    n = a.shape[0]
    blk = pl.BlockSpec((1, LAGS, 256), lambda i, j: (i, 0, j))
    return pl.pallas_call(
        finish_kernel,
        grid=(n, 4),
        in_specs=[blk, blk],
        out_specs=pl.BlockSpec((1, 256, LAGS), lambda i, j: (i, j, 0)),
        out_shape=jax.ShapeDtypeStruct((n, 1024, LAGS), BF),
        compiler_params=VMEM,
        name="finish",
    )(a, b)


def lag_table():
    k = np.arange(1, BINS + 1)[None, :]
    tau = np.arange(LAGS)[:, None] - LAGS // 2
    ph = ((k * tau) % NFFT) * (2 * np.pi / NFFT)
    w = np.concatenate([np.cos(ph), -np.sin(ph)], axis=1) / math.sqrt(BINS)
    return jnp.asarray(w, BF)


def pair_sum(lag):
    tm = lax.axis_index("tm")
    low, core = tm // 2, tm % 2
    lag = lag.reshape(2, 2, LAGS, 1024)
    away = lax.dynamic_index_in_dim(lag, 1 - core, 1, keepdims=False)
    keep = lax.dynamic_index_in_dim(lag, core, 1, keepdims=False)
    got = lax.ppermute(away, "tm", [(t, t ^ 1) for t in range(4)])
    both = (keep.astype(F32) + got.astype(F32)).astype(BF)
    away = lax.dynamic_index_in_dim(both, 1 - low, 0, keepdims=False)
    keep = lax.dynamic_index_in_dim(both, low, 0, keepdims=False)
    got = lax.ppermute(away, "tm", [(t, t ^ 2) for t in range(4)])
    return keep, got


def body(spectra, counts, block_ids):
    counts = counts[0]
    table = lag_table()
    all_counts = lax.all_gather(counts, "station")
    own, rot = whiten(spectra[0], counts)
    pieces = lax.all_to_all(own.reshape(32, 16, SUB, 128), "station", 0, 0)
    parts = []
    for i in range(STEPS):
        block = block_ids[i]
        piece = lax.dynamic_index_in_dim(pieces, block, 0, keepdims=False)
        src = lax.all_gather(piece, "station").reshape(BINS, SUB, 128)
        src_counts = lax.dynamic_index_in_dim(all_counts, block, 0, keepdims=False)
        inv = 1.0 / jnp.minimum(src_counts[:, None], counts[None, :]).astype(F32)
        lag = corr(src, own, rot, inv.reshape(4, 1, 1024), table)
        parts.append(pair_sum(lag))
    keep = jnp.stack([p[0] for p in parts])
    got = jnp.stack([p[1] for p in parts])
    return finish(keep, got).reshape(STEPS, 16, BLOCK, LAGS)


def solution(mesh):
    from jax.sharding import PartitionSpec as P

    return jax.shard_map(
        body,
        mesh=mesh,
        in_specs=(P("tm", None, "station", None), P("tm", "station"), P()),
        out_specs=P(None, "tm", "station", None),
        check_vma=False,
    )
```

time: 951 us -> 418 us (0.44)
  waiting for transfers between devices: 527 us -> 193 us
  matrix products: 122 us -> 0 us
  other arithmetic: 107 us -> 8.78 us
  Pallas kernels: 0 us -> 92.8 us
  local copies, waits for them, and re-layouts: 82.6 us -> 11.5 us
  starting transfers between devices: 0.09 us -> 14.6 us
  blocking collectives: 91.9 us -> 79.6 us
    psum x1 -> x0, waiting for transfers between devices: 453 us -> none  [from_root(): return lax.psum(block, axis)]
    dot_general x6 -> x0, matrix products: 122 us -> none  [the longest x2 61.1 us: inverse(): jnp.dot(flat_rows, lag_rows, precision=lax.Precision.HIGHEST, preferred_e...]
    pallas_call x0 -> x4, Pallas kernels: none -> 92.8 us  [the longest x2 69.4 us: corr(): pl.pallas_call(corr_kernel, grid=(BINS // KC,), in_specs=[blk, blk, blk,...]
    psum x1 -> x0, blocking collectives: 91.9 us -> none  [from_root(): return lax.psum(block, axis)]
    all_to_all x0 -> x1, waiting for transfers between devices: none -> 80.4 us  [body(): pieces = lax.all_to_all(own.reshape(32, 16, SUB, 128), 'station', 0, 0)]
    all_gather x0 -> x1, blocking collectives: none -> 79.6 us  [body(): all_counts = lax.all_gather(counts, 'station')]
    reduce_scatter x2 -> x0, waiting for transfers between devices: 73.4 us -> none  [body(): lax.psum_scatter(inverse(cross_spec, lag_rows), 'tm', scatter_dimension=0...]
    all_gather x0 -> x2, waiting for transfers between devices: none -> 70.6 us  [body(): src = lax.all_gather(piece, 'station').reshape(BINS, SUB, 128)]
  transfers between devices with their start and end apart: 3 -> 7, of which waited for: 2 -> 6; matrix products, arithmetic and copies ran while one was open for 15% -> 4% of each run, Pallas kernels for 0% -> 17%
where the time goes in v1:
time: 418 us
  waiting for transfers between devices  193 us (46%)
  Pallas kernels  92.8 us (22%)
  blocking collectives  79.6 us (19%)
  between operations  17.2 us (4%)
  starting transfers between devices  14.6 us (3%)
  local copies, waits for them, and re-layouts  11.5 us (3%)
  other arithmetic  8.78 us (2%)
    all_to_all x1, waiting for transfers between devices, body(): pieces = lax.all_to_all(own.reshape(32, 16, SUB, 128), 'station', 0, 0)  80.4 us
    all_gather x1, blocking collectives, body(): all_counts = lax.all_gather(counts, 'station')  79.6 us
    all_gather x2, waiting for transfers between devices, body(): src = lax.all_gather(piece, 'station').reshape(BINS, SUB, 128)  70.6 us
    pallas_call x2, Pallas kernels, corr(): pl.pallas_call(corr_kernel, grid=(BINS // KC,), in_specs=[blk, blk, blk,...  69.4 us
    ppermute x2, waiting for transfers between devices, pair_sum(): got = lax.ppermute(away, 'tm', [(t, t ^ 2) for t in range(4)])  40.7 us
    pallas_call x1, Pallas kernels, whiten(): pl.pallas_call(whiten_kernel, grid=(SUB // SB,), in_specs=[pl.BlockSpec((...  17 us
    all_to_all x1, starting transfers between devices, body(): pieces = lax.all_to_all(own.reshape(32, 16, SUB, 128), 'station', 0, 0)  11.6 us
  transfers between devices with their start and end apart: 7, of which 6 were waited for; matrix products, arithmetic and copies ran while one was open for 4% of the time, Pallas kernels for 17%

profile of v1, /device:TPU:1, one launch (start us, length us, event | category | flops | bytes accessed | tf_op | source)
XLA Modules:
  0.0 417.8 jit_solution(9233064936264950951)
XLA Ops:
  6.5 1.4 copy.9.counts
  7.9 17.0 %whiten.1 = (bf16[512,48,128]{2,1,0:T(8,128)(2,1)}, bf16[512,48,128]{2,1,0:T(8,128)(2,1)}) custom-call(bf16[48,64,1024]{2,1,0:T(8,128)(2,1)} %bitcast.37, s32[64,1]{1,0:T(8,128)} %copy.9.counts), custom_call_target="tpu_custom_call" | custom-call | tf_op jit(solution)/shard_map/whiten/pallas_call | solution.py:39
  24.9 11.6 %all-to-all-start = ((bf16[32,16,48,128]{3,2,1,0:T(8,128)(2,1)}), bf16[32,16,48,128]{3,2,1,0:T(8,128)(2,1)}, u32[]{:S(2)}, u32[]{:S(2)}) async-start(bf16[32,16,48,128]{3,2,1,0:T(8,128)(2,1)} %bitcast.32), calls=%async_computation | async-start | bytes 12582912 | tf_op jit(solution)/shard_map/all_to_all | solution.py:154
  36.5 0.6 fusion.4
  40.7 80.4 %all-to-all-done = bf16[32,16,48,128]{3,2,1,0:T(8,128)(2,1)} async-done(((bf16[32,16,48,128]{3,2,1,0:T(8,128)(2,1)}), bf16[32,16,48,128]{3,2,1,0:T(8,128)(2,1)}, u32[]{:S(2)}, u32[]{:S(2)}) %all-to-all-start) | async-done | bytes 6291488 | tf_op jit(solution)/shard_map/all_to_all | solution.py:154
  121.2 1.8 constant_dynamic-slice_fusion.5
  123.0 0.7 all-gather.6.cloned.1.call-update
  123.7 79.6 %all-gather = s32[32,1,64]{2,1,0:T(1,128)S(1)} all-gather(s32[1,1,64]{2,1,0:T(1,128)S(1)} %bitcast.43), channel_id=1, replica_groups=mesh['station'=32,'tm'=4] {'station'}, dimensions={0}, use_global_device_ids=true | all-gather | bytes 8448 | tf_op jit(solution)/shard_map/all_gather | solution.py:152
  203.5 0.1 min.54
  203.8 0.1 min.62
  203.9 0.7 convert_divide_fusion.1
  204.6 16.6 %all-gather.4.cloned.1.call-done = bf16[32,16,48,128]{3,2,1,0:T(8,128)(2,1)} async-done(((bf16[1,16,48,128]{3,2,1,0:T(8,128)(2,1)}), bf16[32,16,48,128]{3,2,1,0:T(8,128)(2,1)}) %all-gather.4.cloned.1.call-update) | async-done | bytes 6291472 | tf_op jit(solution)/shard_map/all_gather | solution.py:159
  221.2 34.6 %corr.2 = bf16[4,512,1024]{2,1,0:T(8,128)(2,1)} custom-call(bf16[512,48,128]{2,1,0:T(8,128)(2,1)} %bitcast.39, bf16[512,48,128]{2,1,0:T(8,128)(2,1)} %get-tuple-element.7.own, bf16[512,48,128]{2,1,0:T(8,128)(2,1)} %get-tuple-element.8.rot, f32[4,1,1024]{2,1,0:T(1,128)} %get-tuple-element.17.inv, bf16[512,1024]{1,0:T(8,128)(2,1)} %constant.73.clone.table), custom_call_target="tpu_custom_call" | custom-call | tf_op jit(solution)/shard_map/corr/pallas_call | solution.py:88
  255.9 3.1 dynamic-slice_bitcast_fusion.1
  259.0 1.1 collective-permute-start
  260.1 53.9 %all-gather.6.cloned.1.call-done = bf16[32,16,48,128]{3,2,1,0:T(8,128)(2,1)} async-done(((bf16[1,16,48,128]{3,2,1,0:T(8,128)(2,1)}), bf16[32,16,48,128]{3,2,1,0:T(8,128)(2,1)}) %all-gather.6.cloned.1.call-update) | async-done | bytes 6291472 | tf_op jit(solution)/shard_map/all_gather | solution.py:159
  314.0 34.7 %corr.3 = bf16[4,512,1024]{2,1,0:T(8,128)(2,1)} custom-call(bf16[512,48,128]{2,1,0:T(8,128)(2,1)} %bitcast.38, bf16[512,48,128]{2,1,0:T(8,128)(2,1)} %get-tuple-element.7.own, bf16[512,48,128]{2,1,0:T(8,128)(2,1)} %get-tuple-element.8.rot, f32[4,1,1024]{2,1,0:T(1,128)} %get-tuple-element.18.inv, bf16[512,1024]{1,0:T(8,128)(2,1)} %constant.73.clone.table), custom_call_target="tpu_custom_call" | custom-call | tf_op jit(solution)/shard_map/corr/pallas_call | solution.py:88
  348.7 3.1 dynamic-slice_bitcast_fusion
  351.8 1.1 collective-permute-start.1
  352.9 2.5 fusion.1
  355.5 0.2 dynamic-slice_bitcast_fusion.3
  355.6 0.4 collective-permute-start.2
  356.0 1.0 collective-permute-done.1
  357.0 0.6 copy-done
  357.6 2.6 fusion
  360.2 0.2 dynamic-slice_bitcast_fusion.2
  360.4 0.4 collective-permute-start.3
  360.8 1.5 pad_maximum_fusion.a
  362.3 18.2 %collective-permute-done.2 = bf16[512,1024]{1,0:T(8,128)(2,1)S(1)} collective-permute-done((bf16[512,1024]{1,0:T(8,128)(2,1)S(1)}, bf16[512,1024]{1,0:T(8,128)(2,1)S(1)}, u32[]{:S(2)}, u32[]{:S(2)}) %collective-permute-start.2) | collective-permute-done | bytes 1048608 | tf_op jit(solution)/shard_map/ppermute | solution.py:145
  380.5 22.5 %collective-permute-done.3 = bf16[512,1024]{1,0:T(8,128)(2,1)S(1)} collective-permute-done((bf16[512,1024]{1,0:T(8,128)(2,1)S(1)}, bf16[512,1024]{1,0:T(8,128)(2,1)S(1)}, u32[]{:S(2)}, u32[]{:S(2)}) %collective-permute-start.3) | collective-permute-done | bytes 1048608 | tf_op jit(solution)/shard_map/ppermute | solution.py:145
  403.0 1.5 pad_maximum_fusion.1.b
  404.5 6.5 %finish.1 = bf16[2,1024,512]{2,1,0:T(8,128)(2,1)} custom-call(bf16[2,512,1024]{2,1,0:T(8,128)(2,1)} %pad_maximum_fusion.a, bf16[2,512,1024]{2,1,0:T(8,128)(2,1)} %pad_maximum_fusion.1.b), custom_call_target="tpu_custom_call" | custom-call | tf_op jit(solution)/shard_map/finish/pallas_call | solution.py:116
  (16 shorter events, 0.5 us)
Async XLA Ops:
  24.8 11.7 %copy-start.2 = (s32[2]{0:T(128)S(1)}, s32[2]{0:T(128)}, u32[]{:S(2)}) copy-start(s32[2]{0:T(128)} %param.6) | copy-start | bytes 28
  24.8 98.9 %copy-start.1 = (s32[1,64]{1,0:T(1,128)S(1)}, s32[1,64]{1,0:T(1,128)}, u32[]{:S(2)}) copy-start(s32[1,64]{1,0:T(1,128)} %param.5) | copy-start | bytes 772
  24.9 96.3 %all-to-all-start = ((bf16[32,16,48,128]{3,2,1,0:T(8,128)(2,1)}), bf16[32,16,48,128]{3,2,1,0:T(8,128)(2,1)}, u32[]{:S(2)}, u32[]{:S(2)}) async-start(bf16[32,16,48,128]{3,2,1,0:T(8,128)(2,1)} %bitcast.32), calls=%async_computation | async-start | bytes 12582912 | tf_op jit(solution)/shard_map/all_to_all | solution.py:154
  36.4 184.8 %all-gather.4.cloned.1.call-start = ((), (), s32[]{:S(2)}) async-start(), calls=%async_computation.1 | async-start | bytes 6488064 | tf_op jit(solution)/shard_map/all_gather | solution.py:159
  123.0 191.0 %all-gather.6.cloned.1.call-start = ((), (), s32[]{:S(2)}) async-start(), calls=%async_computation.2 | async-start | bytes 6488064 | tf_op jit(solution)/shard_map/all_gather | solution.py:159
  259.0 93.9 %collective-permute-start = (bf16[2,512,1024]{2,1,0:T(8,128)(2,1)}, bf16[2,512,1024]{2,1,0:T(8,128)(2,1)S(1)}, u32[]{:S(2)}, u32[]{:S(2)}) collective-permute-start(bf16[2,512,1024]{2,1,0:T(8,128)(2,1)} %dynamic-slice_bitcast_fusion.1), channel_id=1, source_target_pairs={{0,1},{1,0},{2,3},{3,2},{4,5},{5,4},{6,7},{7,6},{8,9},{9,8},{10,11... | collective-permute-start | bytes 6291464 | tf_op jit(solution)/shard_map/ppermute | solution.py:141
  351.8 5.2 %collective-permute-start.1 = (bf16[2,512,1024]{2,1,0:T(8,128)(2,1)}, bf16[2,512,1024]{2,1,0:T(8,128)(2,1)}, u32[]{:S(2)}, u32[]{:S(2)}) collective-permute-start(bf16[2,512,1024]{2,1,0:T(8,128)(2,1)} %dynamic-slice_bitcast_fusion), channel_id=1, source_target_pairs={{0,1},{1,0},{2,3},{3,2},{4,5},{5,4},{6,7},{7,6},{8,9},{9,8},{10,11... | collective-permute-start | bytes 6291464 | tf_op jit(solution)/shard_map/ppermute | solution.py:141
  355.4 2.2 copy-start
  355.6 24.9 %collective-permute-start.2 = (bf16[512,1024]{1,0:T(8,128)(2,1)S(1)}, bf16[512,1024]{1,0:T(8,128)(2,1)S(1)}, u32[]{:S(2)}, u32[]{:S(2)}) collective-permute-start(bf16[512,1024]{1,0:T(8,128)(2,1)S(1)} %get-tuple-element.13), channel_id=1, source_target_pairs={{0,2},{1,3},{2,0},{3,1},{4,6},{5,7},{6,4},{7,5},{8,10},{9,11},{10,... | collective-permute-start | bytes 3145736 | tf_op jit(solution)/shard_map/ppermute | solution.py:145
  360.4 42.6 %collective-permute-start.3 = (bf16[512,1024]{1,0:T(8,128)(2,1)S(1)}, bf16[512,1024]{1,0:T(8,128)(2,1)S(1)}, u32[]{:S(2)}, u32[]{:S(2)}) collective-permute-start(bf16[512,1024]{1,0:T(8,128)(2,1)S(1)} %get-tuple-element.15), channel_id=1, source_target_pairs={{0,2},{1,3},{2,0},{3,1},{4,6},{5,7},{6,4},{7,5},{8,10},{9,11},{10,... | collective-permute-start | bytes 3145736 | tf_op jit(solution)/shard_map/ppermute | solution.py:145
Sparse Core Ops, SparseCore 0:
  123.1 98.0 all-gather.3
  224.2 89.8 all-gather.5

commit v2 on v1

v2 whole, which is shorter than its diff:
```python
import math

import jax
import jax.numpy as jnp
import numpy as np
from jax import lax
from jax.experimental import pallas as pl
from jax.experimental.pallas import tpu as pltpu

NFFT, BINS, LAGS, BLOCK, STEPS, SUB = 2048, 512, 512, 64, 2, 48
EPS = 1e-6
F32, BF = jnp.float32, jnp.bfloat16
VMEM = pltpu.CompilerParams(vmem_limit_bytes=56 * 2**20)
SB = 16
KC = 64
CHUNKS = BINS // KC
HALF = BINS // 2


def whiten_kernel(spec, counts, own, work):
    base = pl.program_id(0) * SB
    live = counts[...]
    for s in range(SB):
        v = spec[s].astype(F32)
        power = jnp.mean(v * v, axis=-1, keepdims=True)
        mask = (base + s < live).astype(F32)
        n = v * lax.rsqrt(power + EPS) * mask
        work[s] = jnp.concatenate([n[:, :BINS], n[:, BINS:]], axis=0).T
    own[...] = jnp.swapaxes(work[...], 0, 1).astype(BF)


def whiten(spectra, counts):
    return pl.pallas_call(
        whiten_kernel,
        grid=(SUB // SB,),
        in_specs=[
            pl.BlockSpec((SB, BLOCK, 2 * BINS), lambda i: (i, 0, 0)),
            pl.BlockSpec((BLOCK, 1), lambda i: (0, 0)),
        ],
        out_specs=pl.BlockSpec((BINS, SB, 128), lambda i: (0, i, 0)),
        out_shape=jax.ShapeDtypeStruct((BINS, SUB, 128), BF),
        scratch_shapes=[pltpu.VMEM((SB, BINS, 128), F32)],
        compiler_params=VMEM,
        cost_estimate=pl.CostEstimate(flops=10**8, bytes_accessed=13 * 10**6, transcendentals=0),
        name="whiten",
    )(spectra, counts[:, None])


def turn_kernel(own, rot):
    v = own[...]
    rot[...] = jnp.concatenate([v[..., BLOCK:], -v[..., :BLOCK]], axis=-1)


def turn(own):
    blk = pl.BlockSpec((KC, SUB, 128), lambda i: (i, 0, 0))
    return pl.pallas_call(
        turn_kernel,
        grid=(CHUNKS,),
        in_specs=[blk],
        out_specs=blk,
        out_shape=jax.ShapeDtypeStruct((BINS, SUB, 128), BF),
        compiler_params=VMEM,
        cost_estimate=pl.CostEstimate(flops=10**6, bytes_accessed=25 * 10**6, transcendentals=0),
        name="turn",
    )(own)


def cross_kernel(n, *refs):
    place = refs[0]
    pieces = refs[1 : 1 + n]
    own, rot = refs[1 + n : 3 + n]
    out, src, work, sems = refs[-4:]
    step = pl.program_id(0)
    copies = []
    for m, piece in enumerate(pieces):
        copies.append(pltpu.make_async_copy(piece, src.at[m], sems.at[m]))

    @pl.when(step == 0)
    def _():
        for copy in copies:
            copy.start()

    for m, copy in enumerate(copies):
        @pl.when(step == m)
        def _(copy=copy):
            copy.wait()

    for k in range(KC):
        x = src[step, k].T
        h = jnp.dot(x[:BLOCK], own[k], preferred_element_type=F32)
        h += jnp.dot(x[BLOCK:], rot[k], preferred_element_type=F32)
        work[k] = h
    z = jnp.swapaxes(work[...], 0, 1)
    low = lax.broadcasted_iota(jnp.int32, (KC, 128), 1) < BLOCK
    for p in range(BLOCK // 2):
        u, v = z[2 * p], z[2 * p + 1]
        lanes = slice(p % 2 * 128, p % 2 * 128 + 128)
        out[p // 2, 0, :, lanes] = jnp.where(low, u, pltpu.roll(v, 64, 1)).astype(BF)
        out[p // 2, 1, :, lanes] = jnp.where(low, pltpu.roll(u, 64, 1), v).astype(BF)


def cross(place, pieces, own, rot, base=None):
    n = len(pieces)
    here = pl.BlockSpec((KC, SUB, 128), lambda i, p: (p[i], 0, 0))
    anywhere = pl.BlockSpec(memory_space=pl.ANY)
    extra = [] if base is None else [base]
    return pl.pallas_call(
        lambda *refs: cross_kernel(n, *refs),
        grid_spec=pltpu.PrefetchScalarGridSpec(
            num_scalar_prefetch=1,
            grid=(n,),
            in_specs=[anywhere] * n + [here, here] + [anywhere] * len(extra),
            out_specs=pl.BlockSpec((BLOCK // 4, 2, KC, 256), lambda i, p: (0, 0, p[i], 0)),
            scratch_shapes=[
                pltpu.VMEM((n, KC, SUB, 128), BF),
                pltpu.VMEM((KC, BLOCK, 128), F32),
                pltpu.SemaphoreType.DMA((n,)),
            ],
        ),
        out_shape=jax.ShapeDtypeStruct((BLOCK // 4, 2, BINS, 256), BF),
        input_output_aliases={n + 3: 0} if extra else {},
        compiler_params=VMEM,
        cost_estimate=pl.CostEstimate(
            flops=n * 16 * 10**8, bytes_accessed=n * 4 * 10**6, transcendentals=0
        ),
        name="cross",
    )(place, *pieces, own, rot, *extra)


def lags_kernel(order, rows, inv, table, out):
    for q in range(4):
        y = jnp.dot(table[...], rows[q].reshape(2 * BINS, 256), preferred_element_type=F32)
        cols = slice(q * 256, q * 256 + 256)
        out[0, :, cols] = (y * inv[0, :, cols]).astype(BF)


def lags(order, rows, inv, table):
    n = order.shape[0]
    return pl.pallas_call(
        lags_kernel,
        grid_spec=pltpu.PrefetchScalarGridSpec(
            num_scalar_prefetch=1,
            grid=(n,),
            in_specs=[
                pl.BlockSpec((4, 2, BINS, 256), lambda i, o: (o[i], 0, 0, 0)),
                pl.BlockSpec((1, 1, 1024), lambda i, o: (o[i], 0, 0)),
                pl.BlockSpec((LAGS, 2 * BINS), lambda i, o: (0, 0)),
            ],
            out_specs=pl.BlockSpec((1, LAGS, 1024), lambda i, o: (i, 0, 0)),
        ),
        out_shape=jax.ShapeDtypeStruct((n, LAGS, 1024), BF),
        compiler_params=VMEM,
        cost_estimate=pl.CostEstimate(
            flops=n * 22 * 10**8, bytes_accessed=n * 3 * 10**6, transcendentals=0
        ),
        name="lags",
    )(order, rows, inv, table)


def finish_kernel(a, b, c, *refs):
    total = a[0].astype(F32) + b[0].astype(F32) + c[...].astype(F32)
    refs[-1][0] = total.T.astype(BF)


def finish(step, near, near_got, far_got, base=None):
    cols = 512
    extra = [] if base is None else [base]
    return pl.pallas_call(
        finish_kernel,
        grid=(1024 // cols,),
        in_specs=[
            pl.BlockSpec((1, LAGS, cols), lambda j: (1, 0, j)),
            pl.BlockSpec((1, LAGS, cols), lambda j: (0, 0, j)),
            pl.BlockSpec((LAGS, cols), lambda j: (0, j)),
        ]
        + [pl.BlockSpec(memory_space=pl.ANY)] * len(extra),
        out_specs=pl.BlockSpec((1, cols, LAGS), lambda j: (step, j, 0)),
        out_shape=jax.ShapeDtypeStruct((STEPS, 1024, LAGS), BF),
        input_output_aliases={3: 0} if extra else {},
        compiler_params=VMEM,
        name="finish",
    )(near, near_got, far_got, *extra)


def lag_table():
    k = np.arange(1, BINS + 1)[None, :]
    tau = np.arange(LAGS)[:, None] - LAGS // 2
    ph = ((k * tau) % NFFT) * (2 * np.pi / NFFT)
    w = np.concatenate([np.cos(ph), -np.sin(ph)], axis=1) / math.sqrt(BINS)
    return jnp.asarray(w, BF)


def along_x(a, d):
    return lax.ppermute(a, "station", [(s, s - s % 4 + (s + d) % 4) for s in range(32)])


def along_z(a, d):
    return lax.ppermute(a, "station", [(s, (s + 8 * d) % 32) for s in range(32)])


def swap_y(a):
    return lax.ppermute(a, "station", [(s, s ^ 4) for s in range(32)])


def cut(a, index, size):
    return lax.dynamic_slice_in_dim(a, index * size, size, 0)


def pick(which, options):
    out = options[0]
    for n in range(1, 4):
        out = jnp.where(which == n, options[n], out)
    return out


def barrier(*arrays):
    return lax.optimization_barrier(arrays)


def spread(sends, shifts, work=None, args=()):
    n = len(sends)
    held = barrier(*sends, *args)
    got = [shift(a) for a, shift in zip(held[:n], shifts)]
    done = list(work(*held[n:])) if work else []
    return barrier(*got, *done)


HOPS = (1, 2, 3)
TO_X = [lambda a, d=d: along_x(a, d) for d in HOPS]
TO_Z = [lambda a, d=d: along_z(a, d) for d in HOPS]


def gather_counts(marks):
    for shift in (TO_X[1], TO_Z[0], TO_Z[1], swap_y):
        marks = jnp.stack([marks, shift(marks)])
    return [marks]


def broadcast(own, marks, roots, z, h, x):
    got = spread(
        [cut(own, (x + d) & 3, 64) for d in HOPS]
        + [cut(own, 4 + ((z + d) & 3), 64) for d in HOPS],
        TO_X + TO_Z,
    )
    got_a = [cut(own, x, 64), *got[:3]]
    got_b = [cut(own, 4 + z, 64), *got[3:6]]
    sel_a = [pick((x - r[2]) & 3, got_a) for r in roots]
    sel_b = [pick((z - r[0]) & 3, got_b) for r in roots]

    def some(sel, q):
        return jnp.stack([cut(a, q, 16) for a in sel])

    got = spread(
        [some(sel_a, (z + d) & 3) for d in HOPS]
        + [some(sel_b, (x + d) & 3) for d in HOPS],
        TO_Z + TO_X,
    )
    got_a = [some(sel_a, z), *got[:3]]
    got_b = [some(sel_b, x), *got[3:6]]
    mine = jnp.stack(
        [
            jnp.stack([pick((z - r[0]) & 3, [g[i] for g in got_a]) for i, r in enumerate(roots)]),
            jnp.stack([pick((x - r[2]) & 3, [g[i] for g in got_b]) for i, r in enumerate(roots)]),
        ]
    )
    other, marks = spread([mine], [swap_y], gather_counts, [marks])
    sub = [
        jnp.stack([jnp.where(h == r[1], mine[n, i], other[n, i]) for i, r in enumerate(roots)])
        for n in range(2)
    ]
    got = spread([sub[0]] * 3 + [sub[1]] * 3, TO_Z + TO_X)
    all_a = [sub[0], *got[:3]]
    all_b = [sub[1], *got[3:6]]
    out = []
    for i in range(STEPS):
        a = jnp.concatenate([pick((z - q) & 3, [v[i] for v in all_a]) for q in range(4)])
        b = jnp.concatenate([pick((x - q) & 3, [v[i] for v in all_b]) for q in range(4)])
        out.append((a, b))
    return out, marks


def other_core(a):
    return lax.ppermute(a, "tm", [(t, t ^ 1) for t in range(4)])


def other_chip(a):
    return lax.ppermute(a, "tm", [(t, t ^ 2) for t in range(4)])


def add(a, b):
    return (a.astype(F32) + b.astype(F32)).astype(BF)


def body(spectra, counts, block_ids):
    counts = counts[0]
    table = lag_table()
    station, tm = lax.axis_index("station"), lax.axis_index("tm")
    z, h, x = station >> 3, station >> 2 & 1, station & 3
    next_counts, own = spread([counts], [TO_X[0]], lambda *a: [whiten(*a)], [spectra[0], counts])
    marks = jnp.stack([counts, next_counts])
    roots = [(block_ids[i] >> 3, block_ids[i] >> 2 & 1, block_ids[i] & 3) for i in range(STEPS)]
    starts, marks = broadcast(own, marks, roots, z, h, x)

    def places(*list_of):
        return jnp.stack(list_of).astype(jnp.int32)

    near_by = places(x, (x + 3) & 3, (x + 1) & 3, 4 + z, 4 + ((z + 3) & 3), 4 + ((z + 1) & 3))
    opposite = places((x + 2) & 3, 4 + ((z + 2) & 3))
    everywhere = jnp.concatenate([near_by, opposite])
    far_blocks = places((tm ^ 2) ^ 1, tm ^ 2)
    near_blocks = places(tm ^ 1, tm)

    def scales(marks):
        out = []
        for r in roots:
            dz, dx = (z - r[0]) & 3, (x - r[2]) & 3
            src_counts = marks[h ^ r[1], dz >> 1, dz & 1, dx >> 1, dx & 1]
            inv = 1.0 / jnp.minimum(src_counts[:, None], counts[None, :]).astype(F32)
            out.append(inv.reshape(4, 1, 1024))
        return out

    def far(i, rows):
        return lags(far_blocks, rows, invs[i], table)

    def near(i, rows):
        return lags(near_blocks, rows, invs[i], table)

    (a0, b0), (a1, b1) = starts
    up, down = [TO_X[0], TO_Z[0]], [TO_X[2], TO_Z[2]]
    a0_up, b0_up, a0_down, b0_down, rot, *invs = spread(
        [a0, b0, a0, b0], up + down, lambda v, m: [turn(v), *scales(m)], [own, marks]
    )
    a0_far, b0_far, a1_down, b1_down, rows = spread(
        [a0_up, b0_up, a1, b1],
        up + down,
        lambda *v: [cross(near_by, v[:6], *v[6:])],
        [a0, a0_up, a0_down, b0, b0_up, b0_down, own, rot],
    )

    def work(rows, *v):
        rows = cross(opposite, v[:2], *v[2:], rows)
        return [far(0, rows), near(0, rows)]

    a1_up, b1_up, a1_far, b1_far, far0, near0 = spread(
        [a1, b1, a1_down, b1_down], up + down, work, [rows, a0_far, b0_far, own, rot]
    )
    far_got0, near_got0 = spread([far0[:1], near0[:1]], [other_core] * 2)
    sum0 = add(far0[1], far_got0[0])

    def work(*v):
        rows = cross(everywhere, v[:8], *v[8:])
        return [rows, far(1, rows)]

    far_sum0, rows, far1 = spread(
        [sum0],
        [other_chip],
        work,
        [a1, a1_up, a1_down, b1, b1_up, b1_down, a1_far, b1_far, own, rot],
    )
    (far_got1,) = spread([far1[:1]], [other_core])
    sum1 = add(far1[1], far_got1[0])

    def work(rows, *step0):
        return [near(1, rows), finish(0, *step0)]

    far_sum1, near1, out = spread(
        [sum1], [other_chip], work, [rows, near0, near_got0, far_sum0]
    )
    near_got1 = other_core(near1[:1])
    out = finish(1, near1, near_got1, far_sum1, out)
    return out.reshape(STEPS, 16, BLOCK, LAGS)


def solution(mesh):
    from jax.sharding import PartitionSpec as P

    return jax.shard_map(
        body,
        mesh=mesh,
        in_specs=(P("tm", None, "station", None), P("tm", "station"), P()),
        out_specs=P(None, "tm", "station", None),
        check_vma=False,
    )
```

time: 418 us -> 298 us (0.71)
  waiting for transfers between devices: 193 us -> 76.7 us
  starting transfers between devices: 14.6 us -> 96.2 us
  blocking collectives: 79.6 us -> 0 us
  between operations: 17.2 us -> 4.22 us
  Pallas kernels: 92.8 us -> 84.2 us
  other arithmetic: 8.78 us -> 16.9 us
  local copies, waits for them, and re-layouts: 11.5 us -> 18.3 us
    ppermute x4 -> x42, starting transfers between devices: 2.94 us -> 96.2 us  [the longest x17 31.6 us: along_z(): lax.ppermute(a, 'station', [(s, (s + 8 * d) % 32) for s in range(32)])]
    all_to_all x1 -> x0, waiting for transfers between devices: 80.4 us -> none  [body(): pieces = lax.all_to_all(own.reshape(32, 16, SUB, 128), 'station', 0, 0)]
    all_gather x1 -> x0, blocking collectives: 79.6 us -> none  [body(): all_counts = lax.all_gather(counts, 'station')]
    all_gather x2 -> x0, waiting for transfers between devices: 70.6 us -> none  [body(): src = lax.all_gather(piece, 'station').reshape(BINS, SUB, 128)]
    ppermute x4 -> x42, waiting for transfers between devices: 41.7 us -> 76.7 us  [the longest x17 37.6 us: along_x(): lax.ppermute(a, 'station', [(s, s - s % 4 + (s + d) % 4) for s in range(3...]
    all_to_all x1 -> x0, starting transfers between devices: 11.6 us -> none  [body(): pieces = lax.all_to_all(own.reshape(32, 16, SUB, 128), 'station', 0, 0)]
    slice x1 -> x5, local copies, waits for them, and re-layouts: 0.56 us -> 7.58 us  [the longest x2 3.64 us: body(): far_got0, near_got0 = spread([far0[:1], near0[:1]], [other_core] * 2)]
    pallas_call x1, Pallas kernels: 17 us -> 9.95 us  [whiten(): pl.pallas_call(whiten_kernel, grid=(SUB // SB,), in_specs=[pl.BlockSpec((...]
  transfers between devices with their start and end apart: 7 -> 42, of which waited for: 6 -> 24; matrix products, arithmetic and copies ran while one was open for 4% -> 3% of each run, Pallas kernels for 17% -> 27%
where the time goes in v2:
time: 298 us; the launch traced here: 297 us
  starting transfers between devices  96.2 us (32%)
  Pallas kernels  84.2 us (28%)
  waiting for transfers between devices  76.7 us (26%)
  local copies, waits for them, and re-layouts  18.3 us (6%)
  other arithmetic  16.9 us (6%)
  between operations  4.22 us (1%)
    ppermute x17, waiting for transfers between devices, along_x(): lax.ppermute(a, 'station', [(s, s - s % 4 + (s + d) % 4) for s in range(3...  37.6 us
    pallas_call x3, Pallas kernels, cross(): pl.pallas_call(lambda *refs: cross_kernel(n, *refs), grid_spec=pltpu.Pref...  35.2 us
    ppermute x17, starting transfers between devices, along_z(): lax.ppermute(a, 'station', [(s, (s + 8 * d) % 32) for s in range(32)])  31.6 us
    ppermute x4, starting transfers between devices, other_core(): return lax.ppermute(a, 'tm', [(t, t ^ 1) for t in range(4)])  27.9 us
    pallas_call x4, Pallas kernels, lags(): pl.pallas_call(lags_kernel, grid_spec=pltpu.PrefetchScalarGridSpec(num_sc...  24.3 us
    ppermute x17, starting transfers between devices, along_x(): lax.ppermute(a, 'station', [(s, s - s % 4 + (s + d) % 4) for s in range(3...  23.4 us
    ppermute x2, waiting for transfers between devices, other_chip(): return lax.ppermute(a, 'tm', [(t, t ^ 2) for t in range(4)])  15.3 us
    ppermute x17, waiting for transfers between devices, along_z(): lax.ppermute(a, 'station', [(s, (s + 8 * d) % 32) for s in range(32)])  14.8 us
  transfers between devices with their start and end apart: 42, of which 24 were waited for; matrix products, arithmetic and copies ran while one was open for 3% of the time, Pallas kernels for 27%

profile of v2, /device:TPU:1, one launch (start us, length us, event | category | flops | bytes accessed | tf_op | source)
XLA Modules:
  0.0 296.6 jit_solution(13838337612280430242)
XLA Ops:
  3.4 9.9 %whiten.1.own.refs_7_.refs_3_.refs_9_ = bf16[512,48,128]{2,1,0:T(8,128)(2,1)} custom-call(bf16[48,64,1024]{2,1,0:T(8,128)(2,1)} %bitcast.270, s32[64,1]{1,0:T(8,128)} %copy.7.counts), custom_call_target="tpu_custom_call" | custom-call | flops 100000000 | bytes 13000000 | tf_op jit(solution)/shard_map/whiten/pallas_call | solution.py:33
  13.4 4.4 %constant_dynamic-slice_fusion.2 = (bf16[64,48,128]{2,1,0:T(8,128)(2,1)}, bf16[64,48,128]{2,1,0:T(8,128)(2,1)}, bf16[64,48,128]{2,1,0:T(8,128)(2,1)}, bf16[64,48...) fusion(bf16[512,48,128]{2,1,0:T(8,128)(2,1)} %whiten.1.own.refs_7_.refs_3_.refs_9_, ...), kind=kLoop, calls=%fused_computation.109 | loop fusion | bytes 9437208 | tf_op jit(solution)/shard_map/dynamic_slice | solution.py:206
  23.9 3.3 %collective-permute-start.5 = (bf16[64,48,128]{2,1,0:T(8,128)(2,1)}, bf16[64,48,128]{2,1,0:T(8,128)(2,1)S(1)}, u32[]{:S(2)}, u32[]{:S(2)}) collective-permute-start(bf16[64,48,128]{2,1,0:T(8,128)(2,1)} %get-tuple-element.129), channel_id=1, source_target_pairs={{0,64},{4,68},{8,72},{12,76},{16,80},{20,84},{24,88},{28,92},{32,9... | collective-permute-start | bytes 2359304 | tf_op jit(solution)/shard_map/ppermute | solution.py:198
  27.2 10.3 %collective-permute-done.1 = bf16[64,48,128]{2,1,0:T(8,128)(2,1)} collective-permute-done((bf16[64,48,128]{2,1,0:T(8,128)(2,1)S(1)}, bf16[64,48,128]{2,1,0:T(8,128)(2,1)}, u32[]{:S(2)}, u32[]{:S(2)}) %collective-permute-start.1) | collective-permute-done | bytes 786464 | tf_op jit(solution)/shard_map/ppermute | solution.py:194
  37.5 3.4 %collective-permute-start.6 = (bf16[64,48,128]{2,1,0:T(8,128)(2,1)}, bf16[64,48,128]{2,1,0:T(8,128)(2,1)}, u32[]{:S(2)}, u32[]{:S(2)}) collective-permute-start(bf16[64,48,128]{2,1,0:T(8,128)(2,1)} %get-tuple-element.130), channel_id=1, source_target_pairs={{0,96},{4,100},{8,104},{12,108},{16,112},{20,116},{24,120},{28,124... | collective-permute-start | bytes 2359304 | tf_op jit(solution)/shard_map/ppermute | solution.py:198
  44.1 9.5 %collective-permute-done.2 = bf16[64,48,128]{2,1,0:T(8,128)(2,1)S(1)} collective-permute-done((bf16[64,48,128]{2,1,0:T(8,128)(2,1)}, bf16[64,48,128]{2,1,0:T(8,128)(2,1)S(1)}, u32[]{:S(2)}, u32[]{:S(2)}) %collective-permute-start.2) | collective-permute-done | bytes 786464 | tf_op jit(solution)/shard_map/ppermute | solution.py:194
  55.2 4.9 %collective-permute-done.5 = bf16[64,48,128]{2,1,0:T(8,128)(2,1)S(1)} collective-permute-done((bf16[64,48,128]{2,1,0:T(8,128)(2,1)}, bf16[64,48,128]{2,1,0:T(8,128)(2,1)S(1)}, u32[]{:S(2)}, u32[]{:S(2)}) %collective-permute-start.5) | collective-permute-done | bytes 786464 | tf_op jit(solution)/shard_map/ppermute | solution.py:198
  69.9 3.0 %collective-permute-start.7 = (bf16[2,16,48,128]{3,2,1,0:T(8,128)(2,1)}, bf16[2,16,48,128]{3,2,1,0:T(8,128)(2,1)}, u32[]{:S(2)}, u32[]{:S(2)}) collective-permute-start(bf16[2,16,48,128]{3,2,1,0:T(8,128)(2,1)} %pad_maximum_fusion.5), channel_id=1, source_target_pairs={{0,32},{4,36},{8,40},{12,44},{16,48},{20,52},{24,56},{28,60},{32,6... | collective-permute-start | bytes 1179656 | tf_op jit(solution)/shard_map/ppermute | solution.py:198
  76.3 7.2 %collective-permute-done.11 = bf16[2,16,48,128]{3,2,1,0:T(8,128)(2,1)} collective-permute-done((bf16[2,16,48,128]{3,2,1,0:T(8,128)(2,1)}, bf16[2,16,48,128]{3,2,1,0:T(8,128)(2,1)}, u32[]{:S(2)}, u32[]{:S(2)}) %collective-permute-start.11) | collective-permute-done | bytes 393248 | tf_op jit(solution)/shard_map/ppermute | solution.py:194
  87.8 7.2 %collective-permute-start.13 = (bf16[2,2,16,48,128]{4,3,2,1,0:T(8,128)(2,1)S(1)}, bf16[2,2,16,48,128]{4,3,2,1,0:T(8,128)(2,1)S(1)}, u32[]{:S(2)}, u32[]{:S(2)}) collective-permute-start(bf16[2,2,16,48,128]{4,3,2,1,0:T(8,128)(2,1)S(1)} %pad_maximum_fusion), channel_id=1, source_target_pairs={{0,16},{4,20},{8,24},{12,28},{16,0},{20,4},{24,8},{28,12},{32,48},... | collective-permute-start | bytes 2359304 | tf_op jit(solution)/shard_map/ppermute | solution.py:202
  95.0 2.8 collective-permute-start.14
  98.9 3.8 %collective-permute-start.15 = (s32[2,2,64]{2,1,0:T(2,128)S(1)}, s32[2,2,64]{2,1,0:T(2,128)S(1)}, u32[]{:S(2)}, u32[]{:S(2)}) collective-permute-start(s32[2,2,64]{2,1,0:T(2,128)S(1)} %get-tuple-element.294), channel_id=1, source_target_pairs={{0,32},{4,36},{8,40},{12,44},{16,48},{20,52},{24,56},{28,60},{32,6... | collective-permute-start | bytes 3080 | tf_op jit(solution)/shard_map/ppermute | solution.py:198
  118.7 3.0 %collective-permute-start.22 = (bf16[2,16,48,128]{3,2,1,0:T(8,128)(2,1)S(1)}, bf16[2,16,48,128]{3,2,1,0:T(8,128)(2,1)S(1)}, u32[]{:S(2)}, u32[]{:S(2)}) collective-permute-start(bf16[2,16,48,128]{3,2,1,0:T(8,128)(2,1)S(1)} %pad_maximum_fusion.12), channel_id=1, source_target_pairs={{0,8},{4,12},{8,0},{12,4},{16,24},{20,28},{24,16},{28,20},{32,40},... | collective-permute-start | bytes 1179656 | tf_op jit(solution)/shard_map/ppermute | solution.py:194
  121.7 4.3 %collective-permute-done.18 = bf16[2,16,48,128]{3,2,1,0:T(8,128)(2,1)S(1)} collective-permute-done((bf16[2,16,48,128]{3,2,1,0:T(8,128)(2,1)}, bf16[2,16,48,128]{3,2,1,0:T(8,128)(2,1)S(1)}, u32[]{:S(2)}, u32[]{:S(2)}) %collective-permute-start.18) | collective-permute-done | bytes 393248 | tf_op jit(solution)/shard_map/ppermute | solution.py:198
  128.6 2.5 collective-permute-done.22
  138.6 2.7 collective-permute-start.27
  142.5 9.0 %turn.1.refs_8_.refs_4_.refs_10_ = bf16[512,48,128]{2,1,0:T(8,128)(2,1)} custom-call(bf16[512,48,128]{2,1,0:T(8,128)(2,1)} %whiten.1.own.refs_7_.refs_3_.refs_9_), custom_call_target="tpu_custom_call" | custom-call | flops 1000000 | bytes 25000000 | tf_op jit(solution)/shard_map/turn/pallas_call | solution.py:56
  156.2 2.7 collective-permute-start.31
  158.9 12.7 %cross.3.refs_5_ = bf16[16,2,512,256]{3,2,1,0:T(8,128)(2,1)} custom-call(s32[6]{0:T(128)} %stack.230.refs_0_, bf16[64,48,128]{2,1,0:T(8,128)(2,1)} %pad_maximum_fusion.3.refs_1_, bf16[64,48,128]{2,1,0:T(8,128)(2,1)} %collective-permute-done.24.refs_2_, bf16[64,48,128]{2,1,0:T(8,128)(2,1)} %collective-permute-done.26.refs_3_, ...), custom_call_target="tpu_custom_call" | custom-call | flops 9600000000 | bytes 24000000 | tf_op jit(solution)/shard_map/cross/pallas_call | solution.py:107
  176.2 2.6 collective-permute-start.34
  179.5 6.6 %cross.4.rows = bf16[16,2,512,256]{3,2,1,0:T(8,128)(2,1)} custom-call(s32[2]{0:T(128)} %pad_add_fusion.6.refs_0_, bf16[64,48,128]{2,1,0:T(8,128)(2,1)} %copy-done.13, bf16[64,48,128]{2,1,0:T(8,128)(2,1)} %copy-done.14, bf16[512,48,128]{2,1,0:T(8,128)(2,1)} %whiten.1.own.refs_7_.refs_3_.refs_9_, ...), custom_call_target="tpu_custom_call", output_to_operand_aliasing={{}: (5, {})} | custom-call | flops 3200000000 | bytes 8000000 | tf_op jit(solution)/shard_map/cross/pallas_call | solution.py:107
  186.2 6.1 %lags.5.a = bf16[2,512,1024]{2,1,0:T(8,128)(2,1)} custom-call(s32[2]{0:T(128)} %get-tuple-element.298.order, bf16[16,2,512,256]{3,2,1,0:T(8,128)(2,1)} %cross.4.rows, f32[4,1,1024]{2,1,0:T(1,128)} %get-tuple-element.203.inv, bf16[512,1024]{1,0:T(8,128)(2,1)} %constant.49.clone.table), custom_call_target="tpu_custom_call" | custom-call | flops 4400000000 | bytes 6000000 | tf_op jit(solution)/shard_map/lags/pallas_call | solution.py:139
  192.3 6.1 %lags.4 = bf16[2,512,1024]{2,1,0:T(8,128)(2,1)} custom-call(s32[2]{0:T(128)} %get-tuple-element.297.order, bf16[16,2,512,256]{3,2,1,0:T(8,128)(2,1)} %cross.4.rows, f32[4,1,1024]{2,1,0:T(1,128)} %get-tuple-element.203.inv, bf16[512,1024]{1,0:T(8,128)(2,1)} %constant.49.clone.table), custom_call_target="tpu_custom_call" | custom-call | flops 4400000000 | bytes 6000000 | tf_op jit(solution)/shard_map/lags/pallas_call | solution.py:139
  198.4 2.6 slice.195
  202.0 25.7 %collective-permute-start.36 = (bf16[1,512,1024]{2,1,0:T(8,128)(2,1)}, bf16[1,512,1024]{2,1,0:T(8,128)(2,1)S(1)}, u32[]{:S(2)}, u32[]{:S(2)}) collective-permute-start(bf16[1,512,1024]{2,1,0:T(8,128)(2,1)} %slice.195), channel_id=1, source_target_pairs={{0,1},{1,0},{2,3},{3,2},{4,5},{5,4},{6,7},{7,6},{8,9},{9,8},{10,11... | collective-permute-start | bytes 3145736 | tf_op jit(solution)/shard_map/ppermute | solution.py:283
  228.3 3.0 %collective-permute-done.36 = bf16[1,512,1024]{2,1,0:T(8,128)(2,1)S(1)} collective-permute-done((bf16[1,512,1024]{2,1,0:T(8,128)(2,1)}, bf16[1,512,1024]{2,1,0:T(8,128)(2,1)S(1)}, u32[]{:S(2)}, u32[]{:S(2)}) %collective-permute-start.36) | collective-permute-done | bytes 1048608 | tf_op jit(solution)/shard_map/ppermute | solution.py:283
  234.4 15.8 %cross.5.rows = bf16[16,2,512,256]{3,2,1,0:T(8,128)(2,1)} custom-call(s32[8]{0:T(128)} %concatenate.20.refs_0_, bf16[64,48,128]{2,1,0:T(8,128)(2,1)} %copy-done.11, bf16[64,48,128]{2,1,0:T(8,128)(2,1)} %copy-done.21, bf16[64,48,128]{2,1,0:T(8,128)(2,1)} %copy-done.19, bf16[64,48,128]{2,1,0:T(8,128)(2,1)} %copy-done.10, ...), custom_call_target="tpu_custom_call" | custom-call | flops 12800000000 | bytes 32000000 | tf_op jit(solution)/shard_map/cross/pallas_call | solution.py:107
  250.2 6.1 %lags.6 = bf16[2,512,1024]{2,1,0:T(8,128)(2,1)} custom-call(s32[2]{0:T(128)} %get-tuple-element.297.order, bf16[16,2,512,256]{3,2,1,0:T(8,128)(2,1)} %cross.5.rows, f32[4,1,1024]{2,1,0:T(1,128)} %get-tuple-element.224.inv, bf16[512,1024]{1,0:T(8,128)(2,1)} %constant.49.clone.table), custom_call_target="tpu_custom_call" | custom-call | flops 4400000000 | bytes 6000000 | tf_op jit(solution)/shard_map/lags/pallas_call | solution.py:139
  264.5 2.9 finish.2.refs_0_
  267.4 6.1 %lags.7.a = bf16[2,512,1024]{2,1,0:T(8,128)(2,1)} custom-call(s32[2]{0:T(128)} %get-tuple-element.298.order, bf16[16,2,512,256]{3,2,1,0:T(8,128)(2,1)} %cross.5.rows, f32[4,1,1024]{2,1,0:T(1,128)} %get-tuple-element.224.inv, bf16[512,1024]{1,0:T(8,128)(2,1)} %constant.49.clone.table), custom_call_target="tpu_custom_call" | custom-call | flops 4400000000 | bytes 6000000 | tf_op jit(solution)/shard_map/lags/pallas_call | solution.py:139
  273.5 13.9 %collective-permute-done.40.c = bf16[512,1024]{1,0:T(8,128)(2,1)S(1)} collective-permute-done((bf16[512,1024]{1,0:T(8,128)(2,1)S(1)}, bf16[512,1024]{1,0:T(8,128)(2,1)S(1)}, u32[]{:S(2)}, u32[]{:S(2)}) %collective-permute-start.40) | collective-permute-done | bytes 1048608 | tf_op jit(solution)/shard_map/ppermute | solution.py:287
  293.7 2.9 finish.3
  (163 shorter events, 85.4 us)
Async XLA Ops:
  0.0 13.4 %collective-permute-start = (s32[64]{0:T(128)}, s32[64]{0:T(128)S(1)}, u32[]{:S(2)}, u32[]{:S(2)}) collective-permute-start(s32[64]{0:T(128)} %bitcast.276), channel_id=1, source_target_pairs={{0,4},{4,8},{8,12},{12,0},{16,20},{20,24},{24,28},{28,16},{32,36},... | collective-permute-start | bytes 776 | tf_op jit(solution)/shard_map/ppermute | solution.py:194
  17.8 19.7 %collective-permute-start.1 = (bf16[64,48,128]{2,1,0:T(8,128)(2,1)S(1)}, bf16[64,48,128]{2,1,0:T(8,128)(2,1)}, u32[]{:S(2)}, u32[]{:S(2)}) collective-permute-start(bf16[64,48,128]{2,1,0:T(8,128)(2,1)S(1)} %get-tuple-element.125), channel_id=1, source_target_pairs={{0,4},{4,8},{8,12},{12,0},{16,20},{20,24},{24,28},{28,16},{32,36},... | collective-permute-start | bytes 2359304 | tf_op jit(solution)/shard_map/ppermute | solution.py:194
  19.0 34.6 %collective-permute-start.2 = (bf16[64,48,128]{2,1,0:T(8,128)(2,1)}, bf16[64,48,128]{2,1,0:T(8,128)(2,1)S(1)}, u32[]{:S(2)}, u32[]{:S(2)}) collective-permute-start(bf16[64,48,128]{2,1,0:T(8,128)(2,1)} %get-tuple-element.126), channel_id=1, source_target_pairs={{0,8},{4,12},{8,0},{12,4},{16,24},{20,28},{24,16},{28,20},{32,40},... | collective-permute-start | bytes 2359304 | tf_op jit(solution)/shard_map/ppermute | solution.py:194
  20.2 34.9 %collective-permute-start.3 = (bf16[64,48,128]{2,1,0:T(8,128)(2,1)}, bf16[64,48,128]{2,1,0:T(8,128)(2,1)S(1)}, u32[]{:S(2)}, u32[]{:S(2)}) collective-permute-start(bf16[64,48,128]{2,1,0:T(8,128)(2,1)} %get-tuple-element.127), channel_id=1, source_target_pairs={{0,12},{4,0},{8,4},{12,8},{16,28},{20,16},{24,20},{28,24},{32,44},... | collective-permute-start | bytes 2359304 | tf_op jit(solution)/shard_map/ppermute | solution.py:194
  22.3 32.9 %collective-permute-start.4 = (bf16[64,48,128]{2,1,0:T(8,128)(2,1)}, bf16[64,48,128]{2,1,0:T(8,128)(2,1)S(1)}, u32[]{:S(2)}, u32[]{:S(2)}) collective-permute-start(bf16[64,48,128]{2,1,0:T(8,128)(2,1)} %get-tuple-element.128), channel_id=1, source_target_pairs={{0,32},{4,36},{8,40},{12,44},{16,48},{20,52},{24,56},{28,60},{32,6... | collective-permute-start | bytes 2359304 | tf_op jit(solution)/shard_map/ppermute | solution.py:198
  23.9 36.1 %collective-permute-start.5 = (bf16[64,48,128]{2,1,0:T(8,128)(2,1)}, bf16[64,48,128]{2,1,0:T(8,128)(2,1)S(1)}, u32[]{:S(2)}, u32[]{:S(2)}) collective-permute-start(bf16[64,48,128]{2,1,0:T(8,128)(2,1)} %get-tuple-element.129), channel_id=1, source_target_pairs={{0,64},{4,68},{8,72},{12,76},{16,80},{20,84},{24,88},{28,92},{32,9... | collective-permute-start | bytes 2359304 | tf_op jit(solution)/shard_map/ppermute | solution.py:198
  37.5 22.6 %collective-permute-start.6 = (bf16[64,48,128]{2,1,0:T(8,128)(2,1)}, bf16[64,48,128]{2,1,0:T(8,128)(2,1)}, u32[]{:S(2)}, u32[]{:S(2)}) collective-permute-start(bf16[64,48,128]{2,1,0:T(8,128)(2,1)} %get-tuple-element.130), channel_id=1, source_target_pairs={{0,96},{4,100},{8,104},{12,108},{16,112},{20,116},{24,120},{28,124... | collective-permute-start | bytes 2359304 | tf_op jit(solution)/shard_map/ppermute | solution.py:198
  67.2 16.3 %collective-permute-start.11 = (bf16[2,16,48,128]{3,2,1,0:T(8,128)(2,1)}, bf16[2,16,48,128]{3,2,1,0:T(8,128)(2,1)}, u32[]{:S(2)}, u32[]{:S(2)}) collective-permute-start(bf16[2,16,48,128]{3,2,1,0:T(8,128)(2,1)} %pad_maximum_fusion.9), channel_id=1, source_target_pairs={{0,8},{4,12},{8,0},{12,4},{16,24},{20,28},{24,16},{28,20},{32,40},... | collective-permute-start | bytes 1179656 | tf_op jit(solution)/shard_map/ppermute | solution.py:194
  68.5 15.1 %collective-permute-start.12 = (bf16[2,16,48,128]{3,2,1,0:T(8,128)(2,1)S(1)}, bf16[2,16,48,128]{3,2,1,0:T(8,128)(2,1)}, u32[]{:S(2)}, u32[]{:S(2)}) collective-permute-start(bf16[2,16,48,128]{3,2,1,0:T(8,128)(2,1)S(1)} %pad_maximum_fusion.10), channel_id=1, source_target_pairs={{0,12},{4,0},{8,4},{12,8},{16,28},{20,16},{24,20},{28,24},{32,44},... | collective-permute-start | bytes 1179656 | tf_op jit(solution)/shard_map/ppermute | solution.py:194
  69.9 13.6 %collective-permute-start.7 = (bf16[2,16,48,128]{3,2,1,0:T(8,128)(2,1)}, bf16[2,16,48,128]{3,2,1,0:T(8,128)(2,1)}, u32[]{:S(2)}, u32[]{:S(2)}) collective-permute-start(bf16[2,16,48,128]{3,2,1,0:T(8,128)(2,1)} %pad_maximum_fusion.5), channel_id=1, source_target_pairs={{0,32},{4,36},{8,40},{12,44},{16,48},{20,52},{24,56},{28,60},{32,6... | collective-permute-start | bytes 1179656 | tf_op jit(solution)/shard_map/ppermute | solution.py:198
  72.9 11.8 %collective-permute-start.8 = (bf16[2,16,48,128]{3,2,1,0:T(8,128)(2,1)}, bf16[2,16,48,128]{3,2,1,0:T(8,128)(2,1)}, u32[]{:S(2)}, u32[]{:S(2)}) collective-permute-start(bf16[2,16,48,128]{3,2,1,0:T(8,128)(2,1)} %pad_maximum_fusion.6), channel_id=1, source_target_pairs={{0,64},{4,68},{8,72},{12,76},{16,80},{20,84},{24,88},{28,92},{32,9... | collective-permute-start | bytes 1179656 | tf_op jit(solution)/shard_map/ppermute | solution.py:198
  87.8 25.0 %collective-permute-start.13 = (bf16[2,2,16,48,128]{4,3,2,1,0:T(8,128)(2,1)S(1)}, bf16[2,2,16,48,128]{4,3,2,1,0:T(8,128)(2,1)S(1)}, u32[]{:S(2)}, u32[]{:S(2)}) collective-permute-start(bf16[2,2,16,48,128]{4,3,2,1,0:T(8,128)(2,1)S(1)} %pad_maximum_fusion), channel_id=1, source_target_pairs={{0,16},{4,20},{8,24},{12,28},{16,0},{20,4},{24,8},{28,12},{32,48},... | collective-permute-start | bytes 2359304 | tf_op jit(solution)/shard_map/ppermute | solution.py:202
  113.7 12.3 %collective-permute-start.18 = (bf16[2,16,48,128]{3,2,1,0:T(8,128)(2,1)}, bf16[2,16,48,128]{3,2,1,0:T(8,128)(2,1)S(1)}, u32[]{:S(2)}, u32[]{:S(2)}) collective-permute-start(bf16[2,16,48,128]{3,2,1,0:T(8,128)(2,1)} %pad_maximum_fusion.11), channel_id=1, source_target_pairs={{0,32},{4,36},{8,40},{12,44},{16,48},{20,52},{24,56},{28,60},{32,6... | collective-permute-start | bytes 1179656 | tf_op jit(solution)/shard_map/ppermute | solution.py:198
  115.4 13.2 %collective-permute-start.19 = (bf16[2,16,48,128]{3,2,1,0:T(8,128)(2,1)}, bf16[2,16,48,128]{3,2,1,0:T(8,128)(2,1)S(1)}, u32[]{:S(2)}, u32[]{:S(2)}) collective-permute-start(bf16[2,16,48,128]{3,2,1,0:T(8,128)(2,1)} %pad_maximum_fusion.11), channel_id=1, source_target_pairs={{0,64},{4,68},{8,72},{12,76},{16,80},{20,84},{24,88},{28,92},{32,9... | collective-permute-start | bytes 1179656 | tf_op jit(solution)/shard_map/ppermute | solution.py:198
  115.9 12.8 %collective-permute-start.20 = (bf16[2,16,48,128]{3,2,1,0:T(8,128)(2,1)}, bf16[2,16,48,128]{3,2,1,0:T(8,128)(2,1)S(1)}, u32[]{:S(2)}, u32[]{:S(2)}) collective-permute-start(bf16[2,16,48,128]{3,2,1,0:T(8,128)(2,1)} %pad_maximum_fusion.11), channel_id=1, source_target_pairs={{0,96},{4,100},{8,104},{12,108},{16,112},{20,116},{24,120},{28,124... | collective-permute-start | bytes 1179656 | tf_op jit(solution)/shard_map/ppermute | solution.py:198
  117.8 10.8 %collective-permute-start.21 = (bf16[2,16,48,128]{3,2,1,0:T(8,128)(2,1)S(1)}, bf16[2,16,48,128]{3,2,1,0:T(8,128)(2,1)S(1)}, u32[]{:S(2)}, u32[]{:S(2)}) collective-permute-start(bf16[2,16,48,128]{3,2,1,0:T(8,128)(2,1)S(1)} %pad_maximum_fusion.12), channel_id=1, source_target_pairs={{0,4},{4,8},{8,12},{12,0},{16,20},{20,24},{24,28},{28,16},{32,36},... | collective-permute-start | bytes 1179656 | tf_op jit(solution)/shard_map/ppermute | solution.py:194
  118.7 12.4 %collective-permute-start.22 = (bf16[2,16,48,128]{3,2,1,0:T(8,128)(2,1)S(1)}, bf16[2,16,48,128]{3,2,1,0:T(8,128)(2,1)S(1)}, u32[]{:S(2)}, u32[]{:S(2)}) collective-permute-start(bf16[2,16,48,128]{3,2,1,0:T(8,128)(2,1)S(1)} %pad_maximum_fusion.12), channel_id=1, source_target_pairs={{0,8},{4,12},{8,0},{12,4},{16,24},{20,28},{24,16},{28,20},{32,40},... | collective-permute-start | bytes 1179656 | tf_op jit(solution)/shard_map/ppermute | solution.py:194
  135.9 16.8 %collective-permute-start.24 = (bf16[64,48,128]{2,1,0:T(8,128)(2,1)}, bf16[64,48,128]{2,1,0:T(8,128)(2,1)}, u32[]{:S(2)}, u32[]{:S(2)}) collective-permute-start(bf16[64,48,128]{2,1,0:T(8,128)(2,1)} %pad_maximum_fusion.3.refs_1_), channel_id=1, source_target_pairs={{0,4},{4,8},{8,12},{12,0},{16,20},{20,24},{24,28},{28,16},{32,36},... | collective-permute-start | bytes 2359304 | tf_op jit(solution)/shard_map/ppermute | solution.py:194
  137.0 15.7 %collective-permute-start.25 = (bf16[64,48,128]{2,1,0:T(8,128)(2,1)}, bf16[64,48,128]{2,1,0:T(8,128)(2,1)}, u32[]{:S(2)}, u32[]{:S(2)}) collective-permute-start(bf16[64,48,128]{2,1,0:T(8,128)(2,1)} %pad_maximum_fusion.4.refs_4_), channel_id=1, source_target_pairs={{0,32},{4,36},{8,40},{12,44},{16,48},{20,52},{24,56},{28,60},{32,6... | collective-permute-start | bytes 2359304 | tf_op jit(solution)/shard_map/ppermute | solution.py:198
  138.2 15.4 %collective-permute-start.26 = (bf16[64,48,128]{2,1,0:T(8,128)(2,1)}, bf16[64,48,128]{2,1,0:T(8,128)(2,1)}, u32[]{:S(2)}, u32[]{:S(2)}) collective-permute-start(bf16[64,48,128]{2,1,0:T(8,128)(2,1)} %pad_maximum_fusion.3.refs_1_), channel_id=1, source_target_pairs={{0,12},{4,0},{8,4},{12,8},{16,28},{20,16},{24,20},{28,24},{32,44},... | collective-permute-start | bytes 2359304 | tf_op jit(solution)/shard_map/ppermute | solution.py:194
  138.6 14.9 %collective-permute-start.27 = (bf16[64,48,128]{2,1,0:T(8,128)(2,1)}, bf16[64,48,128]{2,1,0:T(8,128)(2,1)}, u32[]{:S(2)}, u32[]{:S(2)}) collective-permute-start(bf16[64,48,128]{2,1,0:T(8,128)(2,1)} %pad_maximum_fusion.4.refs_4_), channel_id=1, source_target_pairs={{0,96},{4,100},{8,104},{12,108},{16,112},{20,116},{24,120},{28,124... | collective-permute-start | bytes 2359304 | tf_op jit(solution)/shard_map/ppermute | solution.py:198
  153.5 19.2 %collective-permute-start.28 = (bf16[64,48,128]{2,1,0:T(8,128)(2,1)}, bf16[64,48,128]{2,1,0:T(8,128)(2,1)S(1)}, u32[]{:S(2)}, u32[]{:S(2)}) collective-permute-start(bf16[64,48,128]{2,1,0:T(8,128)(2,1)} %collective-permute-done.24.refs_2_), channel_id=1, source_target_pairs={{0,4},{4,8},{8,12},{12,0},{16,20},{20,24},{24,28},{28,16},{32,36},... | collective-permute-start | bytes 2359304 | tf_op jit(solution)/shard_map/ppermute | solution.py:194
  154.2 19.8 %collective-permute-start.29 = (bf16[64,48,128]{2,1,0:T(8,128)(2,1)}, bf16[64,48,128]{2,1,0:T(8,128)(2,1)S(1)}, u32[]{:S(2)}, u32[]{:S(2)}) collective-permute-start(bf16[64,48,128]{2,1,0:T(8,128)(2,1)} %collective-permute-done.25.refs_5_), channel_id=1, source_target_pairs={{0,32},{4,36},{8,40},{12,44},{16,48},{20,52},{24,56},{28,60},{32,6... | collective-permute-start | bytes 2359304 | tf_op jit(solution)/shard_map/ppermute | solution.py:198
  154.2 19.8 %collective-permute-start.30 = (bf16[64,48,128]{2,1,0:T(8,128)(2,1)S(1)}, bf16[64,48,128]{2,1,0:T(8,128)(2,1)S(1)}, u32[]{:S(2)}, u32[]{:S(2)}) collective-permute-start(bf16[64,48,128]{2,1,0:T(8,128)(2,1)S(1)} %pad_maximum_fusion.1.refs_1_), channel_id=1, source_target_pairs={{0,12},{4,0},{8,4},{12,8},{16,28},{20,16},{24,20},{28,24},{32,44},... | collective-permute-start | bytes 2359304 | tf_op jit(solution)/shard_map/ppermute | solution.py:194
  156.2 17.7 %collective-permute-start.31 = (bf16[64,48,128]{2,1,0:T(8,128)(2,1)S(1)}, bf16[64,48,128]{2,1,0:T(8,128)(2,1)S(1)}, u32[]{:S(2)}, u32[]{:S(2)}) collective-permute-start(bf16[64,48,128]{2,1,0:T(8,128)(2,1)S(1)} %pad_maximum_fusion.2.refs_4_), channel_id=1, source_target_pairs={{0,96},{4,100},{8,104},{12,108},{16,112},{20,116},{24,120},{28,124... | collective-permute-start | bytes 2359304 | tf_op jit(solution)/shard_map/ppermute | solution.py:198
  174.0 24.4 %collective-permute-start.32 = (bf16[64,48,128]{2,1,0:T(8,128)(2,1)S(1)}, bf16[64,48,128]{2,1,0:T(8,128)(2,1)S(1)}, u32[]{:S(2)}, u32[]{:S(2)}) collective-permute-start(bf16[64,48,128]{2,1,0:T(8,128)(2,1)S(1)} %pad_maximum_fusion.1.refs_1_), channel_id=1, source_target_pairs={{0,4},{4,8},{8,12},{12,0},{16,20},{20,24},{24,28},{28,16},{32,36},... | collective-permute-start | bytes 2359304 | tf_op jit(solution)/shard_map/ppermute | solution.py:194
  174.1 24.3 %collective-permute-start.33 = (bf16[64,48,128]{2,1,0:T(8,128)(2,1)S(1)}, bf16[64,48,128]{2,1,0:T(8,128)(2,1)}, u32[]{:S(2)}, u32[]{:S(2)}) collective-permute-start(bf16[64,48,128]{2,1,0:T(8,128)(2,1)S(1)} %pad_maximum_fusion.2.refs_4_), channel_id=1, source_target_pairs={{0,32},{4,36},{8,40},{12,44},{16,48},{20,52},{24,56},{28,60},{32,6... | collective-permute-start | bytes 2359304 | tf_op jit(solution)/shard_map/ppermute | solution.py:198
  176.2 22.2 %collective-permute-start.34 = (bf16[64,48,128]{2,1,0:T(8,128)(2,1)S(1)}, bf16[64,48,128]{2,1,0:T(8,128)(2,1)}, u32[]{:S(2)}, u32[]{:S(2)}) collective-permute-start(bf16[64,48,128]{2,1,0:T(8,128)(2,1)S(1)} %collective-permute-done.30.refs_3_), channel_id=1, source_target_pairs={{0,12},{4,0},{8,4},{12,8},{16,28},{20,16},{24,20},{28,24},{32,44},... | collective-permute-start | bytes 2359304 | tf_op jit(solution)/shard_map/ppermute | solution.py:194
  178.8 19.6 %collective-permute-start.35 = (bf16[64,48,128]{2,1,0:T(8,128)(2,1)S(1)}, bf16[64,48,128]{2,1,0:T(8,128)(2,1)}, u32[]{:S(2)}, u32[]{:S(2)}) collective-permute-start(bf16[64,48,128]{2,1,0:T(8,128)(2,1)S(1)} %collective-permute-done.31.refs_6_), channel_id=1, source_target_pairs={{0,96},{4,100},{8,104},{12,108},{16,112},{20,116},{24,120},{28,124... | collective-permute-start | bytes 2359304 | tf_op jit(solution)/shard_map/ppermute | solution.py:198
  202.0 29.3 %collective-permute-start.36 = (bf16[1,512,1024]{2,1,0:T(8,128)(2,1)}, bf16[1,512,1024]{2,1,0:T(8,128)(2,1)S(1)}, u32[]{:S(2)}, u32[]{:S(2)}) collective-permute-start(bf16[1,512,1024]{2,1,0:T(8,128)(2,1)} %slice.195), channel_id=1, source_target_pairs={{0,1},{1,0},{2,3},{3,2},{4,5},{5,4},{6,7},{7,6},{8,9},{9,8},{10,11... | collective-permute-start | bytes 3145736 | tf_op jit(solution)/shard_map/ppermute | solution.py:283
  232.3 25.3 %collective-permute-start.38 = (bf16[512,1024]{1,0:T(8,128)(2,1)S(1)}, bf16[512,1024]{1,0:T(8,128)(2,1)S(1)}, u32[]{:S(2)}, u32[]{:S(2)}) collective-permute-start(bf16[512,1024]{1,0:T(8,128)(2,1)S(1)} %fusion), channel_id=1, source_target_pairs={{0,2},{1,3},{2,0},{3,1},{4,6},{5,7},{6,4},{7,5},{8,10},{9,11},{10,... | collective-permute-start | bytes 3145736 | tf_op jit(solution)/shard_map/ppermute | solution.py:287
  263.0 24.5 %collective-permute-start.40 = (bf16[512,1024]{1,0:T(8,128)(2,1)S(1)}, bf16[512,1024]{1,0:T(8,128)(2,1)S(1)}, u32[]{:S(2)}, u32[]{:S(2)}) collective-permute-start(bf16[512,1024]{1,0:T(8,128)(2,1)S(1)} %fusion.1), channel_id=1, source_target_pairs={{0,2},{1,3},{2,0},{3,1},{4,6},{5,7},{6,4},{7,5},{8,10},{9,11},{10,... | collective-permute-start | bytes 3145736 | tf_op jit(solution)/shard_map/ppermute | solution.py:287
  (32 other events, 264.1 us)

commit v3 on v2

v3 whole, which is shorter than its diff:
```python
import math

import jax
import jax.numpy as jnp
import numpy as np
from jax import lax
from jax.experimental import pallas as pl
from jax.experimental.pallas import tpu as pltpu

NFFT, BINS, LAGS, BLOCK, STEPS, SUB = 2048, 512, 512, 64, 2, 48
EPS = 1e-6
F32, BF = jnp.float32, jnp.bfloat16
VMEM = pltpu.CompilerParams(vmem_limit_bytes=56 * 2**20)
SB = 16
KC = 64
CHUNKS = BINS // KC
HALF = BINS // 2


def whiten_kernel(place, spec, counts, *refs):
    own, pieces, work = refs[0], refs[1:-1], refs[-1]
    base = pl.program_id(0) * SB
    live = counts[...]
    for s in range(SB):
        v = spec[s].astype(F32)
        power = jnp.mean(v * v, axis=-1, keepdims=True)
        mask = (base + s < live).astype(F32)
        n = v * lax.rsqrt(power + EPS) * mask
        work[s] = jnp.concatenate([n[:, :BINS], n[:, BINS:]], axis=0).T
    own[...] = jnp.swapaxes(work[...], 0, 1).astype(BF)
    for m, piece in enumerate(pieces):
        piece[...] = own[pl.ds(pl.multiple_of(place[m] * KC, KC), KC)]


def whiten(place, spectra, counts):
    n = place.shape[0]
    return pl.pallas_call(
        whiten_kernel,
        grid_spec=pltpu.PrefetchScalarGridSpec(
            num_scalar_prefetch=1,
            grid=(SUB // SB,),
            in_specs=[
                pl.BlockSpec((SB, BLOCK, 2 * BINS), lambda i, p: (i, 0, 0)),
                pl.BlockSpec((BLOCK, 1), lambda i, p: (0, 0)),
            ],
            out_specs=[pl.BlockSpec((BINS, SB, 128), lambda i, p: (0, i, 0))]
            + [pl.BlockSpec((KC, SB, 128), lambda i, p: (0, i, 0))] * n,
            scratch_shapes=[pltpu.VMEM((SB, BINS, 128), F32)],
        ),
        out_shape=[jax.ShapeDtypeStruct((BINS, SUB, 128), BF)]
        + [jax.ShapeDtypeStruct((KC, SUB, 128), BF)] * n,
        compiler_params=VMEM,
        cost_estimate=pl.CostEstimate(flops=10**8, bytes_accessed=18 * 10**6, transcendentals=0),
        name="whiten",
    )(place, spectra, counts[:, None])


def choose(scalars, inputs, shapes, tasks):
    n = len(inputs)

    def kernel(*refs):
        s, ins, outs, sems = refs[0], refs[1 : 1 + n], refs[1 + n : -1], refs[-1]
        copies = []
        for m, (dst, which, sources) in enumerate(tasks):
            options = [pltpu.make_async_copy(src(ins, s), dst(outs), sems.at[m]) for src in sources]
            for number, copy in enumerate(options):
                @pl.when(s[which] == number)
                def _(copy=copy):
                    copy.start()
            copies.append(options[0])
        for copy in copies:
            copy.wait()

    anywhere = pl.BlockSpec(memory_space=pl.ANY)
    return pl.pallas_call(
        kernel,
        grid_spec=pltpu.PrefetchScalarGridSpec(
            num_scalar_prefetch=1,
            grid=(1,),
            in_specs=[anywhere] * n,
            out_specs=[pl.BlockSpec(shape, lambda i, s, n=len(shape): (0,) * n) for shape in shapes],
            scratch_shapes=[pltpu.SemaphoreType.DMA((len(tasks),))],
        ),
        out_shape=[jax.ShapeDtypeStruct(shape, BF) for shape in shapes],
        compiler_params=VMEM,
        cost_estimate=pl.CostEstimate(flops=10**6, bytes_accessed=6 * 10**6, transcendentals=0),
        name="choose",
    )(scalars, *inputs)


def turn_kernel(own, rot):
    v = own[...]
    rot[...] = jnp.concatenate([v[..., BLOCK:], -v[..., :BLOCK]], axis=-1)


def turn(own):
    blk = pl.BlockSpec((KC, SUB, 128), lambda i: (i, 0, 0))
    return pl.pallas_call(
        turn_kernel,
        grid=(CHUNKS,),
        in_specs=[blk],
        out_specs=blk,
        out_shape=jax.ShapeDtypeStruct((BINS, SUB, 128), BF),
        compiler_params=VMEM,
        cost_estimate=pl.CostEstimate(flops=10**6, bytes_accessed=25 * 10**6, transcendentals=0),
        name="turn",
    )(own)


def corr_kernel(place, order, *refs):
    pieces = refs[:CHUNKS]
    own, rot, inv, table = refs[CHUNKS : CHUNKS + 4]
    outs = refs[CHUNKS + 4 : CHUNKS + 8]
    src, work, rows, sems = refs[CHUNKS + 8 :]
    step = pl.program_id(0)
    copies = [pltpu.make_async_copy(piece, src.at[m], sems.at[m]) for m, piece in enumerate(pieces)]

    @pl.when(step == 0)
    def _():
        for copy in copies:
            copy.start()

    for m, copy in enumerate(copies):
        @pl.when(step == m)
        def _(copy=copy):
            copy.wait()

    for k in range(KC):
        x = src[step, k].T
        h = jnp.dot(x[:BLOCK], own[k], preferred_element_type=F32)
        h += jnp.dot(x[BLOCK:], rot[k], preferred_element_type=F32)
        work[k] = h
    z = jnp.swapaxes(work[...], 0, 1)
    off = pl.multiple_of(place[step] * KC, KC)
    low = lax.broadcasted_iota(jnp.int32, (KC, 128), 1) < BLOCK
    for p in range(BLOCK // 2):
        u, v = z[2 * p], z[2 * p + 1]
        lanes = slice(p % 2 * 128, p % 2 * 128 + 128)
        rows[p // 2, pl.ds(off, KC), lanes] = jnp.where(low, u, pltpu.roll(v, 64, 1)).astype(BF)
        rows[p // 2, pl.ds(off + BINS, KC), lanes] = jnp.where(low, pltpu.roll(u, 64, 1), v).astype(BF)

    @pl.when(step == CHUNKS - 1)
    def _():
        for m in range(4):
            block = order[m]
            for q in range(4):
                y = jnp.dot(table[...], rows[4 * block + q], preferred_element_type=F32)
                cols = slice(q * 256, q * 256 + 256)
                outs[m][:, cols] = (y * inv[block, :, cols]).astype(BF)


def corr(place, order, pieces, own, rot, inv, table):
    here = pl.BlockSpec((KC, SUB, 128), lambda i, p, o: (p[i], 0, 0))
    return pl.pallas_call(
        corr_kernel,
        grid_spec=pltpu.PrefetchScalarGridSpec(
            num_scalar_prefetch=2,
            grid=(CHUNKS,),
            in_specs=[pl.BlockSpec(memory_space=pl.ANY)] * CHUNKS
            + [
                here,
                here,
                pl.BlockSpec((4, 1, 1024), lambda i, p, o: (0, 0, 0)),
                pl.BlockSpec((LAGS, 2 * BINS), lambda i, p, o: (0, 0)),
            ],
            out_specs=[pl.BlockSpec((LAGS, 1024), lambda i, p, o: (0, 0))] * 4,
            scratch_shapes=[
                pltpu.VMEM((CHUNKS, KC, SUB, 128), BF),
                pltpu.VMEM((KC, BLOCK, 128), F32),
                pltpu.VMEM((BLOCK // 4, 2 * BINS, 256), BF),
                pltpu.SemaphoreType.DMA((CHUNKS,)),
            ],
        ),
        out_shape=[jax.ShapeDtypeStruct((LAGS, 1024), BF)] * 4,
        compiler_params=VMEM,
        cost_estimate=pl.CostEstimate(flops=22 * 10**9, bytes_accessed=40 * 10**6, transcendentals=0),
        name="corr",
    )(place, order, *pieces, own, rot, inv, table)


def finish_kernel(a, b, c, *refs):
    total = a[...].astype(F32) + b[...].astype(F32) + c[...].astype(F32)
    refs[-1][0] = total.T.astype(BF)


def finish(step, near, near_got, far_sum, base=None):
    cols = 512
    extra = [] if base is None else [base]
    return pl.pallas_call(
        finish_kernel,
        grid=(1024 // cols,),
        in_specs=[pl.BlockSpec((LAGS, cols), lambda j: (0, j))] * 3
        + [pl.BlockSpec(memory_space=pl.ANY)] * len(extra),
        out_specs=pl.BlockSpec((1, cols, LAGS), lambda j: (step, j, 0)),
        out_shape=jax.ShapeDtypeStruct((STEPS, 1024, LAGS), BF),
        input_output_aliases={3: 0} if extra else {},
        compiler_params=VMEM,
        name="finish",
    )(near, near_got, far_sum, *extra)


def lag_table():
    k = np.arange(1, BINS + 1)[None, :]
    tau = np.arange(LAGS)[:, None] - LAGS // 2
    ph = ((k * tau) % NFFT) * (2 * np.pi / NFFT)
    w = np.concatenate([np.cos(ph), -np.sin(ph)], axis=1) / math.sqrt(BINS)
    return jnp.asarray(w, BF)


def along_x(a, d):
    return lax.ppermute(a, "station", [(s, s - s % 4 + (s + d) % 4) for s in range(32)])


def along_z(a, d):
    return lax.ppermute(a, "station", [(s, (s + 8 * d) % 32) for s in range(32)])


def swap_y(a):
    return lax.ppermute(a, "station", [(s, s ^ 4) for s in range(32)])


def cut(a, index, size):
    return lax.dynamic_slice_in_dim(a, index * size, size, 0)


def pick(which, options):
    out = options[0]
    for n in range(1, 4):
        out = jnp.where(which == n, options[n], out)
    return out


def barrier(*arrays):
    return lax.optimization_barrier(arrays)


def spread(sends, shifts, work=None, args=()):
    n = len(sends)
    held = barrier(*sends, *args)
    got = [shift(a) for a, shift in zip(held[:n], shifts)]
    done = list(work(*held[n:])) if work else []
    return barrier(*got, *done)


HOPS = (1, 2, 3)
TO_X = [lambda a, d=d: along_x(a, d) for d in HOPS]
TO_Z = [lambda a, d=d: along_z(a, d) for d in HOPS]


def broadcast(own, ready, marks, roots, z, h, x):
    got = spread(ready, TO_X + TO_Z)

    def own_a(q):
        return lambda ins, s: ins[0].at[pl.ds(s[4] * 64 + s[q] * 16, 16)]

    def own_b(q):
        return lambda ins, s: ins[0].at[pl.ds(s[5] * 64 + s[q] * 16, 16)]

    def came(n, q):
        return lambda ins, s: ins[n].at[pl.ds(s[q] * 16, 16)]

    scalars = jnp.stack(
        [(x - r[2]) & 3 for r in roots]
        + [(z - r[0]) & 3 for r in roots]
        + [x, 4 + z]
        + [(z + d) & 3 for d in range(4)]
        + [(x + d) & 3 for d in range(4)]
    ).astype(jnp.int32)
    tasks = []
    for d in range(4):
        for i in range(STEPS):
            tasks.append(
                (lambda outs, d=d, i=i: outs[d].at[i], i, [own_a(6 + d)] + [came(n, 6 + d) for n in (1, 2, 3)])
            )
            tasks.append(
                (lambda outs, d=d, i=i: outs[4 + d].at[i], 2 + i, [own_b(10 + d)] + [came(n, 10 + d) for n in (4, 5, 6)])
            )
    cuts = choose(scalars, [own, *got], [(STEPS, 16, SUB, 128)] * 8, tasks)
    got = spread(cuts[1:4] + cuts[5:], TO_Z + TO_X)
    got_a = [cuts[0], *got[:3]]
    got_b = [cuts[4], *got[3:]]
    mine = jnp.stack(
        [
            jnp.stack([pick((z - r[0]) & 3, [g[i] for g in got_a]) for i, r in enumerate(roots)]),
            jnp.stack([pick((x - r[2]) & 3, [g[i] for g in got_b]) for i, r in enumerate(roots)]),
        ]
    )

    def hops(marks):
        for shift in (TO_X[1], TO_Z[0]):
            marks = jnp.stack([marks, shift(marks)])
        return [marks]

    other, marks = spread([mine], [swap_y], hops, [marks])
    sub = [
        jnp.stack([jnp.where(h == r[1], mine[n, i], other[n, i]) for i, r in enumerate(roots)])
        for n in range(2)
    ]
    got = spread([sub[0]] * 3 + [sub[1]] * 3, TO_Z + TO_X)
    all_a = [sub[0], *got[:3]]
    all_b = [sub[1], *got[3:6]]
    out = []
    for i in range(STEPS):
        a = jnp.concatenate([pick((z - q) & 3, [v[i] for v in all_a]) for q in range(4)])
        b = jnp.concatenate([pick((x - q) & 3, [v[i] for v in all_b]) for q in range(4)])
        out.append((a, b))
    return out, marks


def other_core(a):
    return lax.ppermute(a, "tm", [(t, t ^ 1) for t in range(4)])


def other_chip(a):
    return lax.ppermute(a, "tm", [(t, t ^ 2) for t in range(4)])


def add(a, b):
    return (a.astype(F32) + b.astype(F32)).astype(BF)


def body(spectra, counts, block_ids):
    counts = counts[0]
    table = lag_table()
    station, tm = lax.axis_index("station"), lax.axis_index("tm")
    z, h, x = station >> 3, station >> 2 & 1, station & 3

    def places(*list_of):
        return jnp.stack(list_of).astype(jnp.int32)

    ahead = places(*[(x + d) & 3 for d in HOPS], *[4 + ((z + d) & 3) for d in HOPS])
    next_counts, own, *ready = spread(
        [counts], [TO_X[0]], lambda *a: whiten(*a), [ahead, spectra[0], counts]
    )
    marks = jnp.stack([counts, next_counts])
    roots = [(block_ids[i] >> 3, block_ids[i] >> 2 & 1, block_ids[i] & 3) for i in range(STEPS)]
    ((a0, b0), (a1, b1)), marks = broadcast(own, ready, marks, roots, z, h, x)

    place = places(
        *[(x + d) & 3 for d in (0, 3, 1, 2)], *[4 + ((z + d) & 3) for d in (0, 3, 1, 2)]
    )
    order = places((tm ^ 2) ^ 1, tm ^ 2, tm ^ 1, tm)

    def scales(marks):
        out = []
        for r in roots:
            dz, dx = (z - r[0]) & 3, (x - r[2]) & 3
            src_counts = marks[h ^ r[1], dz >> 1, dz & 1, dx >> 1, dx & 1]
            inv = 1.0 / jnp.minimum(src_counts[:, None], counts[None, :]).astype(F32)
            out.append(inv.reshape(4, 1, 1024))
        return out

    up, down = [TO_X[0], TO_Z[0]], [TO_X[2], TO_Z[2]]
    a0_up, b0_up, a0_down, b0_down, far_marks, rot = spread(
        [a0, b0, a0, b0, marks], up + down + [TO_Z[1]], lambda v: [turn(v)], [own]
    )
    marks = jnp.stack([marks, far_marks])
    a0_far, b0_far, a1_down, b1_down, far_marks = spread(
        [a0_up, b0_up, a1, b1, marks], up + down + [swap_y]
    )
    inv0, inv1 = scales(jnp.stack([marks, far_marks]))
    a1_up, b1_up, a1_far, b1_far, *lag0 = spread(
        [a1, b1, a1_down, b1_down],
        up + down,
        lambda *v: corr(place, order, v[:8], *v[8:], table),
        [a0, a0_up, a0_down, a0_far, b0, b0_up, b0_down, b0_far, own, rot, inv0],
    )
    far_got, near_got0 = spread([lag0[0], lag0[2]], [other_core] * 2)
    far_sum0, *lag1 = spread(
        [add(lag0[1], far_got)],
        [other_chip],
        lambda *v: corr(place, order, v[:8], *v[8:], table),
        [a1, a1_up, a1_down, a1_far, b1, b1_up, b1_down, b1_far, own, rot, inv1],
    )
    far_got, near_got1 = spread([lag1[0], lag1[2]], [other_core] * 2)
    far_sum1, out = spread(
        [add(lag1[1], far_got)],
        [other_chip],
        lambda *v: [finish(0, *v)],
        [lag0[3], near_got0, far_sum0],
    )
    out = finish(1, lag1[3], near_got1, far_sum1, out)
    return out.reshape(STEPS, 16, BLOCK, LAGS)


def solution(mesh):
    from jax.sharding import PartitionSpec as P

    return jax.shard_map(
        body,
        mesh=mesh,
        in_specs=(P("tm", None, "station", None), P("tm", "station"), P()),
        out_specs=P(None, "tm", "station", None),
        check_vma=False,
    )
```

time: 298 us -> 275 us (0.923)
  Pallas kernels: 84.2 us -> 72.7 us
  local copies, waits for them, and re-layouts: 18.3 us -> 6.8 us
  waiting for transfers between devices: 76.7 us -> 87.2 us
  other arithmetic: 16.9 us -> 8.36 us
    ppermute x4, starting transfers between devices: 27.9 us -> 7.83 us  [other_core(): return lax.ppermute(a, 'tm', [(t, t ^ 1) for t in range(4)])]
    pallas_call x8 -> x4, Pallas kernels: 69.4 us -> 57.6 us  [the longest x2 41.3 us: corr(): pl.pallas_call(corr_kernel, grid_spec=pltpu.PrefetchScalarGridSpec(num_sc...]
    ppermute x17, starting transfers between devices: 23.4 us -> 34.4 us  [along_x(): lax.ppermute(a, 'station', [(s, s - s % 4 + (s + d) % 4) for s in range(3...]
    ppermute x17, waiting for transfers between devices: 37.6 us -> 46.5 us  [along_x(): lax.ppermute(a, 'station', [(s, s - s % 4 + (s + d) % 4) for s in range(3...]
    ppermute x2, waiting for transfers between devices: 15.3 us -> 22.5 us  [other_chip(): return lax.ppermute(a, 'tm', [(t, t ^ 2) for t in range(4)])]
    slice x5 -> x1, local copies, waits for them, and re-layouts: 7.58 us -> 0.65 us  [body(): block_ids[i] & 3]
    another operation x12 -> x4, other arithmetic: 6.58 us -> 0.06 us  [the longest x2 0.05 us: body(): inv0, inv1 = scales(jnp.stack([marks, far_marks]))]
    dynamic_slice x2 -> x0, local copies, waits for them, and re-layouts: 5.05 us -> none  [the longest x1 4.39 us: cut(): return lax.dynamic_slice_in_dim(a, index * size, size, 0)]
  transfers between devices with their start and end apart: 42 -> 42, of which waited for: 24 -> 22; matrix products, arithmetic and copies ran while one was open for 3% -> 2% of each run, Pallas kernels for 27% -> 24%
where the time goes in v3:
time: 275 us; the launch traced here: 274 us
  starting transfers between devices  94.9 us (35%)
  waiting for transfers between devices  87.2 us (32%)
  Pallas kernels  72.7 us (26%)
  other arithmetic  8.36 us (3%)
  local copies, waits for them, and re-layouts  6.8 us (2%)
  between operations  4.2 us (2%)
    ppermute x17, waiting for transfers between devices, along_x(): lax.ppermute(a, 'station', [(s, s - s % 4 + (s + d) % 4) for s in range(3...  46.5 us
    pallas_call x2, Pallas kernels, corr(): pl.pallas_call(corr_kernel, grid_spec=pltpu.PrefetchScalarGridSpec(num_sc...  41.3 us
    ppermute x17, starting transfers between devices, along_x(): lax.ppermute(a, 'station', [(s, s - s % 4 + (s + d) % 4) for s in range(3...  34.4 us
    ppermute x17, starting transfers between devices, along_z(): lax.ppermute(a, 'station', [(s, (s + 8 * d) % 32) for s in range(32)])  31.7 us
    ppermute x2, waiting for transfers between devices, other_chip(): return lax.ppermute(a, 'tm', [(t, t ^ 2) for t in range(4)])  22.5 us
    ppermute x2, starting transfers between devices, swap_y(): return lax.ppermute(a, 'station', [(s, s ^ 4) for s in range(32)])  13.9 us
    pallas_call x1, Pallas kernels, whiten(): pl.pallas_call(whiten_kernel, grid_spec=pltpu.PrefetchScalarGridSpec(num_...  11.9 us
    ppermute x17, waiting for transfers between devices, along_z(): lax.ppermute(a, 'station', [(s, (s + 8 * d) % 32) for s in range(32)])  10.2 us
  transfers between devices with their start and end apart: 42, of which 22 were waited for; matrix products, arithmetic and copies ran while one was open for 2% of the time, Pallas kernels for 24%

profile of v3, /device:TPU:1, one launch (start us, length us, event | category | flops | bytes accessed | tf_op | source)
XLA Modules:
  0.0 274.2 jit_solution(16337676246832640099)
XLA Ops:
  4.1 11.9 %whiten.1 = (bf16[512,48,128]{2,1,0:T(8,128)(2,1)}, bf16[64,48,128]{2,1,0:T(8,128)(2,1)}, bf16[64,48,128]{2,1,0:T(8,128)(2,1)}, bf16[64,48,128]{2,1,0:T(8,128)(2...) custom-call(s32[6]{0:T(128)} %stack.177.place, ...), custom_call_target="tpu_custom_call" | custom-call | flops 100000000 | bytes 18000000 | tf_op jit(solution)/shard_map/whiten/pallas_call | solution.py:37
  22.2 3.3 %collective-permute-start.5 = (bf16[64,48,128]{2,1,0:T(8,128)(2,1)}, bf16[64,48,128]{2,1,0:T(8,128)(2,1)}, u32[]{:S(2)}, u32[]{:S(2)}) collective-permute-start(bf16[64,48,128]{2,1,0:T(8,128)(2,1)} %get-tuple-element.178), channel_id=1, source_target_pairs={{0,64},{4,68},{8,72},{12,76},{16,80},{20,84},{24,88},{28,92},{32,9... | collective-permute-start | bytes 2359304 | tf_op jit(solution)/shard_map/ppermute | solution.py:215
  25.5 10.4 %collective-permute-done.1.refs_2_ = bf16[64,48,128]{2,1,0:T(8,128)(2,1)S(1)} collective-permute-done((bf16[64,48,128]{2,1,0:T(8,128)(2,1)}, bf16[64,48,128]{2,1,0:T(8,128)(2,1)S(1)}, u32[]{:S(2)}, u32[]{:S(2)}) %collective-permute-start.1) | collective-permute-done | bytes 786464 | tf_op jit(solution)/shard_map/ppermute | solution.py:211
  35.8 3.5 %collective-permute-start.6 = (bf16[64,48,128]{2,1,0:T(8,128)(2,1)}, bf16[64,48,128]{2,1,0:T(8,128)(2,1)}, u32[]{:S(2)}, u32[]{:S(2)}) collective-permute-start(bf16[64,48,128]{2,1,0:T(8,128)(2,1)} %get-tuple-element.179), channel_id=1, source_target_pairs={{0,96},{4,100},{8,104},{12,108},{16,112},{20,116},{24,120},{28,124... | collective-permute-start | bytes 2359304 | tf_op jit(solution)/shard_map/ppermute | solution.py:215
  43.2 9.0 %collective-permute-done.2.refs_3_ = bf16[64,48,128]{2,1,0:T(8,128)(2,1)S(1)} collective-permute-done((bf16[64,48,128]{2,1,0:T(8,128)(2,1)}, bf16[64,48,128]{2,1,0:T(8,128)(2,1)S(1)}, u32[]{:S(2)}, u32[]{:S(2)}) %collective-permute-start.2) | collective-permute-done | bytes 786464 | tf_op jit(solution)/shard_map/ppermute | solution.py:211
  53.4 5.0 %collective-permute-done.5.refs_6_ = bf16[64,48,128]{2,1,0:T(8,128)(2,1)} collective-permute-done((bf16[64,48,128]{2,1,0:T(8,128)(2,1)}, bf16[64,48,128]{2,1,0:T(8,128)(2,1)}, u32[]{:S(2)}, u32[]{:S(2)}) %collective-permute-start.5) | collective-permute-done | bytes 786464 | tf_op jit(solution)/shard_map/ppermute | solution.py:215
  58.4 4.4 %choose.1 = (bf16[2,16,48,128]{3,2,1,0:T(8,128)(2,1)}, bf16[2,16,48,128]{3,2,1,0:T(8,128)(2,1)}, bf16[2,16,48,128]{3,2,1,0:T(8,128)(2,1)}, bf16[2,16,48,128]{3,2...) custom-call(s32[14]{0:T(128)} %stack.173.refs_0_, ...), custom_call_target="tpu_custom_call" | custom-call | flops 1000000 | bytes 6000000 | tf_op jit(solution)/shard_map/choose/pallas_call | solution.py:75
  65.6 2.8 %collective-permute-start.7 = (bf16[2,16,48,128]{3,2,1,0:T(8,128)(2,1)}, bf16[2,16,48,128]{3,2,1,0:T(8,128)(2,1)S(1)}, u32[]{:S(2)}, u32[]{:S(2)}) collective-permute-start(bf16[2,16,48,128]{3,2,1,0:T(8,128)(2,1)} %get-tuple-element.192), channel_id=1, source_target_pairs={{0,32},{4,36},{8,40},{12,44},{16,48},{20,52},{24,56},{28,60},{32,6... | collective-permute-start | bytes 1179656 | tf_op jit(solution)/shard_map/ppermute | solution.py:215
  71.6 7.7 %collective-permute-done.11 = bf16[2,16,48,128]{3,2,1,0:T(8,128)(2,1)S(1)} collective-permute-done((bf16[2,16,48,128]{3,2,1,0:T(8,128)(2,1)}, bf16[2,16,48,128]{3,2,1,0:T(8,128)(2,1)S(1)}, u32[]{:S(2)}, u32[]{:S(2)}) %collective-permute-start.11) | collective-permute-done | bytes 393248 | tf_op jit(solution)/shard_map/ppermute | solution.py:211
  81.7 6.9 %collective-permute-start.13 = (bf16[2,2,16,48,128]{4,3,2,1,0:T(8,128)(2,1)S(1)}, bf16[2,2,16,48,128]{4,3,2,1,0:T(8,128)(2,1)S(1)}, u32[]{:S(2)}, u32[]{:S(2)}) collective-permute-start(bf16[2,2,16,48,128]{4,3,2,1,0:T(8,128)(2,1)S(1)} %pad_maximum_fusion), channel_id=1, source_target_pairs={{0,16},{4,20},{8,24},{12,28},{16,0},{20,4},{24,8},{28,12},{32,48},... | collective-permute-start | bytes 2359304 | tf_op jit(solution)/shard_map/ppermute | solution.py:219
  88.6 3.1 %collective-permute-start.14 = (s32[2,64]{1,0:T(2,128)S(1)}, s32[2,64]{1,0:T(2,128)S(1)}, u32[]{:S(2)}, u32[]{:S(2)}) collective-permute-start(s32[2,64]{1,0:T(2,128)S(1)} %pad_add_fusion.3), channel_id=1, source_target_pairs={{0,8},{4,12},{8,0},{12,4},{16,24},{20,28},{24,16},{28,20},{32,40},... | collective-permute-start | bytes 1544 | tf_op jit(solution)/shard_map/ppermute | solution.py:211
  92.6 4.0 %collective-permute-start.15 = (s32[2,2,64]{2,1,0:T(2,128)S(1)}, s32[2,2,64]{2,1,0:T(2,128)S(1)}, u32[]{:S(2)}, u32[]{:S(2)}) collective-permute-start(s32[2,2,64]{2,1,0:T(2,128)S(1)} %get-tuple-element.340), channel_id=1, source_target_pairs={{0,32},{4,36},{8,40},{12,44},{16,48},{20,52},{24,56},{28,60},{32,6... | collective-permute-start | bytes 3080 | tf_op jit(solution)/shard_map/ppermute | solution.py:215
  98.9 2.7 collective-permute-start.16
  104.0 7.3 %collective-permute-start.19 = (bf16[2,16,48,128]{3,2,1,0:T(8,128)(2,1)S(1)}, bf16[2,16,48,128]{3,2,1,0:T(8,128)(2,1)S(1)}, u32[]{:S(2)}, u32[]{:S(2)}) collective-permute-start(bf16[2,16,48,128]{3,2,1,0:T(8,128)(2,1)S(1)} %pad_maximum_fusion.6), channel_id=1, source_target_pairs={{0,4},{4,8},{8,12},{12,0},{16,20},{20,24},{24,28},{28,16},{32,36},... | collective-permute-start | bytes 1179656 | tf_op jit(solution)/shard_map/ppermute | solution.py:211
  111.2 3.6 %collective-permute-start.20 = (bf16[2,16,48,128]{3,2,1,0:T(8,128)(2,1)S(1)}, bf16[2,16,48,128]{3,2,1,0:T(8,128)(2,1)S(1)}, u32[]{:S(2)}, u32[]{:S(2)}) collective-permute-start(bf16[2,16,48,128]{3,2,1,0:T(8,128)(2,1)S(1)} %pad_maximum_fusion.6), channel_id=1, source_target_pairs={{0,8},{4,12},{8,0},{12,4},{16,24},{20,28},{24,16},{28,20},{32,40},... | collective-permute-start | bytes 1179656 | tf_op jit(solution)/shard_map/ppermute | solution.py:211
  116.9 11.3 %collective-permute-done.20 = bf16[2,16,48,128]{3,2,1,0:T(8,128)(2,1)S(1)} collective-permute-done((bf16[2,16,48,128]{3,2,1,0:T(8,128)(2,1)S(1)}, bf16[2,16,48,128]{3,2,1,0:T(8,128)(2,1)S(1)}, u32[]{:S(2)}, u32[]{:S(2)}) %collective-permute-start.20) | collective-permute-done | bytes 393248 | tf_op jit(solution)/shard_map/ppermute | solution.py:211
  129.7 3.7 %collective-permute-start.22 = (bf16[64,48,128]{2,1,0:T(8,128)(2,1)S(1)}, bf16[64,48,128]{2,1,0:T(8,128)(2,1)}, u32[]{:S(2)}, u32[]{:S(2)}) collective-permute-start(bf16[64,48,128]{2,1,0:T(8,128)(2,1)S(1)} %pad_maximum_fusion.3.refs_0_), channel_id=1, source_target_pairs={{0,4},{4,8},{8,12},{12,0},{16,20},{20,24},{24,28},{28,16},{32,36},... | collective-permute-start | bytes 2359304 | tf_op jit(solution)/shard_map/ppermute | solution.py:211
  137.5 9.4 %turn.1.refs_9_ = bf16[512,48,128]{2,1,0:T(8,128)(2,1)} custom-call(bf16[512,48,128]{2,1,0:T(8,128)(2,1)} %get-tuple-element.283.refs_1_.own.refs_8_), custom_call_target="tpu_custom_call" | custom-call | flops 1000000 | bytes 25000000 | tf_op jit(solution)/shard_map/turn/pallas_call | solution.py:98
  153.8 2.4 collective-permute-start.30
  156.2 7.0 %collective-permute-start.31 = (s32[2,2,2,2,64]{4,3,2,1,0:T(2,128)S(1)}, s32[2,2,2,2,64]{4,3,2,1,0:T(2,128)S(1)}, u32[]{:S(2)}, u32[]{:S(2)}) collective-permute-start(s32[2,2,2,2,64]{4,3,2,1,0:T(2,128)S(1)} %get-tuple-element.236), channel_id=1, source_target_pairs={{0,16},{4,20},{8,24},{12,28},{16,0},{20,4},{24,8},{28,12},{32,48},... | collective-permute-start | bytes 12296 | tf_op jit(solution)/shard_map/ppermute | solution.py:219
  164.6 2.4 collective-permute-done.27.refs_3_
  170.3 2.6 collective-permute-start.34
  175.2 20.7 %corr.2 = (bf16[512,1024]{1,0:T(8,128)(2,1)}, bf16[512,1024]{1,0:T(8,128)(2,1)}, bf16[512,1024]{1,0:T(8,128)(2,1)}, bf16[512,1024]{1,0:T(8,128)(2,1)}) custom-call(s32[8]{0:T(128)} %stack.200.place, s32[4]{0:T(128)} %pad_add_fusion.4.order, bf16[64,48,128]{2,1,0:T(8,128)(2,1)} %copy-done.6, bf16[64,48,128]{2,1,0:T(8,128)(2,1)} %collective-permute-done.22.refs_1_, ...), custom_call_target="tpu_custom_call" | custom-call | flops 22000001024 | bytes 40000000 | tf_op jit(solution)/shard_map/corr/pallas_call | solution.py:154
  197.2 6.9 %collective-permute-start.36 = (bf16[512,1024]{1,0:T(8,128)(2,1)}, bf16[512,1024]{1,0:T(8,128)(2,1)S(1)}, u32[]{:S(2)}, u32[]{:S(2)}) collective-permute-start(bf16[512,1024]{1,0:T(8,128)(2,1)} %get-tuple-element.267), channel_id=1, source_target_pairs={{0,1},{1,0},{2,3},{3,2},{4,5},{5,4},{6,7},{7,6},{8,9},{9,8},{10,11... | collective-permute-start | bytes 3145736 | tf_op jit(solution)/shard_map/ppermute | solution.py:311
  204.1 2.5 collective-permute-done.36
  210.1 5.6 %collective-permute-start.38 = (bf16[512,1024]{1,0:T(8,128)(2,1)S(1)}, bf16[512,1024]{1,0:T(8,128)(2,1)S(1)}, u32[]{:S(2)}, u32[]{:S(2)}) collective-permute-start(bf16[512,1024]{1,0:T(8,128)(2,1)S(1)} %add_convert_fusion.1), channel_id=1, source_target_pairs={{0,2},{1,3},{2,0},{3,1},{4,6},{5,7},{6,4},{7,5},{8,10},{9,11},{10,... | collective-permute-start | bytes 3145736 | tf_op jit(solution)/shard_map/ppermute | solution.py:315
  215.8 20.7 %corr.3 = (bf16[512,1024]{1,0:T(8,128)(2,1)}, bf16[512,1024]{1,0:T(8,128)(2,1)}, bf16[512,1024]{1,0:T(8,128)(2,1)}, bf16[512,1024]{1,0:T(8,128)(2,1)}) custom-call(s32[8]{0:T(128)} %stack.200.place, s32[4]{0:T(128)} %pad_add_fusion.4.order, bf16[64,48,128]{2,1,0:T(8,128)(2,1)} %copy-done.7, bf16[64,48,128]{2,1,0:T(8,128)(2,1)} %copy-done.19, ...), custom_call_target="tpu_custom_call" | custom-call | flops 22000001024 | bytes 40000000 | tf_op jit(solution)/shard_map/corr/pallas_call | solution.py:154
  236.4 2.5 collective-permute-done.38.c
  239.9 2.5 collective-permute-done.39
  247.4 2.9 %finish.2.refs_0_ = bf16[2,1024,512]{2,1,0:T(8,128)(2,1)} custom-call(bf16[512,1024]{1,0:T(8,128)(2,1)} %get-tuple-element.302.a, bf16[512,1024]{1,0:T(8,128)(2,1)} %copy-done, bf16[512,1024]{1,0:T(8,128)(2,1)} %copy-done.1), custom_call_target="tpu_custom_call" | custom-call | tf_op jit(solution)/shard_map/finish/pallas_call | solution.py:189
  250.3 20.0 %collective-permute-done.41.c = bf16[512,1024]{1,0:T(8,128)(2,1)S(1)} collective-permute-done((bf16[512,1024]{1,0:T(8,128)(2,1)S(1)}, bf16[512,1024]{1,0:T(8,128)(2,1)S(1)}, u32[]{:S(2)}, u32[]{:S(2)}) %collective-permute-start.41) | collective-permute-done | bytes 1048608 | tf_op jit(solution)/shard_map/ppermute | solution.py:315
  271.3 2.9 %finish.3 = bf16[2,1024,512]{2,1,0:T(8,128)(2,1)} custom-call(bf16[512,1024]{1,0:T(8,128)(2,1)} %get-tuple-element.290.a, bf16[512,1024]{1,0:T(8,128)(2,1)} %copy-done.2, bf16[512,1024]{1,0:T(8,128)(2,1)} %copy-done.3, bf16[2,1024,512]{2,1,0:T(8,128)(2,1)} %finish.2.refs_0_), custom_call_target="tpu_custom_call", output_to_operand_aliasing={{}: (3, {})} | custom-call | tf_op jit(solution)/shard_map/finish/pallas_call | solution.py:189
  (144 shorter events, 58.5 us)
Async XLA Ops:
  0.6 15.3 %collective-permute-start = (s32[64]{0:T(128)}, s32[64]{0:T(128)S(1)}, u32[]{:S(2)}, u32[]{:S(2)}) collective-permute-start(s32[64]{0:T(128)} %bitcast.202), channel_id=1, source_target_pairs={{0,4},{4,8},{8,12},{12,0},{16,20},{20,24},{24,28},{28,16},{32,36},... | collective-permute-start | bytes 776 | tf_op jit(solution)/shard_map/ppermute | solution.py:211
  15.9 19.9 %collective-permute-start.1 = (bf16[64,48,128]{2,1,0:T(8,128)(2,1)}, bf16[64,48,128]{2,1,0:T(8,128)(2,1)S(1)}, u32[]{:S(2)}, u32[]{:S(2)}) collective-permute-start(bf16[64,48,128]{2,1,0:T(8,128)(2,1)} %get-tuple-element.174), channel_id=1, source_target_pairs={{0,4},{4,8},{8,12},{12,0},{16,20},{20,24},{24,28},{28,16},{32,36},... | collective-permute-start | bytes 2359304 | tf_op jit(solution)/shard_map/ppermute | solution.py:211
  17.2 35.0 %collective-permute-start.2 = (bf16[64,48,128]{2,1,0:T(8,128)(2,1)}, bf16[64,48,128]{2,1,0:T(8,128)(2,1)S(1)}, u32[]{:S(2)}, u32[]{:S(2)}) collective-permute-start(bf16[64,48,128]{2,1,0:T(8,128)(2,1)} %get-tuple-element.175), channel_id=1, source_target_pairs={{0,8},{4,12},{8,0},{12,4},{16,24},{20,28},{24,16},{28,20},{32,40},... | collective-permute-start | bytes 2359304 | tf_op jit(solution)/shard_map/ppermute | solution.py:211
  18.5 34.9 %collective-permute-start.3 = (bf16[64,48,128]{2,1,0:T(8,128)(2,1)}, bf16[64,48,128]{2,1,0:T(8,128)(2,1)S(1)}, u32[]{:S(2)}, u32[]{:S(2)}) collective-permute-start(bf16[64,48,128]{2,1,0:T(8,128)(2,1)} %get-tuple-element.176), channel_id=1, source_target_pairs={{0,12},{4,0},{8,4},{12,8},{16,28},{20,16},{24,20},{28,24},{32,44},... | collective-permute-start | bytes 2359304 | tf_op jit(solution)/shard_map/ppermute | solution.py:211
  20.5 32.9 %collective-permute-start.4 = (bf16[64,48,128]{2,1,0:T(8,128)(2,1)}, bf16[64,48,128]{2,1,0:T(8,128)(2,1)S(1)}, u32[]{:S(2)}, u32[]{:S(2)}) collective-permute-start(bf16[64,48,128]{2,1,0:T(8,128)(2,1)} %get-tuple-element.177), channel_id=1, source_target_pairs={{0,32},{4,36},{8,40},{12,44},{16,48},{20,52},{24,56},{28,60},{32,6... | collective-permute-start | bytes 2359304 | tf_op jit(solution)/shard_map/ppermute | solution.py:215
  22.2 36.2 %collective-permute-start.5 = (bf16[64,48,128]{2,1,0:T(8,128)(2,1)}, bf16[64,48,128]{2,1,0:T(8,128)(2,1)}, u32[]{:S(2)}, u32[]{:S(2)}) collective-permute-start(bf16[64,48,128]{2,1,0:T(8,128)(2,1)} %get-tuple-element.178), channel_id=1, source_target_pairs={{0,64},{4,68},{8,72},{12,76},{16,80},{20,84},{24,88},{28,92},{32,9... | collective-permute-start | bytes 2359304 | tf_op jit(solution)/shard_map/ppermute | solution.py:215
  35.8 22.6 %collective-permute-start.6 = (bf16[64,48,128]{2,1,0:T(8,128)(2,1)}, bf16[64,48,128]{2,1,0:T(8,128)(2,1)}, u32[]{:S(2)}, u32[]{:S(2)}) collective-permute-start(bf16[64,48,128]{2,1,0:T(8,128)(2,1)} %get-tuple-element.179), channel_id=1, source_target_pairs={{0,96},{4,100},{8,104},{12,108},{16,112},{20,116},{24,120},{28,124... | collective-permute-start | bytes 2359304 | tf_op jit(solution)/shard_map/ppermute | solution.py:215
  62.9 16.4 %collective-permute-start.11 = (bf16[2,16,48,128]{3,2,1,0:T(8,128)(2,1)}, bf16[2,16,48,128]{3,2,1,0:T(8,128)(2,1)S(1)}, u32[]{:S(2)}, u32[]{:S(2)}) collective-permute-start(bf16[2,16,48,128]{3,2,1,0:T(8,128)(2,1)} %get-tuple-element.196), channel_id=1, source_target_pairs={{0,8},{4,12},{8,0},{12,4},{16,24},{20,28},{24,16},{28,20},{32,40},... | collective-permute-start | bytes 1179656 | tf_op jit(solution)/shard_map/ppermute | solution.py:211
  64.1 15.2 %collective-permute-start.12 = (bf16[2,16,48,128]{3,2,1,0:T(8,128)(2,1)}, bf16[2,16,48,128]{3,2,1,0:T(8,128)(2,1)S(1)}, u32[]{:S(2)}, u32[]{:S(2)}) collective-permute-start(bf16[2,16,48,128]{3,2,1,0:T(8,128)(2,1)} %get-tuple-element.197), channel_id=1, source_target_pairs={{0,12},{4,0},{8,4},{12,8},{16,28},{20,16},{24,20},{28,24},{32,44},... | collective-permute-start | bytes 1179656 | tf_op jit(solution)/shard_map/ppermute | solution.py:211
  65.6 13.7 %collective-permute-start.7 = (bf16[2,16,48,128]{3,2,1,0:T(8,128)(2,1)}, bf16[2,16,48,128]{3,2,1,0:T(8,128)(2,1)S(1)}, u32[]{:S(2)}, u32[]{:S(2)}) collective-permute-start(bf16[2,16,48,128]{3,2,1,0:T(8,128)(2,1)} %get-tuple-element.192), channel_id=1, source_target_pairs={{0,32},{4,36},{8,40},{12,44},{16,48},{20,52},{24,56},{28,60},{32,6... | collective-permute-start | bytes 1179656 | tf_op jit(solution)/shard_map/ppermute | solution.py:215
  81.7 16.2 %collective-permute-start.13 = (bf16[2,2,16,48,128]{4,3,2,1,0:T(8,128)(2,1)S(1)}, bf16[2,2,16,48,128]{4,3,2,1,0:T(8,128)(2,1)S(1)}, u32[]{:S(2)}, u32[]{:S(2)}) collective-permute-start(bf16[2,2,16,48,128]{4,3,2,1,0:T(8,128)(2,1)S(1)} %pad_maximum_fusion), channel_id=1, source_target_pairs={{0,16},{4,20},{8,24},{12,28},{16,0},{20,4},{24,8},{28,12},{32,48},... | collective-permute-start | bytes 2359304 | tf_op jit(solution)/shard_map/ppermute | solution.py:219
  98.9 15.9 %collective-permute-start.16 = (bf16[2,16,48,128]{3,2,1,0:T(8,128)(2,1)}, bf16[2,16,48,128]{3,2,1,0:T(8,128)(2,1)S(1)}, u32[]{:S(2)}, u32[]{:S(2)}) collective-permute-start(bf16[2,16,48,128]{3,2,1,0:T(8,128)(2,1)} %pad_maximum_fusion.5), channel_id=1, source_target_pairs={{0,32},{4,36},{8,40},{12,44},{16,48},{20,52},{24,56},{28,60},{32,6... | collective-permute-start | bytes 1179656 | tf_op jit(solution)/shard_map/ppermute | solution.py:215
  101.6 15.3 %collective-permute-start.17 = (bf16[2,16,48,128]{3,2,1,0:T(8,128)(2,1)}, bf16[2,16,48,128]{3,2,1,0:T(8,128)(2,1)S(1)}, u32[]{:S(2)}, u32[]{:S(2)}) collective-permute-start(bf16[2,16,48,128]{3,2,1,0:T(8,128)(2,1)} %pad_maximum_fusion.5), channel_id=1, source_target_pairs={{0,64},{4,68},{8,72},{12,76},{16,80},{20,84},{24,88},{28,92},{32,9... | collective-permute-start | bytes 1179656 | tf_op jit(solution)/shard_map/ppermute | solution.py:215
  101.9 15.1 %collective-permute-start.18 = (bf16[2,16,48,128]{3,2,1,0:T(8,128)(2,1)}, bf16[2,16,48,128]{3,2,1,0:T(8,128)(2,1)S(1)}, u32[]{:S(2)}, u32[]{:S(2)}) collective-permute-start(bf16[2,16,48,128]{3,2,1,0:T(8,128)(2,1)} %pad_maximum_fusion.5), channel_id=1, source_target_pairs={{0,96},{4,100},{8,104},{12,108},{16,112},{20,116},{24,120},{28,124... | collective-permute-start | bytes 1179656 | tf_op jit(solution)/shard_map/ppermute | solution.py:215
  104.0 13.0 %collective-permute-start.19 = (bf16[2,16,48,128]{3,2,1,0:T(8,128)(2,1)S(1)}, bf16[2,16,48,128]{3,2,1,0:T(8,128)(2,1)S(1)}, u32[]{:S(2)}, u32[]{:S(2)}) collective-permute-start(bf16[2,16,48,128]{3,2,1,0:T(8,128)(2,1)S(1)} %pad_maximum_fusion.6), channel_id=1, source_target_pairs={{0,4},{4,8},{8,12},{12,0},{16,20},{20,24},{24,28},{28,16},{32,36},... | collective-permute-start | bytes 1179656 | tf_op jit(solution)/shard_map/ppermute | solution.py:211
  111.2 17.0 %collective-permute-start.20 = (bf16[2,16,48,128]{3,2,1,0:T(8,128)(2,1)S(1)}, bf16[2,16,48,128]{3,2,1,0:T(8,128)(2,1)S(1)}, u32[]{:S(2)}, u32[]{:S(2)}) collective-permute-start(bf16[2,16,48,128]{3,2,1,0:T(8,128)(2,1)S(1)} %pad_maximum_fusion.6), channel_id=1, source_target_pairs={{0,8},{4,12},{8,0},{12,4},{16,24},{20,28},{24,16},{28,20},{32,40},... | collective-permute-start | bytes 1179656 | tf_op jit(solution)/shard_map/ppermute | solution.py:211
  114.8 14.3 %collective-permute-start.21 = (bf16[2,16,48,128]{3,2,1,0:T(8,128)(2,1)S(1)}, bf16[2,16,48,128]{3,2,1,0:T(8,128)(2,1)S(1)}, u32[]{:S(2)}, u32[]{:S(2)}) collective-permute-start(bf16[2,16,48,128]{3,2,1,0:T(8,128)(2,1)S(1)} %pad_maximum_fusion.6), channel_id=1, source_target_pairs={{0,12},{4,0},{8,4},{12,8},{16,28},{20,16},{24,20},{28,24},{32,44},... | collective-permute-start | bytes 1179656 | tf_op jit(solution)/shard_map/ppermute | solution.py:211
  129.7 19.1 %collective-permute-start.22 = (bf16[64,48,128]{2,1,0:T(8,128)(2,1)S(1)}, bf16[64,48,128]{2,1,0:T(8,128)(2,1)}, u32[]{:S(2)}, u32[]{:S(2)}) collective-permute-start(bf16[64,48,128]{2,1,0:T(8,128)(2,1)S(1)} %pad_maximum_fusion.3.refs_0_), channel_id=1, source_target_pairs={{0,4},{4,8},{8,12},{12,0},{16,20},{20,24},{24,28},{28,16},{32,36},... | collective-permute-start | bytes 2359304 | tf_op jit(solution)/shard_map/ppermute | solution.py:211
  133.4 16.7 %collective-permute-start.23 = (bf16[64,48,128]{2,1,0:T(8,128)(2,1)S(1)}, bf16[64,48,128]{2,1,0:T(8,128)(2,1)}, u32[]{:S(2)}, u32[]{:S(2)}) collective-permute-start(bf16[64,48,128]{2,1,0:T(8,128)(2,1)S(1)} %pad_maximum_fusion.4.refs_4_), channel_id=1, source_target_pairs={{0,32},{4,36},{8,40},{12,44},{16,48},{20,52},{24,56},{28,60},{32,6... | collective-permute-start | bytes 2359304 | tf_op jit(solution)/shard_map/ppermute | solution.py:215
  135.2 15.6 %collective-permute-start.24 = (bf16[64,48,128]{2,1,0:T(8,128)(2,1)S(1)}, bf16[64,48,128]{2,1,0:T(8,128)(2,1)S(1)}, u32[]{:S(2)}, u32[]{:S(2)}) collective-permute-start(bf16[64,48,128]{2,1,0:T(8,128)(2,1)S(1)} %pad_maximum_fusion.3.refs_0_), channel_id=1, source_target_pairs={{0,12},{4,0},{8,4},{12,8},{16,28},{20,16},{24,20},{28,24},{32,44},... | collective-permute-start | bytes 2359304 | tf_op jit(solution)/shard_map/ppermute | solution.py:211
  135.2 15.6 %collective-permute-start.25 = (bf16[64,48,128]{2,1,0:T(8,128)(2,1)S(1)}, bf16[64,48,128]{2,1,0:T(8,128)(2,1)S(1)}, u32[]{:S(2)}, u32[]{:S(2)}) collective-permute-start(bf16[64,48,128]{2,1,0:T(8,128)(2,1)S(1)} %pad_maximum_fusion.4.refs_4_), channel_id=1, source_target_pairs={{0,96},{4,100},{8,104},{12,108},{16,112},{20,116},{24,120},{28,124... | collective-permute-start | bytes 2359304 | tf_op jit(solution)/shard_map/ppermute | solution.py:215
  136.2 12.7 %collective-permute-start.26 = (s32[2,2,2,64]{3,2,1,0:T(2,128)S(1)}, s32[2,2,2,64]{3,2,1,0:T(2,128)S(1)}, u32[]{:S(2)}, u32[]{:S(2)}) collective-permute-start(s32[2,2,2,64]{3,2,1,0:T(2,128)S(1)} %pad_add_fusion.1), channel_id=1, source_target_pairs={{0,64},{4,68},{8,72},{12,76},{16,80},{20,84},{24,88},{28,92},{32,9... | collective-permute-start | bytes 6152 | tf_op jit(solution)/shard_map/ppermute | solution.py:215
  150.8 16.2 %collective-permute-start.27 = (bf16[64,48,128]{2,1,0:T(8,128)(2,1)}, bf16[64,48,128]{2,1,0:T(8,128)(2,1)}, u32[]{:S(2)}, u32[]{:S(2)}) collective-permute-start(bf16[64,48,128]{2,1,0:T(8,128)(2,1)} %collective-permute-done.22.refs_1_), channel_id=1, source_target_pairs={{0,4},{4,8},{8,12},{12,0},{16,20},{20,24},{24,28},{28,16},{32,36},... | collective-permute-start | bytes 2359304 | tf_op jit(solution)/shard_map/ppermute | solution.py:211
  152.1 15.6 %collective-permute-start.28 = (bf16[64,48,128]{2,1,0:T(8,128)(2,1)}, bf16[64,48,128]{2,1,0:T(8,128)(2,1)}, u32[]{:S(2)}, u32[]{:S(2)}) collective-permute-start(bf16[64,48,128]{2,1,0:T(8,128)(2,1)} %collective-permute-done.23.refs_5_), channel_id=1, source_target_pairs={{0,32},{4,36},{8,40},{12,44},{16,48},{20,52},{24,56},{28,60},{32,6... | collective-permute-start | bytes 2359304 | tf_op jit(solution)/shard_map/ppermute | solution.py:215
  152.4 15.2 %collective-permute-start.29 = (bf16[64,48,128]{2,1,0:T(8,128)(2,1)S(1)}, bf16[64,48,128]{2,1,0:T(8,128)(2,1)S(1)}, u32[]{:S(2)}, u32[]{:S(2)}) collective-permute-start(bf16[64,48,128]{2,1,0:T(8,128)(2,1)S(1)} %pad_maximum_fusion.1.refs_0_), channel_id=1, source_target_pairs={{0,12},{4,0},{8,4},{12,8},{16,28},{20,16},{24,20},{28,24},{32,44},... | collective-permute-start | bytes 2359304 | tf_op jit(solution)/shard_map/ppermute | solution.py:211
  153.8 13.9 %collective-permute-start.30 = (bf16[64,48,128]{2,1,0:T(8,128)(2,1)S(1)}, bf16[64,48,128]{2,1,0:T(8,128)(2,1)S(1)}, u32[]{:S(2)}, u32[]{:S(2)}) collective-permute-start(bf16[64,48,128]{2,1,0:T(8,128)(2,1)S(1)} %pad_maximum_fusion.2.refs_4_), channel_id=1, source_target_pairs={{0,96},{4,100},{8,104},{12,108},{16,112},{20,116},{24,120},{28,124... | collective-permute-start | bytes 2359304 | tf_op jit(solution)/shard_map/ppermute | solution.py:215
  169.0 26.9 %collective-permute-start.32 = (bf16[64,48,128]{2,1,0:T(8,128)(2,1)S(1)}, bf16[64,48,128]{2,1,0:T(8,128)(2,1)S(1)}, u32[]{:S(2)}, u32[]{:S(2)}) collective-permute-start(bf16[64,48,128]{2,1,0:T(8,128)(2,1)S(1)} %pad_maximum_fusion.1.refs_0_), channel_id=1, source_target_pairs={{0,4},{4,8},{8,12},{12,0},{16,20},{20,24},{24,28},{28,16},{32,36},... | collective-permute-start | bytes 2359304 | tf_op jit(solution)/shard_map/ppermute | solution.py:211
  169.0 26.9 %collective-permute-start.33 = (bf16[64,48,128]{2,1,0:T(8,128)(2,1)S(1)}, bf16[64,48,128]{2,1,0:T(8,128)(2,1)S(1)}, u32[]{:S(2)}, u32[]{:S(2)}) collective-permute-start(bf16[64,48,128]{2,1,0:T(8,128)(2,1)S(1)} %pad_maximum_fusion.2.refs_4_), channel_id=1, source_target_pairs={{0,32},{4,36},{8,40},{12,44},{16,48},{20,52},{24,56},{28,60},{32,6... | collective-permute-start | bytes 2359304 | tf_op jit(solution)/shard_map/ppermute | solution.py:215
  170.3 25.7 %collective-permute-start.34 = (bf16[64,48,128]{2,1,0:T(8,128)(2,1)S(1)}, bf16[64,48,128]{2,1,0:T(8,128)(2,1)S(1)}, u32[]{:S(2)}, u32[]{:S(2)}) collective-permute-start(bf16[64,48,128]{2,1,0:T(8,128)(2,1)S(1)} %collective-permute-done.29.refs_2_), channel_id=1, source_target_pairs={{0,12},{4,0},{8,4},{12,8},{16,28},{20,16},{24,20},{28,24},{32,44},... | collective-permute-start | bytes 2359304 | tf_op jit(solution)/shard_map/ppermute | solution.py:211
  172.9 23.1 %collective-permute-start.35 = (bf16[64,48,128]{2,1,0:T(8,128)(2,1)S(1)}, bf16[64,48,128]{2,1,0:T(8,128)(2,1)S(1)}, u32[]{:S(2)}, u32[]{:S(2)}) collective-permute-start(bf16[64,48,128]{2,1,0:T(8,128)(2,1)S(1)} %collective-permute-done.30.refs_6_), channel_id=1, source_target_pairs={{0,96},{4,100},{8,104},{12,108},{16,112},{20,116},{24,120},{28,124... | collective-permute-start | bytes 2359304 | tf_op jit(solution)/shard_map/ppermute | solution.py:215
  210.1 28.9 %collective-permute-start.38 = (bf16[512,1024]{1,0:T(8,128)(2,1)S(1)}, bf16[512,1024]{1,0:T(8,128)(2,1)S(1)}, u32[]{:S(2)}, u32[]{:S(2)}) collective-permute-start(bf16[512,1024]{1,0:T(8,128)(2,1)S(1)} %add_convert_fusion.1), channel_id=1, source_target_pairs={{0,2},{1,3},{2,0},{3,1},{4,6},{5,7},{6,4},{7,5},{8,10},{9,11},{10,... | collective-permute-start | bytes 3145736 | tf_op jit(solution)/shard_map/ppermute | solution.py:315
  245.9 24.5 %collective-permute-start.41 = (bf16[512,1024]{1,0:T(8,128)(2,1)S(1)}, bf16[512,1024]{1,0:T(8,128)(2,1)S(1)}, u32[]{:S(2)}, u32[]{:S(2)}) collective-permute-start(bf16[512,1024]{1,0:T(8,128)(2,1)S(1)} %add_convert_fusion), channel_id=1, source_target_pairs={{0,2},{1,3},{2,0},{3,1},{4,6},{5,7},{6,4},{7,5},{8,10},{9,11},{10,... | collective-permute-start | bytes 3145736 | tf_op jit(solution)/shard_map/ppermute | solution.py:315
  (33 other events, 413.0 us)

commit v4 on v3

--- a/solution.py
+++ b/solution.py
@@ -20,20 +20,23 @@
 def whiten_kernel(place, spec, counts, *refs):
     own, pieces, work = refs[0], refs[1:-1], refs[-1]
     base = pl.program_id(0) * SB
-    live = counts[...]
+    live = jnp.concatenate([counts[...]] * 2, axis=1)
     for s in range(SB):
         v = spec[s].astype(F32)
         power = jnp.mean(v * v, axis=-1, keepdims=True)
+        n = v * lax.rsqrt(power + EPS)
         mask = (base + s < live).astype(F32)
-        n = v * lax.rsqrt(power + EPS) * mask
-        work[s] = jnp.concatenate([n[:, :BINS], n[:, BINS:]], axis=0).T
+        work[s] = jnp.concatenate([n[:, :BINS], n[:, BINS:]], axis=0).T * mask
     own[...] = jnp.swapaxes(work[...], 0, 1).astype(BF)
     for m, piece in enumerate(pieces):
-        piece[...] = own[pl.ds(pl.multiple_of(place[m] * KC, KC), KC)]
+        piece[:KC] = own[pl.ds(pl.multiple_of(place[m] * KC, KC), KC)]
+        if m % 2 == 0:
+            piece[KC] = jnp.broadcast_to(live.astype(F32), (SB, 128)).astype(BF)
 
 
 def whiten(place, spectra, counts):
     n = place.shape[0]
+    sizes = [KC + 1 - m % 2 for m in range(n)]
     return pl.pallas_call(
         whiten_kernel,
         grid_spec=pltpu.PrefetchScalarGridSpec(
@@ -41,18 +44,18 @@
             grid=(SUB // SB,),
             in_specs=[
                 pl.BlockSpec((SB, BLOCK, 2 * BINS), lambda i, p: (i, 0, 0)),
-                pl.BlockSpec((BLOCK, 1), lambda i, p: (0, 0)),
+                pl.BlockSpec((1, BLOCK), lambda i, p: (0, 0)),
             ],
             out_specs=[pl.BlockSpec((BINS, SB, 128), lambda i, p: (0, i, 0))]
-            + [pl.BlockSpec((KC, SB, 128), lambda i, p: (0, i, 0))] * n,
+            + [pl.BlockSpec((size, SB, 128), lambda i, p: (0, i, 0)) for size in sizes],
             scratch_shapes=[pltpu.VMEM((SB, BINS, 128), F32)],
         ),
         out_shape=[jax.ShapeDtypeStruct((BINS, SUB, 128), BF)]
-        + [jax.ShapeDtypeStruct((KC, SUB, 128), BF)] * n,
+        + [jax.ShapeDtypeStruct((size, SUB, 128), BF) for size in sizes],
         compiler_params=VMEM,
         cost_estimate=pl.CostEstimate(flops=10**8, bytes_accessed=18 * 10**6, transcendentals=0),
         name="whiten",
-    )(place, spectra, counts[:, None])
+    )(place, spectra, counts)
 
 
 def choose(scalars, inputs, shapes, tasks):
@@ -109,9 +112,10 @@
 
 def corr_kernel(place, order, *refs):
     pieces = refs[:CHUNKS]
-    own, rot, inv, table = refs[CHUNKS : CHUNKS + 4]
-    outs = refs[CHUNKS + 4 : CHUNKS + 8]
-    src, work, rows, sems = refs[CHUNKS + 8 :]
+    own, rot = refs[CHUNKS : CHUNKS + 2], refs[CHUNKS + 2 : CHUNKS + 4]
+    inv, table = refs[CHUNKS + 4 : CHUNKS + 6]
+    outs = refs[CHUNKS + 6 : CHUNKS + 10]
+    src, work, rows, sems = refs[CHUNKS + 10 :]
     step = pl.program_id(0)
     copies = [pltpu.make_async_copy(piece, src.at[m], sems.at[m]) for m, piece in enumerate(pieces)]
 
@@ -121,25 +125,37 @@
             copy.start()
 
     for m, copy in enumerate(copies):
-        @pl.when(step == m)
+        @pl.when(step == m // 2)
         def _(copy=copy):
             copy.wait()
 
-    for k in range(KC):
-        x = src[step, k].T
-        h = jnp.dot(x[:BLOCK], own[k], preferred_element_type=F32)
-        h += jnp.dot(x[BLOCK:], rot[k], preferred_element_type=F32)
-        work[k] = h
+    zero = jnp.zeros((SUB, 128), BF)
+
+    def diagonal(a, b):
+        return jnp.concatenate(
+            [jnp.concatenate([a, zero], axis=1), jnp.concatenate([zero, b], axis=1)], axis=0
+        )
+
+    for e in range(2):
+        for k in range(0, KC, 2):
+            x = src[2 * step + e, k : k + 2].reshape(2 * SUB, 128).T
+            h = jnp.dot(x[:BLOCK], diagonal(own[e][k], own[e][k + 1]), preferred_element_type=F32)
+            h += jnp.dot(x[BLOCK:], diagonal(rot[e][k], rot[e][k + 1]), preferred_element_type=F32)
+            work[e * KC + k] = h[:, :128]
+            work[e * KC + k + 1] = h[:, 128:]
     z = jnp.swapaxes(work[...], 0, 1)
-    off = pl.multiple_of(place[step] * KC, KC)
-    low = lax.broadcasted_iota(jnp.int32, (KC, 128), 1) < BLOCK
+    low = lax.broadcasted_iota(jnp.int32, (2 * KC, 128), 1) < BLOCK
+    offs = [pl.multiple_of(place[2 * step + e] * KC, KC) for e in range(2)]
     for p in range(BLOCK // 2):
         u, v = z[2 * p], z[2 * p + 1]
         lanes = slice(p % 2 * 128, p % 2 * 128 + 128)
-        rows[p // 2, pl.ds(off, KC), lanes] = jnp.where(low, u, pltpu.roll(v, 64, 1)).astype(BF)
-        rows[p // 2, pl.ds(off + BINS, KC), lanes] = jnp.where(low, pltpu.roll(u, 64, 1), v).astype(BF)
-
-    @pl.when(step == CHUNKS - 1)
+        re = jnp.where(low, u, pltpu.roll(v, 64, 1)).astype(BF)
+        im = jnp.where(low, pltpu.roll(u, 64, 1), v).astype(BF)
+        for e in range(2):
+            rows[p // 2, pl.ds(offs[e], KC), lanes] = re[e * KC : e * KC + KC]
+            rows[p // 2, pl.ds(offs[e] + BINS, KC), lanes] = im[e * KC : e * KC + KC]
+
+    @pl.when(step == CHUNKS // 2 - 1)
     def _():
         for m in range(4):
             block = order[m]
@@ -150,23 +166,22 @@
 
 
 def corr(place, order, pieces, own, rot, inv, table):
-    here = pl.BlockSpec((KC, SUB, 128), lambda i, p, o: (p[i], 0, 0))
+    here = [pl.BlockSpec((KC, SUB, 128), lambda i, p, o, e=e: (p[2 * i + e], 0, 0)) for e in range(2)]
     return pl.pallas_call(
         corr_kernel,
         grid_spec=pltpu.PrefetchScalarGridSpec(
             num_scalar_prefetch=2,
-            grid=(CHUNKS,),
+            grid=(CHUNKS // 2,),
             in_specs=[pl.BlockSpec(memory_space=pl.ANY)] * CHUNKS
+            + here * 2
             + [
-                here,
-                here,
                 pl.BlockSpec((4, 1, 1024), lambda i, p, o: (0, 0, 0)),
                 pl.BlockSpec((LAGS, 2 * BINS), lambda i, p, o: (0, 0)),
             ],
             out_specs=[pl.BlockSpec((LAGS, 1024), lambda i, p, o: (0, 0))] * 4,
             scratch_shapes=[
                 pltpu.VMEM((CHUNKS, KC, SUB, 128), BF),
-                pltpu.VMEM((KC, BLOCK, 128), F32),
+                pltpu.VMEM((2 * KC, BLOCK, 128), F32),
                 pltpu.VMEM((BLOCK // 4, 2 * BINS, 256), BF),
                 pltpu.SemaphoreType.DMA((CHUNKS,)),
             ],
@@ -175,7 +190,7 @@
         compiler_params=VMEM,
         cost_estimate=pl.CostEstimate(flops=22 * 10**9, bytes_accessed=40 * 10**6, transcendentals=0),
         name="corr",
-    )(place, order, *pieces, own, rot, inv, table)
+    )(place, order, *pieces, own, own, rot, rot, inv, table)
 
 
 def finish_kernel(a, b, c, *refs):
@@ -242,13 +257,19 @@
     return barrier(*got, *done)
 
 
-HOPS = (1, 2, 3)
-TO_X = [lambda a, d=d: along_x(a, d) for d in HOPS]
-TO_Z = [lambda a, d=d: along_z(a, d) for d in HOPS]
-
-
-def broadcast(own, ready, marks, roots, z, h, x):
-    got = spread(ready, TO_X + TO_Z)
+HOPS = (2, 1, 3)
+TO_X = {d: lambda a, d=d: along_x(a, d) for d in HOPS}
+TO_Z = {d: lambda a, d=d: along_z(a, d) for d in HOPS}
+X_THEN_Z = [to[d] for d in HOPS for to in (TO_X, TO_Z)]
+Z_THEN_X = [to[d] for d in HOPS for to in (TO_Z, TO_X)]
+
+
+def by_hop(got):
+    return [[got[2 * HOPS.index(d) + n] for d in (1, 2, 3)] for n in range(2)]
+
+
+def broadcast(own, ready, counts, roots, z, h, x):
+    from_x, from_z = by_hop(spread(ready, X_THEN_Z))
 
     def own_a(q):
         return lambda ins, s: ins[0].at[pl.ds(s[4] * 64 + s[q] * 16, 16)]
@@ -258,6 +279,9 @@
 
     def came(n, q):
         return lambda ins, s: ins[n].at[pl.ds(s[q] * 16, 16)]
+
+    def row(n):
+        return lambda ins, s: ins[n].at[64:65]
 
     scalars = jnp.stack(
         [(x - r[2]) & 3 for r in roots]
@@ -269,42 +293,51 @@
     tasks = []
     for d in range(4):
         for i in range(STEPS):
-            tasks.append(
-                (lambda outs, d=d, i=i: outs[d].at[i], i, [own_a(6 + d)] + [came(n, 6 + d) for n in (1, 2, 3)])
-            )
-            tasks.append(
-                (lambda outs, d=d, i=i: outs[4 + d].at[i], 2 + i, [own_b(10 + d)] + [came(n, 10 + d) for n in (4, 5, 6)])
-            )
-    cuts = choose(scalars, [own, *got], [(STEPS, 16, SUB, 128)] * 8, tasks)
-    got = spread(cuts[1:4] + cuts[5:], TO_Z + TO_X)
+            tasks += [
+                (lambda outs, d=d, i=i: outs[d].at[i, :16], i, [own_a(6 + d)] + [came(n, 6 + d) for n in (2, 3, 4)]),
+                (lambda outs, d=d, i=i: outs[d].at[i, 16:], i, [row(n) for n in (1, 2, 3, 4)]),
+                (lambda outs, d=d, i=i: outs[4 + d].at[i], 2 + i, [own_b(10 + d)] + [came(n, 10 + d) for n in (5, 6, 7)]),
+            ]
+    shapes = [(STEPS, 17, SUB, 128)] * 4 + [(STEPS, 16, SUB, 128)] * 4
+    cuts = choose(scalars, [own, ready[0], *from_x, *from_z], shapes, tasks)
+    got = spread(
+        cuts[1:4] + cuts[5:], [TO_Z[d] for d in (1, 2, 3)] + [TO_X[d] for d in (1, 2, 3)]
+    )
     got_a = [cuts[0], *got[:3]]
     got_b = [cuts[4], *got[3:]]
     mine = jnp.stack(
         [
-            jnp.stack([pick((z - r[0]) & 3, [g[i] for g in got_a]) for i, r in enumerate(roots)]),
-            jnp.stack([pick((x - r[2]) & 3, [g[i] for g in got_b]) for i, r in enumerate(roots)]),
+            jnp.concatenate(
+                [pick((z - r[0]) & 3, [g[i] for g in got_a]), pick((x - r[2]) & 3, [g[i] for g in got_b])]
+            )
+            for i, r in enumerate(roots)
         ]
     )
-
-    def hops(marks):
-        for shift in (TO_X[1], TO_Z[0]):
-            marks = jnp.stack([marks, shift(marks)])
-        return [marks]
-
-    other, marks = spread([mine], [swap_y], hops, [marks])
+    (other,) = spread([mine], [swap_y])
+    here = [h == r[1] for r in roots]
     sub = [
-        jnp.stack([jnp.where(h == r[1], mine[n, i], other[n, i]) for i, r in enumerate(roots)])
-        for n in range(2)
+        jnp.stack([jnp.where(here[i], mine[i, rows], other[i, rows]) for i in range(STEPS)])
+        for rows in (slice(0, 16), slice(17, 33))
     ]
-    got = spread([sub[0]] * 3 + [sub[1]] * 3, TO_Z + TO_X)
-    all_a = [sub[0], *got[:3]]
-    all_b = [sub[1], *got[3:6]]
+
+    def scales(mine, other):
+        out = []
+        for i in range(STEPS):
+            src_counts = jnp.where(here[i], mine[i, 16, 0, :BLOCK], other[i, 16, 0, :BLOCK]).astype(F32)
+            inv = 1.0 / jnp.minimum(src_counts[:, None], counts[None, :].astype(F32))
+            out.append(inv.reshape(4, 1, 1024))
+        return out
+
+    got = spread(sub * 3, Z_THEN_X, scales, [mine, other])
+    from_z, from_x = by_hop(got[:6])
+    all_a = [sub[0], *from_z]
+    all_b = [sub[1], *from_x]
     out = []
     for i in range(STEPS):
         a = jnp.concatenate([pick((z - q) & 3, [v[i] for v in all_a]) for q in range(4)])
         b = jnp.concatenate([pick((x - q) & 3, [v[i] for v in all_b]) for q in range(4)])
         out.append((a, b))
-    return out, marks
+    return out, got[6:]
 
 
 def other_core(a):
@@ -320,62 +353,45 @@
 
 
 def body(spectra, counts, block_ids):
-    counts = counts[0]
-    table = lag_table()
     station, tm = lax.axis_index("station"), lax.axis_index("tm")
     z, h, x = station >> 3, station >> 2 & 1, station & 3
 
     def places(*list_of):
         return jnp.stack(list_of).astype(jnp.int32)
 
-    ahead = places(*[(x + d) & 3 for d in HOPS], *[4 + ((z + d) & 3) for d in HOPS])
-    next_counts, own, *ready = spread(
-        [counts], [TO_X[0]], lambda *a: whiten(*a), [ahead, spectra[0], counts]
-    )
-    marks = jnp.stack([counts, next_counts])
+    ahead = places(*[v for d in HOPS for v in ((x + d) & 3, 4 + ((z + d) & 3))])
+    own, *ready = whiten(ahead, spectra[0], counts)
     roots = [(block_ids[i] >> 3, block_ids[i] >> 2 & 1, block_ids[i] & 3) for i in range(STEPS)]
-    ((a0, b0), (a1, b1)), marks = broadcast(own, ready, marks, roots, z, h, x)
+    ((a0, b0), (a1, b1)), (inv0, inv1) = broadcast(own, ready, counts[0], roots, z, h, x)
 
     place = places(
         *[(x + d) & 3 for d in (0, 3, 1, 2)], *[4 + ((z + d) & 3) for d in (0, 3, 1, 2)]
     )
+    table = lag_table()
     order = places((tm ^ 2) ^ 1, tm ^ 2, tm ^ 1, tm)
 
-    def scales(marks):
-        out = []
-        for r in roots:
-            dz, dx = (z - r[0]) & 3, (x - r[2]) & 3
-            src_counts = marks[h ^ r[1], dz >> 1, dz & 1, dx >> 1, dx & 1]
-            inv = 1.0 / jnp.minimum(src_counts[:, None], counts[None, :]).astype(F32)
-            out.append(inv.reshape(4, 1, 1024))
-        return out
-
-    up, down = [TO_X[0], TO_Z[0]], [TO_X[2], TO_Z[2]]
-    a0_up, b0_up, a0_down, b0_down, far_marks, rot = spread(
-        [a0, b0, a0, b0, marks], up + down + [TO_Z[1]], lambda v: [turn(v)], [own]
-    )
-    marks = jnp.stack([marks, far_marks])
-    a0_far, b0_far, a1_down, b1_down, far_marks = spread(
-        [a0_up, b0_up, a1, b1, marks], up + down + [swap_y]
-    )
-    inv0, inv1 = scales(jnp.stack([marks, far_marks]))
+    up, down = [TO_X[1], TO_Z[1]], [TO_X[3], TO_Z[3]]
+    a0_up, b0_up, a0_down, b0_down, rot = spread(
+        [a0, b0, a0, b0], up + down, lambda v: [turn(v)], [own]
+    )
+    a0_far, b0_far, a1_down, b1_down = spread([a0_up, b0_up, a1, b1], up + down)
     a1_up, b1_up, a1_far, b1_far, *lag0 = spread(
         [a1, b1, a1_down, b1_down],
         up + down,
         lambda *v: corr(place, order, v[:8], *v[8:], table),
         [a0, a0_up, a0_down, a0_far, b0, b0_up, b0_down, b0_far, own, rot, inv0],
     )
-    far_got, near_got0 = spread([lag0[0], lag0[2]], [other_core] * 2)
-    far_sum0, *lag1 = spread(
-        [add(lag0[1], far_got)],
-        [other_chip],
+    (far_got,) = spread([lag0[0]], [other_core])
+    far_sum0, near_got0, *lag1 = spread(
+        [add(lag0[1], far_got), lag0[2]],
+        [other_chip, other_core],
         lambda *v: corr(place, order, v[:8], *v[8:], table),
         [a1, a1_up, a1_down, a1_far, b1, b1_up, b1_down, b1_far, own, rot, inv1],
     )
-    far_got, near_got1 = spread([lag1[0], lag1[2]], [other_core] * 2)
-    far_sum1, out = spread(
-        [add(lag1[1], far_got)],
-        [other_chip],
+    (far_got,) = spread([lag1[0]], [other_core])
+    far_sum1, near_got1, out = spread(
+        [add(lag1[1], far_got), lag1[2]],
+        [other_chip, other_core],
         lambda *v: [finish(0, *v)],
         [lag0[3], near_got0, far_sum0],
     )

time: 275 us -> 265 us (0.964)
  starting transfers between devices: 94.9 us -> 67.8 us
  waiting for transfers between devices: 87.2 us -> 98.5 us
  local copies, waits for them, and re-layouts: 6.8 us -> 12.7 us
    ppermute x17 -> x15, waiting for transfers between devices: 46.5 us -> 27.5 us  [along_x(): lax.ppermute(a, 'station', [(s, s - s % 4 + (s + d) % 4) for s in range(3...]
    ppermute x17 -> x15, waiting for transfers between devices: 10.2 us -> 29.1 us  [along_z(): lax.ppermute(a, 'station', [(s, (s + 8 * d) % 32) for s in range(32)])]
    ppermute x2 -> x1, waiting for transfers between devices: 0.03 us -> 14.4 us  [swap_y(): return lax.ppermute(a, 'station', [(s, s ^ 4) for s in range(32)])]
    ppermute x2 -> x1, starting transfers between devices: 13.9 us -> 2.99 us  [swap_y(): return lax.ppermute(a, 'station', [(s, s ^ 4) for s in range(32)])]
    ppermute x17 -> x15, starting transfers between devices: 34.4 us -> 24.7 us  [along_x(): lax.ppermute(a, 'station', [(s, s - s % 4 + (s + d) % 4) for s in range(3...]
    ppermute x17 -> x15, starting transfers between devices: 31.7 us -> 26.9 us  [along_z(): lax.ppermute(a, 'station', [(s, (s + 8 * d) % 32) for s in range(32)])]
    ppermute x2, starting transfers between devices: 7.18 us -> 2.74 us  [other_chip(): return lax.ppermute(a, 'tm', [(t, t ^ 2) for t in range(4)])]
    min x8 -> x6, local copies, waits for them, and re-layouts: 0.57 us -> 5 us  [scales(): inv = 1.0 / jnp.minimum(src_counts[:, None], counts[None, :].astype(F32))]
  transfers between devices with their start and end apart: 42 -> 37, of which waited for: 22 -> 20; matrix products, arithmetic and copies ran while one was open for 2% -> 4% of each run, Pallas kernels for 24% -> 19%
where the time goes in v4:
time: 265 us; the launch traced here: 264 us
  waiting for transfers between devices  98.5 us (37%)
  Pallas kernels  70 us (26%)
  starting transfers between devices  67.8 us (26%)
  local copies, waits for them, and re-layouts  12.7 us (5%)
  other arithmetic  10.8 us (4%)
  between operations  4.33 us (2%)
    pallas_call x2, Pallas kernels, corr(): pl.pallas_call(corr_kernel, grid_spec=pltpu.PrefetchScalarGridSpec(num_sc...  38.8 us
    ppermute x15, waiting for transfers between devices, along_z(): lax.ppermute(a, 'station', [(s, (s + 8 * d) % 32) for s in range(32)])  29.1 us
    ppermute x15, waiting for transfers between devices, along_x(): lax.ppermute(a, 'station', [(s, s - s % 4 + (s + d) % 4) for s in range(3...  27.5 us
    ppermute x15, starting transfers between devices, along_z(): lax.ppermute(a, 'station', [(s, (s + 8 * d) % 32) for s in range(32)])  26.9 us
    ppermute x15, starting transfers between devices, along_x(): lax.ppermute(a, 'station', [(s, s - s % 4 + (s + d) % 4) for s in range(3...  24.7 us
    ppermute x2, waiting for transfers between devices, other_chip(): return lax.ppermute(a, 'tm', [(t, t ^ 2) for t in range(4)])  22.5 us
    ppermute x1, waiting for transfers between devices, swap_y(): return lax.ppermute(a, 'station', [(s, s ^ 4) for s in range(32)])  14.4 us
    pallas_call x1, Pallas kernels, whiten(): pl.pallas_call(whiten_kernel, grid_spec=pltpu.PrefetchScalarGridSpec(num_...  11.8 us
  transfers between devices with their start and end apart: 37, of which 20 were waited for; matrix products, arithmetic and copies ran while one was open for 4% of the time, Pallas kernels for 19%

profile of v4, /device:TPU:1, one launch (start us, length us, event | category | flops | bytes accessed | tf_op | source)
XLA Modules:
  0.0 264.1 jit_solution(5440495812160042468)
XLA Ops:
  0.6 11.8 %whiten.1 = (bf16[512,48,128]{2,1,0:T(8,128)(2,1)}, bf16[65,48,128]{2,1,0:T(8,128)(2,1)}, bf16[64,48,128]{2,1,0:T(8,128)(2,1)}, bf16[65,48,128]{2,1,0:T(8,128)(2...) custom-call(s32[6]{0:T(128)} %stack.125.place, ...), custom_call_target="tpu_custom_call" | custom-call | flops 100000000 | bytes 18000000 | tf_op jit(solution)/shard_map/whiten/pallas_call | solution.py:40
  12.4 4.4 %collective-permute-start.1 = (bf16[64,48,128]{2,1,0:T(8,128)(2,1)}, bf16[64,48,128]{2,1,0:T(8,128)(2,1)S(1)}, u32[]{:S(2)}, u32[]{:S(2)}) collective-permute-start(bf16[64,48,128]{2,1,0:T(8,128)(2,1)} %get-tuple-element.144), channel_id=1, source_target_pairs={{0,64},{4,68},{8,72},{12,76},{16,80},{20,84},{24,88},{28,92},{32,9... | collective-permute-start | bytes 2359304 | tf_op jit(solution)/shard_map/ppermute | solution.py:230
  16.8 2.7 %collective-permute-start = (bf16[65,48,128]{2,1,0:T(8,128)(2,1)}, bf16[65,48,128]{2,1,0:T(8,128)(2,1)S(1)}, u32[]{:S(2)}, u32[]{:S(2)}) collective-permute-start(bf16[65,48,128]{2,1,0:T(8,128)(2,1)} %get-tuple-element.143.refs_2_), channel_id=1, source_target_pairs={{0,8},{4,12},{8,0},{12,4},{16,24},{20,28},{24,16},{28,20},{32,40},... | collective-permute-start | bytes 2396168 | tf_op jit(solution)/shard_map/ppermute | solution.py:226
  19.9 2.4 collective-permute-start.4
  23.0 11.4 %collective-permute-done.1.refs_7_ = bf16[64,48,128]{2,1,0:T(8,128)(2,1)S(1)} collective-permute-done((bf16[64,48,128]{2,1,0:T(8,128)(2,1)}, bf16[64,48,128]{2,1,0:T(8,128)(2,1)S(1)}, u32[]{:S(2)}, u32[]{:S(2)}) %collective-permute-start.1) | collective-permute-done | bytes 786464 | tf_op jit(solution)/shard_map/ppermute | solution.py:230
  34.3 2.8 %collective-permute-start.5 = (bf16[64,48,128]{2,1,0:T(8,128)(2,1)}, bf16[64,48,128]{2,1,0:T(8,128)(2,1)}, u32[]{:S(2)}, u32[]{:S(2)}) collective-permute-start(bf16[64,48,128]{2,1,0:T(8,128)(2,1)} %get-tuple-element.148), channel_id=1, source_target_pairs={{0,96},{4,100},{8,104},{12,108},{16,112},{20,116},{24,120},{28,124... | collective-permute-start | bytes 2359304 | tf_op jit(solution)/shard_map/ppermute | solution.py:230
  41.1 10.9 %collective-permute-done.3.refs_6_ = bf16[64,48,128]{2,1,0:T(8,128)(2,1)} collective-permute-done((bf16[64,48,128]{2,1,0:T(8,128)(2,1)}, bf16[64,48,128]{2,1,0:T(8,128)(2,1)}, u32[]{:S(2)}, u32[]{:S(2)}) %collective-permute-start.3) | collective-permute-done | bytes 786464 | tf_op jit(solution)/shard_map/ppermute | solution.py:230
  52.7 2.7 %collective-permute-done.2.refs_3_ = bf16[65,48,128]{2,1,0:T(8,128)(2,1)S(1)} collective-permute-done((bf16[65,48,128]{2,1,0:T(8,128)(2,1)}, bf16[65,48,128]{2,1,0:T(8,128)(2,1)S(1)}, u32[]{:S(2)}, u32[]{:S(2)}) %collective-permute-start.2) | collective-permute-done | bytes 798752 | tf_op jit(solution)/shard_map/ppermute | solution.py:226
  56.5 4.6 %choose.1 = (bf16[2,17,48,128]{3,2,1,0:T(8,128)(2,1)}, bf16[2,17,48,128]{3,2,1,0:T(8,128)(2,1)}, bf16[2,17,48,128]{3,2,1,0:T(8,128)(2,1)}, bf16[2,17,48,128]{3,2...) custom-call(s32[14]{0:T(128)} %stack.121.refs_0_, ...), custom_call_target="tpu_custom_call" | custom-call | flops 1000000 | bytes 6000000 | tf_op jit(solution)/shard_map/choose/pallas_call | solution.py:78
  63.0 3.1 %collective-permute-start.7 = (bf16[2,17,48,128]{3,2,1,0:T(8,128)(2,1)}, bf16[2,17,48,128]{3,2,1,0:T(8,128)(2,1)S(1)}, u32[]{:S(2)}, u32[]{:S(2)}) collective-permute-start(bf16[2,17,48,128]{3,2,1,0:T(8,128)(2,1)} %get-tuple-element.162), channel_id=1, source_target_pairs={{0,64},{4,68},{8,72},{12,76},{16,80},{20,84},{24,88},{28,92},{32,9... | collective-permute-start | bytes 1253384 | tf_op jit(solution)/shard_map/ppermute | solution.py:230
  67.7 5.4 %collective-permute-done.10 = bf16[2,16,48,128]{3,2,1,0:T(8,128)(2,1)S(1)} collective-permute-done((bf16[2,16,48,128]{3,2,1,0:T(8,128)(2,1)}, bf16[2,16,48,128]{3,2,1,0:T(8,128)(2,1)S(1)}, u32[]{:S(2)}, u32[]{:S(2)}) %collective-permute-start.10) | collective-permute-done | bytes 393248 | tf_op jit(solution)/shard_map/ppermute | solution.py:226
  73.8 7.7 %collective-permute-done.11 = bf16[2,16,48,128]{3,2,1,0:T(8,128)(2,1)S(1)} collective-permute-done((bf16[2,16,48,128]{3,2,1,0:T(8,128)(2,1)}, bf16[2,16,48,128]{3,2,1,0:T(8,128)(2,1)S(1)}, u32[]{:S(2)}, u32[]{:S(2)}) %collective-permute-start.11) | collective-permute-done | bytes 393248 | tf_op jit(solution)/shard_map/ppermute | solution.py:226
  85.9 3.0 %collective-permute-start.12 = (bf16[2,33,48,128]{3,2,1,0:T(8,128)(2,1)S(1)}, bf16[2,33,48,128]{3,2,1,0:T(8,128)(2,1)}, u32[]{:S(2)}, u32[]{:S(2)}) collective-permute-start(bf16[2,33,48,128]{3,2,1,0:T(8,128)(2,1)S(1)} %pad_maximum_fusion), channel_id=1, source_target_pairs={{0,16},{4,20},{8,24},{12,28},{16,0},{20,4},{24,8},{28,12},{32,48},... | collective-permute-start | bytes 2433032 | tf_op jit(solution)/shard_map/ppermute | solution.py:234
  90.2 14.4 %collective-permute-done.12 = bf16[2,33,48,128]{3,2,1,0:T(8,128)(2,1)} collective-permute-done((bf16[2,33,48,128]{3,2,1,0:T(8,128)(2,1)S(1)}, bf16[2,33,48,128]{3,2,1,0:T(8,128)(2,1)}, u32[]{:S(2)}, u32[]{:S(2)}) %collective-permute-start.12) | collective-permute-done | bytes 811040 | tf_op jit(solution)/shard_map/ppermute | solution.py:234
  110.4 3.9 %collective-permute-start.15 = (bf16[2,16,48,128]{3,2,1,0:T(8,128)(2,1)}, bf16[2,16,48,128]{3,2,1,0:T(8,128)(2,1)S(1)}, u32[]{:S(2)}, u32[]{:S(2)}) collective-permute-start(bf16[2,16,48,128]{3,2,1,0:T(8,128)(2,1)} %pad_maximum_fusion.5), channel_id=1, source_target_pairs={{0,32},{4,36},{8,40},{12,44},{16,48},{20,52},{24,56},{28,60},{32,6... | collective-permute-start | bytes 1179656 | tf_op jit(solution)/shard_map/ppermute | solution.py:230
  115.7 3.5 %collective-permute-start.18 = (bf16[2,16,48,128]{3,2,1,0:T(8,128)(2,1)S(1)}, bf16[2,16,48,128]{3,2,1,0:T(8,128)(2,1)S(1)}, u32[]{:S(2)}, u32[]{:S(2)}) collective-permute-start(bf16[2,16,48,128]{3,2,1,0:T(8,128)(2,1)S(1)} %pad_maximum_fusion.6), channel_id=1, source_target_pairs={{0,12},{4,0},{8,4},{12,8},{16,28},{20,16},{24,20},{28,24},{32,44},... | collective-permute-start | bytes 1179656 | tf_op jit(solution)/shard_map/ppermute | solution.py:226
  133.8 2.6 collective-permute-start.21
  137.5 9.0 %turn.1.refs_10_.refs_11_ = bf16[512,48,128]{2,1,0:T(8,128)(2,1)} custom-call(bf16[512,48,128]{2,1,0:T(8,128)(2,1)} %get-tuple-element.245.refs_1_.own.refs_8_.refs_9_), custom_call_target="tpu_custom_call" | custom-call | flops 1000000 | bytes 25000000 | tf_op jit(solution)/shard_map/turn/pallas_call | solution.py:101
  146.9 2.6 collective-permute-done.20.refs_5_
  151.2 2.6 collective-permute-start.25
  153.8 2.7 %collective-permute-start.26 = (bf16[64,48,128]{2,1,0:T(8,128)(2,1)S(1)}, bf16[64,48,128]{2,1,0:T(8,128)(2,1)S(1)}, u32[]{:S(2)}, u32[]{:S(2)}) collective-permute-start(bf16[64,48,128]{2,1,0:T(8,128)(2,1)S(1)} %pad_maximum_fusion.2.refs_4_), channel_id=1, source_target_pairs={{0,96},{4,100},{8,104},{12,108},{16,112},{20,116},{24,120},{28,124... | collective-permute-start | bytes 2359304 | tf_op jit(solution)/shard_map/ppermute | solution.py:230
  157.7 8.7 %collective-permute-done.23.refs_3_ = bf16[64,48,128]{2,1,0:T(8,128)(2,1)} collective-permute-done((bf16[64,48,128]{2,1,0:T(8,128)(2,1)}, bf16[64,48,128]{2,1,0:T(8,128)(2,1)}, u32[]{:S(2)}, u32[]{:S(2)}) %collective-permute-start.23) | collective-permute-done | bytes 786464 | tf_op jit(solution)/shard_map/ppermute | solution.py:226
  169.9 3.5 %collective-permute-start.30 = (bf16[64,48,128]{2,1,0:T(8,128)(2,1)S(1)}, bf16[64,48,128]{2,1,0:T(8,128)(2,1)S(1)}, u32[]{:S(2)}, u32[]{:S(2)}) collective-permute-start(bf16[64,48,128]{2,1,0:T(8,128)(2,1)S(1)} %collective-permute-done.26.refs_6_), channel_id=1, source_target_pairs={{0,96},{4,100},{8,104},{12,108},{16,112},{20,116},{24,120},{28,124... | collective-permute-start | bytes 2359304 | tf_op jit(solution)/shard_map/ppermute | solution.py:230
  173.4 19.4 %corr.2 = (bf16[512,1024]{1,0:T(8,128)(2,1)}, bf16[512,1024]{1,0:T(8,128)(2,1)}, bf16[512,1024]{1,0:T(8,128)(2,1)}, bf16[512,1024]{1,0:T(8,128)(2,1)}) custom-call(s32[8]{0:T(128)} %stack.132.place, s32[4]{0:T(128)} %pad_add_fusion.order, bf16[64,48,128]{2,1,0:T(8,128)(2,1)} %copy-done.11, bf16[64,48,128]{2,1,0:T(8,128)(2,1)} %collective-permute-done.19.refs_1_, ...), custom_call_target="tpu_custom_call" | custom-call | flops 22000001024 | bytes 40000000 | tf_op jit(solution)/shard_map/corr/pallas_call | solution.py:170
  193.0 7.8 %collective-permute-start.31 = (bf16[512,1024]{1,0:T(8,128)(2,1)}, bf16[512,1024]{1,0:T(8,128)(2,1)S(1)}, u32[]{:S(2)}, u32[]{:S(2)}) collective-permute-start(bf16[512,1024]{1,0:T(8,128)(2,1)} %get-tuple-element.228), channel_id=1, source_target_pairs={{0,1},{1,0},{2,3},{3,2},{4,5},{5,4},{6,7},{7,6},{8,9},{9,8},{10,11... | collective-permute-start | bytes 3145736 | tf_op jit(solution)/shard_map/ppermute | solution.py:344
  200.8 2.5 collective-permute-done.31
  206.9 19.4 %corr.3 = (bf16[512,1024]{1,0:T(8,128)(2,1)}, bf16[512,1024]{1,0:T(8,128)(2,1)}, bf16[512,1024]{1,0:T(8,128)(2,1)}, bf16[512,1024]{1,0:T(8,128)(2,1)}) custom-call(s32[8]{0:T(128)} %stack.132.place, s32[4]{0:T(128)} %pad_add_fusion.order, bf16[64,48,128]{2,1,0:T(8,128)(2,1)} %copy-done.12, bf16[64,48,128]{2,1,0:T(8,128)(2,1)} %copy-done.26, ...), custom_call_target="tpu_custom_call" | custom-call | flops 22000001024 | bytes 40000000 | tf_op jit(solution)/shard_map/corr/pallas_call | solution.py:170
  226.4 3.0 %collective-permute-done.32.c = bf16[512,1024]{1,0:T(8,128)(2,1)S(1)} collective-permute-done((bf16[512,1024]{1,0:T(8,128)(2,1)S(1)}, bf16[512,1024]{1,0:T(8,128)(2,1)S(1)}, u32[]{:S(2)}, u32[]{:S(2)}) %collective-permute-start.32) | collective-permute-done | bytes 1048608 | tf_op jit(solution)/shard_map/ppermute | solution.py:348
  230.7 2.5 collective-permute-done.34
  236.8 2.9 %finish.2.refs_0_ = bf16[2,1024,512]{2,1,0:T(8,128)(2,1)} custom-call(bf16[512,1024]{1,0:T(8,128)(2,1)} %get-tuple-element.261.a, bf16[512,1024]{1,0:T(8,128)(2,1)} %copy-done.1, bf16[512,1024]{1,0:T(8,128)(2,1)} %copy-done), custom_call_target="tpu_custom_call" | custom-call | tf_op jit(solution)/shard_map/finish/pallas_call | solution.py:204
  239.7 19.5 %collective-permute-done.35.c = bf16[512,1024]{1,0:T(8,128)(2,1)S(1)} collective-permute-done((bf16[512,1024]{1,0:T(8,128)(2,1)S(1)}, bf16[512,1024]{1,0:T(8,128)(2,1)S(1)}, u32[]{:S(2)}, u32[]{:S(2)}) %collective-permute-start.35) | collective-permute-done | bytes 1048608 | tf_op jit(solution)/shard_map/ppermute | solution.py:348
  261.2 2.9 %finish.3 = bf16[2,1024,512]{2,1,0:T(8,128)(2,1)} custom-call(bf16[512,1024]{1,0:T(8,128)(2,1)} %get-tuple-element.252.a, bf16[512,1024]{1,0:T(8,128)(2,1)} %copy-done.3, bf16[512,1024]{1,0:T(8,128)(2,1)} %copy-done.2, bf16[2,1024,512]{2,1,0:T(8,128)(2,1)} %finish.2.refs_0_), custom_call_target="tpu_custom_call", output_to_operand_aliasing={{}: (3, {})} | custom-call | tf_op jit(solution)/shard_map/finish/pallas_call | solution.py:204
  (144 shorter events, 53.5 us)
Async XLA Ops:
  12.4 21.9 %collective-permute-start.1 = (bf16[64,48,128]{2,1,0:T(8,128)(2,1)}, bf16[64,48,128]{2,1,0:T(8,128)(2,1)S(1)}, u32[]{:S(2)}, u32[]{:S(2)}) collective-permute-start(bf16[64,48,128]{2,1,0:T(8,128)(2,1)} %get-tuple-element.144), channel_id=1, source_target_pairs={{0,64},{4,68},{8,72},{12,76},{16,80},{20,84},{24,88},{28,92},{32,9... | collective-permute-start | bytes 2359304 | tf_op jit(solution)/shard_map/ppermute | solution.py:230
  16.8 35.9 %collective-permute-start = (bf16[65,48,128]{2,1,0:T(8,128)(2,1)}, bf16[65,48,128]{2,1,0:T(8,128)(2,1)S(1)}, u32[]{:S(2)}, u32[]{:S(2)}) collective-permute-start(bf16[65,48,128]{2,1,0:T(8,128)(2,1)} %get-tuple-element.143.refs_2_), channel_id=1, source_target_pairs={{0,8},{4,12},{8,0},{12,4},{16,24},{20,28},{24,16},{28,20},{32,40},... | collective-permute-start | bytes 2396168 | tf_op jit(solution)/shard_map/ppermute | solution.py:226
  19.6 35.8 %collective-permute-start.2 = (bf16[65,48,128]{2,1,0:T(8,128)(2,1)}, bf16[65,48,128]{2,1,0:T(8,128)(2,1)S(1)}, u32[]{:S(2)}, u32[]{:S(2)}) collective-permute-start(bf16[65,48,128]{2,1,0:T(8,128)(2,1)} %get-tuple-element.145), channel_id=1, source_target_pairs={{0,4},{4,8},{8,12},{12,0},{16,20},{20,24},{24,28},{28,16},{32,36},... | collective-permute-start | bytes 2396168 | tf_op jit(solution)/shard_map/ppermute | solution.py:226
  19.9 35.5 %collective-permute-start.4 = (bf16[65,48,128]{2,1,0:T(8,128)(2,1)}, bf16[65,48,128]{2,1,0:T(8,128)(2,1)S(1)}, u32[]{:S(2)}, u32[]{:S(2)}) collective-permute-start(bf16[65,48,128]{2,1,0:T(8,128)(2,1)} %get-tuple-element.147), channel_id=1, source_target_pairs={{0,12},{4,0},{8,4},{12,8},{16,28},{20,16},{24,20},{28,24},{32,44},... | collective-permute-start | bytes 2396168 | tf_op jit(solution)/shard_map/ppermute | solution.py:226
  22.2 29.7 %collective-permute-start.3 = (bf16[64,48,128]{2,1,0:T(8,128)(2,1)}, bf16[64,48,128]{2,1,0:T(8,128)(2,1)}, u32[]{:S(2)}, u32[]{:S(2)}) collective-permute-start(bf16[64,48,128]{2,1,0:T(8,128)(2,1)} %get-tuple-element.146), channel_id=1, source_target_pairs={{0,32},{4,36},{8,40},{12,44},{16,48},{20,52},{24,56},{28,60},{32,6... | collective-permute-start | bytes 2359304 | tf_op jit(solution)/shard_map/ppermute | solution.py:230
  34.3 18.4 %collective-permute-start.5 = (bf16[64,48,128]{2,1,0:T(8,128)(2,1)}, bf16[64,48,128]{2,1,0:T(8,128)(2,1)}, u32[]{:S(2)}, u32[]{:S(2)}) collective-permute-start(bf16[64,48,128]{2,1,0:T(8,128)(2,1)} %get-tuple-element.148), channel_id=1, source_target_pairs={{0,96},{4,100},{8,104},{12,108},{16,112},{20,116},{24,120},{28,124... | collective-permute-start | bytes 2359304 | tf_op jit(solution)/shard_map/ppermute | solution.py:230
  62.3 21.3 %collective-permute-start.6 = (bf16[2,17,48,128]{3,2,1,0:T(8,128)(2,1)}, bf16[2,17,48,128]{3,2,1,0:T(8,128)(2,1)S(1)}, u32[]{:S(2)}, u32[]{:S(2)}) collective-permute-start(bf16[2,17,48,128]{3,2,1,0:T(8,128)(2,1)} %get-tuple-element.161), channel_id=1, source_target_pairs={{0,32},{4,36},{8,40},{12,44},{16,48},{20,52},{24,56},{28,60},{32,6... | collective-permute-start | bytes 1253384 | tf_op jit(solution)/shard_map/ppermute | solution.py:230
  63.0 20.5 %collective-permute-start.7 = (bf16[2,17,48,128]{3,2,1,0:T(8,128)(2,1)}, bf16[2,17,48,128]{3,2,1,0:T(8,128)(2,1)S(1)}, u32[]{:S(2)}, u32[]{:S(2)}) collective-permute-start(bf16[2,17,48,128]{3,2,1,0:T(8,128)(2,1)} %get-tuple-element.162), channel_id=1, source_target_pairs={{0,64},{4,68},{8,72},{12,76},{16,80},{20,84},{24,88},{28,92},{32,9... | collective-permute-start | bytes 1253384 | tf_op jit(solution)/shard_map/ppermute | solution.py:230
  66.2 17.7 %collective-permute-start.8 = (bf16[2,17,48,128]{3,2,1,0:T(8,128)(2,1)}, bf16[2,17,48,128]{3,2,1,0:T(8,128)(2,1)S(1)}, u32[]{:S(2)}, u32[]{:S(2)}) collective-permute-start(bf16[2,17,48,128]{3,2,1,0:T(8,128)(2,1)} %get-tuple-element.163), channel_id=1, source_target_pairs={{0,96},{4,100},{8,104},{12,108},{16,112},{20,116},{24,120},{28,124... | collective-permute-start | bytes 1253384 | tf_op jit(solution)/shard_map/ppermute | solution.py:230
  66.2 15.3 %collective-permute-start.11 = (bf16[2,16,48,128]{3,2,1,0:T(8,128)(2,1)}, bf16[2,16,48,128]{3,2,1,0:T(8,128)(2,1)S(1)}, u32[]{:S(2)}, u32[]{:S(2)}) collective-permute-start(bf16[2,16,48,128]{3,2,1,0:T(8,128)(2,1)} %get-tuple-element.166), channel_id=1, source_target_pairs={{0,12},{4,0},{8,4},{12,8},{16,28},{20,16},{24,20},{28,24},{32,44},... | collective-permute-start | bytes 1179656 | tf_op jit(solution)/shard_map/ppermute | solution.py:226
  85.9 18.7 %collective-permute-start.12 = (bf16[2,33,48,128]{3,2,1,0:T(8,128)(2,1)S(1)}, bf16[2,33,48,128]{3,2,1,0:T(8,128)(2,1)}, u32[]{:S(2)}, u32[]{:S(2)}) collective-permute-start(bf16[2,33,48,128]{3,2,1,0:T(8,128)(2,1)S(1)} %pad_maximum_fusion), channel_id=1, source_target_pairs={{0,16},{4,20},{8,24},{12,28},{16,0},{20,4},{24,8},{28,12},{32,48},... | collective-permute-start | bytes 2433032 | tf_op jit(solution)/shard_map/ppermute | solution.py:234
  109.0 19.2 %collective-permute-start.14 = (bf16[2,16,48,128]{3,2,1,0:T(8,128)(2,1)S(1)}, bf16[2,16,48,128]{3,2,1,0:T(8,128)(2,1)S(1)}, u32[]{:S(2)}, u32[]{:S(2)}) collective-permute-start(bf16[2,16,48,128]{3,2,1,0:T(8,128)(2,1)S(1)} %pad_maximum_fusion.6), channel_id=1, source_target_pairs={{0,8},{4,12},{8,0},{12,4},{16,24},{20,28},{24,16},{28,20},{32,40},... | collective-permute-start | bytes 1179656 | tf_op jit(solution)/shard_map/ppermute | solution.py:226
  110.4 17.7 %collective-permute-start.15 = (bf16[2,16,48,128]{3,2,1,0:T(8,128)(2,1)}, bf16[2,16,48,128]{3,2,1,0:T(8,128)(2,1)S(1)}, u32[]{:S(2)}, u32[]{:S(2)}) collective-permute-start(bf16[2,16,48,128]{3,2,1,0:T(8,128)(2,1)} %pad_maximum_fusion.5), channel_id=1, source_target_pairs={{0,32},{4,36},{8,40},{12,44},{16,48},{20,52},{24,56},{28,60},{32,6... | collective-permute-start | bytes 1179656 | tf_op jit(solution)/shard_map/ppermute | solution.py:230
  114.3 14.8 %collective-permute-start.16 = (bf16[2,16,48,128]{3,2,1,0:T(8,128)(2,1)S(1)}, bf16[2,16,48,128]{3,2,1,0:T(8,128)(2,1)S(1)}, u32[]{:S(2)}, u32[]{:S(2)}) collective-permute-start(bf16[2,16,48,128]{3,2,1,0:T(8,128)(2,1)S(1)} %pad_maximum_fusion.6), channel_id=1, source_target_pairs={{0,4},{4,8},{8,12},{12,0},{16,20},{20,24},{24,28},{28,16},{32,36},... | collective-permute-start | bytes 1179656 | tf_op jit(solution)/shard_map/ppermute | solution.py:226
  115.3 14.1 %collective-permute-start.17 = (bf16[2,16,48,128]{3,2,1,0:T(8,128)(2,1)}, bf16[2,16,48,128]{3,2,1,0:T(8,128)(2,1)S(1)}, u32[]{:S(2)}, u32[]{:S(2)}) collective-permute-start(bf16[2,16,48,128]{3,2,1,0:T(8,128)(2,1)} %pad_maximum_fusion.5), channel_id=1, source_target_pairs={{0,96},{4,100},{8,104},{12,108},{16,112},{20,116},{24,120},{28,124... | collective-permute-start | bytes 1179656 | tf_op jit(solution)/shard_map/ppermute | solution.py:230
  115.7 13.7 %collective-permute-start.18 = (bf16[2,16,48,128]{3,2,1,0:T(8,128)(2,1)S(1)}, bf16[2,16,48,128]{3,2,1,0:T(8,128)(2,1)S(1)}, u32[]{:S(2)}, u32[]{:S(2)}) collective-permute-start(bf16[2,16,48,128]{3,2,1,0:T(8,128)(2,1)S(1)} %pad_maximum_fusion.6), channel_id=1, source_target_pairs={{0,12},{4,0},{8,4},{12,8},{16,28},{20,16},{24,20},{28,24},{32,44},... | collective-permute-start | bytes 1179656 | tf_op jit(solution)/shard_map/ppermute | solution.py:226
  129.9 16.9 %collective-permute-start.19 = (bf16[64,48,128]{2,1,0:T(8,128)(2,1)S(1)}, bf16[64,48,128]{2,1,0:T(8,128)(2,1)}, u32[]{:S(2)}, u32[]{:S(2)}) collective-permute-start(bf16[64,48,128]{2,1,0:T(8,128)(2,1)S(1)} %pad_maximum_fusion.3.refs_0_), channel_id=1, source_target_pairs={{0,4},{4,8},{8,12},{12,0},{16,20},{20,24},{24,28},{28,16},{32,36},... | collective-permute-start | bytes 2359304 | tf_op jit(solution)/shard_map/ppermute | solution.py:226
  132.1 17.4 %collective-permute-start.20 = (bf16[64,48,128]{2,1,0:T(8,128)(2,1)S(1)}, bf16[64,48,128]{2,1,0:T(8,128)(2,1)}, u32[]{:S(2)}, u32[]{:S(2)}) collective-permute-start(bf16[64,48,128]{2,1,0:T(8,128)(2,1)S(1)} %pad_maximum_fusion.4.refs_4_), channel_id=1, source_target_pairs={{0,32},{4,36},{8,40},{12,44},{16,48},{20,52},{24,56},{28,60},{32,6... | collective-permute-start | bytes 2359304 | tf_op jit(solution)/shard_map/ppermute | solution.py:230
  133.8 15.7 %collective-permute-start.21 = (bf16[64,48,128]{2,1,0:T(8,128)(2,1)S(1)}, bf16[64,48,128]{2,1,0:T(8,128)(2,1)S(1)}, u32[]{:S(2)}, u32[]{:S(2)}) collective-permute-start(bf16[64,48,128]{2,1,0:T(8,128)(2,1)S(1)} %pad_maximum_fusion.3.refs_0_), channel_id=1, source_target_pairs={{0,12},{4,0},{8,4},{12,8},{16,28},{20,16},{24,20},{28,24},{32,44},... | collective-permute-start | bytes 2359304 | tf_op jit(solution)/shard_map/ppermute | solution.py:226
  136.4 14.7 %collective-permute-start.22 = (bf16[64,48,128]{2,1,0:T(8,128)(2,1)S(1)}, bf16[64,48,128]{2,1,0:T(8,128)(2,1)S(1)}, u32[]{:S(2)}, u32[]{:S(2)}) collective-permute-start(bf16[64,48,128]{2,1,0:T(8,128)(2,1)S(1)} %pad_maximum_fusion.4.refs_4_), channel_id=1, source_target_pairs={{0,96},{4,100},{8,104},{12,108},{16,112},{20,116},{24,120},{28,124... | collective-permute-start | bytes 2359304 | tf_op jit(solution)/shard_map/ppermute | solution.py:230
  151.1 15.3 %collective-permute-start.23 = (bf16[64,48,128]{2,1,0:T(8,128)(2,1)}, bf16[64,48,128]{2,1,0:T(8,128)(2,1)}, u32[]{:S(2)}, u32[]{:S(2)}) collective-permute-start(bf16[64,48,128]{2,1,0:T(8,128)(2,1)} %collective-permute-done.19.refs_1_), channel_id=1, source_target_pairs={{0,4},{4,8},{8,12},{12,0},{16,20},{20,24},{24,28},{28,16},{32,36},... | collective-permute-start | bytes 2359304 | tf_op jit(solution)/shard_map/ppermute | solution.py:226
  151.1 15.3 %collective-permute-start.24 = (bf16[64,48,128]{2,1,0:T(8,128)(2,1)}, bf16[64,48,128]{2,1,0:T(8,128)(2,1)}, u32[]{:S(2)}, u32[]{:S(2)}) collective-permute-start(bf16[64,48,128]{2,1,0:T(8,128)(2,1)} %collective-permute-done.20.refs_5_), channel_id=1, source_target_pairs={{0,32},{4,36},{8,40},{12,44},{16,48},{20,52},{24,56},{28,60},{32,6... | collective-permute-start | bytes 2359304 | tf_op jit(solution)/shard_map/ppermute | solution.py:230
  151.2 15.2 %collective-permute-start.25 = (bf16[64,48,128]{2,1,0:T(8,128)(2,1)S(1)}, bf16[64,48,128]{2,1,0:T(8,128)(2,1)S(1)}, u32[]{:S(2)}, u32[]{:S(2)}) collective-permute-start(bf16[64,48,128]{2,1,0:T(8,128)(2,1)S(1)} %pad_maximum_fusion.1.refs_0_), channel_id=1, source_target_pairs={{0,12},{4,0},{8,4},{12,8},{16,28},{20,16},{24,20},{28,24},{32,44},... | collective-permute-start | bytes 2359304 | tf_op jit(solution)/shard_map/ppermute | solution.py:226
  153.8 13.4 %collective-permute-start.26 = (bf16[64,48,128]{2,1,0:T(8,128)(2,1)S(1)}, bf16[64,48,128]{2,1,0:T(8,128)(2,1)S(1)}, u32[]{:S(2)}, u32[]{:S(2)}) collective-permute-start(bf16[64,48,128]{2,1,0:T(8,128)(2,1)S(1)} %pad_maximum_fusion.2.refs_4_), channel_id=1, source_target_pairs={{0,96},{4,100},{8,104},{12,108},{16,112},{20,116},{24,120},{28,124... | collective-permute-start | bytes 2359304 | tf_op jit(solution)/shard_map/ppermute | solution.py:230
  167.2 25.7 %collective-permute-start.27 = (bf16[64,48,128]{2,1,0:T(8,128)(2,1)S(1)}, bf16[64,48,128]{2,1,0:T(8,128)(2,1)S(1)}, u32[]{:S(2)}, u32[]{:S(2)}) collective-permute-start(bf16[64,48,128]{2,1,0:T(8,128)(2,1)S(1)} %pad_maximum_fusion.1.refs_0_), channel_id=1, source_target_pairs={{0,4},{4,8},{8,12},{12,0},{16,20},{20,24},{24,28},{28,16},{32,36},... | collective-permute-start | bytes 2359304 | tf_op jit(solution)/shard_map/ppermute | solution.py:226
  167.6 25.3 %collective-permute-start.28 = (bf16[64,48,128]{2,1,0:T(8,128)(2,1)S(1)}, bf16[64,48,128]{2,1,0:T(8,128)(2,1)S(1)}, u32[]{:S(2)}, u32[]{:S(2)}) collective-permute-start(bf16[64,48,128]{2,1,0:T(8,128)(2,1)S(1)} %pad_maximum_fusion.2.refs_4_), channel_id=1, source_target_pairs={{0,32},{4,36},{8,40},{12,44},{16,48},{20,52},{24,56},{28,60},{32,6... | collective-permute-start | bytes 2359304 | tf_op jit(solution)/shard_map/ppermute | solution.py:230
  167.7 25.3 %collective-permute-start.29 = (bf16[64,48,128]{2,1,0:T(8,128)(2,1)S(1)}, bf16[64,48,128]{2,1,0:T(8,128)(2,1)S(1)}, u32[]{:S(2)}, u32[]{:S(2)}) collective-permute-start(bf16[64,48,128]{2,1,0:T(8,128)(2,1)S(1)} %collective-permute-done.25.refs_2_), channel_id=1, source_target_pairs={{0,12},{4,0},{8,4},{12,8},{16,28},{20,16},{24,20},{28,24},{32,44},... | collective-permute-start | bytes 2359304 | tf_op jit(solution)/shard_map/ppermute | solution.py:226
  169.9 23.1 %collective-permute-start.30 = (bf16[64,48,128]{2,1,0:T(8,128)(2,1)S(1)}, bf16[64,48,128]{2,1,0:T(8,128)(2,1)S(1)}, u32[]{:S(2)}, u32[]{:S(2)}) collective-permute-start(bf16[64,48,128]{2,1,0:T(8,128)(2,1)S(1)} %collective-permute-done.26.refs_6_), channel_id=1, source_target_pairs={{0,96},{4,100},{8,104},{12,108},{16,112},{20,116},{24,120},{28,124... | collective-permute-start | bytes 2359304 | tf_op jit(solution)/shard_map/ppermute | solution.py:230
  204.9 24.5 %collective-permute-start.32 = (bf16[512,1024]{1,0:T(8,128)(2,1)S(1)}, bf16[512,1024]{1,0:T(8,128)(2,1)S(1)}, u32[]{:S(2)}, u32[]{:S(2)}) collective-permute-start(bf16[512,1024]{1,0:T(8,128)(2,1)S(1)} %add_convert_fusion.1), channel_id=1, source_target_pairs={{0,2},{1,3},{2,0},{3,1},{4,6},{5,7},{6,4},{7,5},{8,10},{9,11},{10,... | collective-permute-start | bytes 3145736 | tf_op jit(solution)/shard_map/ppermute | solution.py:348
  206.3 23.1 %collective-permute-start.33 = (bf16[512,1024]{1,0:T(8,128)(2,1)S(1)}, bf16[512,1024]{1,0:T(8,128)(2,1)S(1)}, u32[]{:S(2)}, u32[]{:S(2)}) collective-permute-start(bf16[512,1024]{1,0:T(8,128)(2,1)S(1)} %copy-done.20), channel_id=1, source_target_pairs={{0,1},{1,0},{2,3},{3,2},{4,5},{5,4},{6,7},{7,6},{8,9},{9,8},{10,11... | collective-permute-start | bytes 3145736 | tf_op jit(solution)/shard_map/ppermute | solution.py:344
  234.8 24.5 %collective-permute-start.35 = (bf16[512,1024]{1,0:T(8,128)(2,1)S(1)}, bf16[512,1024]{1,0:T(8,128)(2,1)S(1)}, u32[]{:S(2)}, u32[]{:S(2)}) collective-permute-start(bf16[512,1024]{1,0:T(8,128)(2,1)S(1)} %add_convert_fusion), channel_id=1, source_target_pairs={{0,2},{1,3},{2,0},{3,1},{4,6},{5,7},{6,4},{7,5},{8,10},{9,11},{10,... | collective-permute-start | bytes 3145736 | tf_op jit(solution)/shard_map/ppermute | solution.py:348
  236.1 23.1 %collective-permute-start.36 = (bf16[512,1024]{1,0:T(8,128)(2,1)S(1)}, bf16[512,1024]{1,0:T(8,128)(2,1)S(1)}, u32[]{:S(2)}, u32[]{:S(2)}) collective-permute-start(bf16[512,1024]{1,0:T(8,128)(2,1)S(1)} %copy-done.21), channel_id=1, source_target_pairs={{0,1},{1,0},{2,3},{3,2},{4,5},{5,4},{6,7},{7,6},{8,9},{9,8},{10,11... | collective-permute-start | bytes 3145736 | tf_op jit(solution)/shard_map/ppermute | solution.py:344
  (35 other events, 440.4 us)

commit v5 on v4

--- a/solution.py
+++ b/solution.py
@@ -305,19 +305,13 @@
     )
     got_a = [cuts[0], *got[:3]]
     got_b = [cuts[4], *got[3:]]
-    mine = jnp.stack(
-        [
-            jnp.concatenate(
-                [pick((z - r[0]) & 3, [g[i] for g in got_a]), pick((x - r[2]) & 3, [g[i] for g in got_b])]
-            )
-            for i, r in enumerate(roots)
-        ]
-    )
-    (other,) = spread([mine], [swap_y])
+    mine_a = jnp.stack([pick((z - r[0]) & 3, [g[i] for g in got_a]) for i, r in enumerate(roots)])
+    mine_b = jnp.stack([pick((x - r[2]) & 3, [g[i] for g in got_b]) for i, r in enumerate(roots)])
+    other_a, other_b = spread([mine_a, mine_b], [swap_y] * 2)
     here = [h == r[1] for r in roots]
     sub = [
-        jnp.stack([jnp.where(here[i], mine[i, rows], other[i, rows]) for i in range(STEPS)])
-        for rows in (slice(0, 16), slice(17, 33))
+        jnp.stack([jnp.where(here[i], mine[i, :16], other[i, :16]) for i in range(STEPS)])
+        for mine, other in ((mine_a, other_a), (mine_b, other_b))
     ]
 
     def scales(mine, other):
@@ -328,7 +322,7 @@
             out.append(inv.reshape(4, 1, 1024))
         return out
 
-    got = spread(sub * 3, Z_THEN_X, scales, [mine, other])
+    got = spread(sub * 3, Z_THEN_X, scales, [mine_a, other_a])
     from_z, from_x = by_hop(got[:6])
     all_a = [sub[0], *from_z]
     all_b = [sub[1], *from_x]

time: 265 us -> 264 us (level)
    ppermute x1 -> x2, waiting for transfers between devices: 14.4 us -> 14.6 us  [swap_y(): return lax.ppermute(a, 'station', [(s, s ^ 4) for s in range(32)])]
  transfers between devices with their start and end apart: 37 -> 38, of which waited for: 20 -> 21; matrix products, arithmetic and copies ran while one was open for 4% -> 4% of each run, Pallas kernels for 19% -> 19%
where the time goes in v5:
time: 264 us; the launch traced here: 263 us
  waiting for transfers between devices  100 us (38%)
  Pallas kernels  70 us (27%)
  starting transfers between devices  67.5 us (26%)
  local copies, waits for them, and re-layouts  12.1 us (5%)
  other arithmetic  9.48 us (4%)
  between operations  4.02 us (2%)
    pallas_call x2, Pallas kernels, corr(): pl.pallas_call(corr_kernel, grid_spec=pltpu.PrefetchScalarGridSpec(num_sc...  38.8 us
    ppermute x15, waiting for transfers between devices, along_z(): lax.ppermute(a, 'station', [(s, (s + 8 * d) % 32) for s in range(32)])  30.2 us
    ppermute x15, waiting for transfers between devices, along_x(): lax.ppermute(a, 'station', [(s, s - s % 4 + (s + d) % 4) for s in range(3...  27.7 us
    ppermute x15, starting transfers between devices, along_z(): lax.ppermute(a, 'station', [(s, (s + 8 * d) % 32) for s in range(32)])  26.9 us
    ppermute x15, starting transfers between devices, along_x(): lax.ppermute(a, 'station', [(s, s - s % 4 + (s + d) % 4) for s in range(3...  24.7 us
    ppermute x2, waiting for transfers between devices, other_chip(): return lax.ppermute(a, 'tm', [(t, t ^ 2) for t in range(4)])  22.5 us
    ppermute x2, waiting for transfers between devices, swap_y(): return lax.ppermute(a, 'station', [(s, s ^ 4) for s in range(32)])  14.6 us
    pallas_call x1, Pallas kernels, whiten(): pl.pallas_call(whiten_kernel, grid_spec=pltpu.PrefetchScalarGridSpec(num_...  11.7 us
  transfers between devices with their start and end apart: 38, of which 21 were waited for; matrix products, arithmetic and copies ran while one was open for 4% of the time, Pallas kernels for 19%

profile of v5, /device:TPU:1, one launch (start us, length us, event | category | flops | bytes accessed | tf_op | source)
XLA Modules:
  0.0 263.2 jit_solution(16647590362296319037)
XLA Ops:
  0.6 11.7 %whiten.1 = (bf16[512,48,128]{2,1,0:T(8,128)(2,1)}, bf16[65,48,128]{2,1,0:T(8,128)(2,1)}, bf16[64,48,128]{2,1,0:T(8,128)(2,1)}, bf16[65,48,128]{2,1,0:T(8,128)(2...) custom-call(s32[6]{0:T(128)} %stack.126.place, ...), custom_call_target="tpu_custom_call" | custom-call | flops 100000000 | bytes 18000000 | tf_op jit(solution)/shard_map/whiten/pallas_call | solution.py:40
  12.4 4.4 %collective-permute-start.1 = (bf16[64,48,128]{2,1,0:T(8,128)(2,1)}, bf16[64,48,128]{2,1,0:T(8,128)(2,1)S(1)}, u32[]{:S(2)}, u32[]{:S(2)}) collective-permute-start(bf16[64,48,128]{2,1,0:T(8,128)(2,1)} %get-tuple-element.148), channel_id=1, source_target_pairs={{0,64},{4,68},{8,72},{12,76},{16,80},{20,84},{24,88},{28,92},{32,9... | collective-permute-start | bytes 2359304 | tf_op jit(solution)/shard_map/ppermute | solution.py:230
  16.8 2.7 %collective-permute-start = (bf16[65,48,128]{2,1,0:T(8,128)(2,1)}, bf16[65,48,128]{2,1,0:T(8,128)(2,1)S(1)}, u32[]{:S(2)}, u32[]{:S(2)}) collective-permute-start(bf16[65,48,128]{2,1,0:T(8,128)(2,1)} %get-tuple-element.147.refs_2_), channel_id=1, source_target_pairs={{0,8},{4,12},{8,0},{12,4},{16,24},{20,28},{24,16},{28,20},{32,40},... | collective-permute-start | bytes 2396168 | tf_op jit(solution)/shard_map/ppermute | solution.py:226
  23.0 11.4 %collective-permute-done.1.refs_7_ = bf16[64,48,128]{2,1,0:T(8,128)(2,1)S(1)} collective-permute-done((bf16[64,48,128]{2,1,0:T(8,128)(2,1)}, bf16[64,48,128]{2,1,0:T(8,128)(2,1)S(1)}, u32[]{:S(2)}, u32[]{:S(2)}) %collective-permute-start.1) | collective-permute-done | bytes 786464 | tf_op jit(solution)/shard_map/ppermute | solution.py:230
  34.3 2.8 %collective-permute-start.5 = (bf16[64,48,128]{2,1,0:T(8,128)(2,1)}, bf16[64,48,128]{2,1,0:T(8,128)(2,1)}, u32[]{:S(2)}, u32[]{:S(2)}) collective-permute-start(bf16[64,48,128]{2,1,0:T(8,128)(2,1)} %get-tuple-element.152), channel_id=1, source_target_pairs={{0,96},{4,100},{8,104},{12,108},{16,112},{20,116},{24,120},{28,124... | collective-permute-start | bytes 2359304 | tf_op jit(solution)/shard_map/ppermute | solution.py:230
  40.8 11.2 %collective-permute-done.3.refs_6_ = bf16[64,48,128]{2,1,0:T(8,128)(2,1)} collective-permute-done((bf16[64,48,128]{2,1,0:T(8,128)(2,1)}, bf16[64,48,128]{2,1,0:T(8,128)(2,1)}, u32[]{:S(2)}, u32[]{:S(2)}) %collective-permute-start.3) | collective-permute-done | bytes 786464 | tf_op jit(solution)/shard_map/ppermute | solution.py:230
  52.7 2.7 %collective-permute-done.2.refs_3_ = bf16[65,48,128]{2,1,0:T(8,128)(2,1)S(1)} collective-permute-done((bf16[65,48,128]{2,1,0:T(8,128)(2,1)}, bf16[65,48,128]{2,1,0:T(8,128)(2,1)S(1)}, u32[]{:S(2)}, u32[]{:S(2)}) %collective-permute-start.2) | collective-permute-done | bytes 798752 | tf_op jit(solution)/shard_map/ppermute | solution.py:226
  56.5 4.6 %choose.1 = (bf16[2,17,48,128]{3,2,1,0:T(8,128)(2,1)}, bf16[2,17,48,128]{3,2,1,0:T(8,128)(2,1)}, bf16[2,17,48,128]{3,2,1,0:T(8,128)(2,1)}, bf16[2,17,48,128]{3,2...) custom-call(s32[14]{0:T(128)} %stack.122.refs_0_, ...), custom_call_target="tpu_custom_call" | custom-call | flops 1000000 | bytes 6000000 | tf_op jit(solution)/shard_map/choose/pallas_call | solution.py:78
  63.1 3.1 %collective-permute-start.7 = (bf16[2,17,48,128]{3,2,1,0:T(8,128)(2,1)}, bf16[2,17,48,128]{3,2,1,0:T(8,128)(2,1)S(1)}, u32[]{:S(2)}, u32[]{:S(2)}) collective-permute-start(bf16[2,17,48,128]{3,2,1,0:T(8,128)(2,1)} %get-tuple-element.166), channel_id=1, source_target_pairs={{0,64},{4,68},{8,72},{12,76},{16,80},{20,84},{24,88},{28,92},{32,9... | collective-permute-start | bytes 1253384 | tf_op jit(solution)/shard_map/ppermute | solution.py:230
  67.7 5.4 %collective-permute-done.10 = bf16[2,16,48,128]{3,2,1,0:T(8,128)(2,1)S(1)} collective-permute-done((bf16[2,16,48,128]{3,2,1,0:T(8,128)(2,1)}, bf16[2,16,48,128]{3,2,1,0:T(8,128)(2,1)S(1)}, u32[]{:S(2)}, u32[]{:S(2)}) %collective-permute-start.10) | collective-permute-done | bytes 393248 | tf_op jit(solution)/shard_map/ppermute | solution.py:226
  73.8 7.7 %collective-permute-done.11 = bf16[2,16,48,128]{3,2,1,0:T(8,128)(2,1)S(1)} collective-permute-done((bf16[2,16,48,128]{3,2,1,0:T(8,128)(2,1)}, bf16[2,16,48,128]{3,2,1,0:T(8,128)(2,1)S(1)}, u32[]{:S(2)}, u32[]{:S(2)}) %collective-permute-start.11) | collective-permute-done | bytes 393248 | tf_op jit(solution)/shard_map/ppermute | solution.py:226
  85.2 3.0 %collective-permute-start.12 = (bf16[2,17,48,128]{3,2,1,0:T(8,128)(2,1)S(1)}, bf16[2,17,48,128]{3,2,1,0:T(8,128)(2,1)S(1)}, u32[]{:S(2)}, u32[]{:S(2)}) collective-permute-start(bf16[2,17,48,128]{3,2,1,0:T(8,128)(2,1)S(1)} %pad_maximum_fusion.4), channel_id=1, source_target_pairs={{0,16},{4,20},{8,24},{12,28},{16,0},{20,4},{24,8},{28,12},{32,48},... | collective-permute-start | bytes 1253384 | tf_op jit(solution)/shard_map/ppermute | solution.py:234
  89.5 14.6 %collective-permute-done.13 = bf16[2,16,48,128]{3,2,1,0:T(8,128)(2,1)S(1)} collective-permute-done((bf16[2,16,48,128]{3,2,1,0:T(8,128)(2,1)S(1)}, bf16[2,16,48,128]{3,2,1,0:T(8,128)(2,1)S(1)}, u32[]{:S(2)}, u32[]{:S(2)}) %collective-permute-start.13) | collective-permute-done | bytes 393248 | tf_op jit(solution)/shard_map/ppermute | solution.py:234
  108.9 3.9 %collective-permute-start.16 = (bf16[2,16,48,128]{3,2,1,0:T(8,128)(2,1)}, bf16[2,16,48,128]{3,2,1,0:T(8,128)(2,1)S(1)}, u32[]{:S(2)}, u32[]{:S(2)}) collective-permute-start(bf16[2,16,48,128]{3,2,1,0:T(8,128)(2,1)} %pad_maximum_fusion.6), channel_id=1, source_target_pairs={{0,32},{4,36},{8,40},{12,44},{16,48},{20,52},{24,56},{28,60},{32,6... | collective-permute-start | bytes 1179656 | tf_op jit(solution)/shard_map/ppermute | solution.py:230
  114.3 3.8 %collective-permute-start.19 = (bf16[2,16,48,128]{3,2,1,0:T(8,128)(2,1)S(1)}, bf16[2,16,48,128]{3,2,1,0:T(8,128)(2,1)S(1)}, u32[]{:S(2)}, u32[]{:S(2)}) collective-permute-start(bf16[2,16,48,128]{3,2,1,0:T(8,128)(2,1)S(1)} %pad_maximum_fusion.7), channel_id=1, source_target_pairs={{0,12},{4,0},{8,4},{12,8},{16,28},{20,16},{24,20},{28,24},{32,44},... | collective-permute-start | bytes 1179656 | tf_op jit(solution)/shard_map/ppermute | solution.py:226
  132.5 2.6 collective-permute-start.22
  135.9 9.0 %turn.1.refs_10_.refs_11_ = bf16[512,48,128]{2,1,0:T(8,128)(2,1)} custom-call(bf16[512,48,128]{2,1,0:T(8,128)(2,1)} %get-tuple-element.253.refs_1_.own.refs_8_.refs_9_), custom_call_target="tpu_custom_call" | custom-call | flops 1000000 | bytes 25000000 | tf_op jit(solution)/shard_map/turn/pallas_call | solution.py:101
  145.3 2.6 collective-permute-done.21.refs_5_
  150.2 2.7 %collective-permute-start.26 = (bf16[64,48,128]{2,1,0:T(8,128)(2,1)S(1)}, bf16[64,48,128]{2,1,0:T(8,128)(2,1)S(1)}, u32[]{:S(2)}, u32[]{:S(2)}) collective-permute-start(bf16[64,48,128]{2,1,0:T(8,128)(2,1)S(1)} %pad_maximum_fusion.refs_0_), channel_id=1, source_target_pairs={{0,12},{4,0},{8,4},{12,8},{16,28},{20,16},{24,20},{28,24},{32,44},... | collective-permute-start | bytes 2359304 | tf_op jit(solution)/shard_map/ppermute | solution.py:226
  152.9 2.7 %collective-permute-start.27 = (bf16[64,48,128]{2,1,0:T(8,128)(2,1)S(1)}, bf16[64,48,128]{2,1,0:T(8,128)(2,1)S(1)}, u32[]{:S(2)}, u32[]{:S(2)}) collective-permute-start(bf16[64,48,128]{2,1,0:T(8,128)(2,1)S(1)} %pad_maximum_fusion.1.refs_4_), channel_id=1, source_target_pairs={{0,96},{4,100},{8,104},{12,108},{16,112},{20,116},{24,120},{28,124... | collective-permute-start | bytes 2359304 | tf_op jit(solution)/shard_map/ppermute | solution.py:230
  156.8 9.1 %collective-permute-done.24.refs_3_ = bf16[64,48,128]{2,1,0:T(8,128)(2,1)} collective-permute-done((bf16[64,48,128]{2,1,0:T(8,128)(2,1)}, bf16[64,48,128]{2,1,0:T(8,128)(2,1)}, u32[]{:S(2)}, u32[]{:S(2)}) %collective-permute-start.24) | collective-permute-done | bytes 786464 | tf_op jit(solution)/shard_map/ppermute | solution.py:226
  166.7 2.7 %collective-permute-start.30 = (bf16[64,48,128]{2,1,0:T(8,128)(2,1)S(1)}, bf16[64,48,128]{2,1,0:T(8,128)(2,1)S(1)}, u32[]{:S(2)}, u32[]{:S(2)}) collective-permute-start(bf16[64,48,128]{2,1,0:T(8,128)(2,1)S(1)} %collective-permute-done.26.refs_2_), channel_id=1, source_target_pairs={{0,12},{4,0},{8,4},{12,8},{16,28},{20,16},{24,20},{28,24},{32,44},... | collective-permute-start | bytes 2359304 | tf_op jit(solution)/shard_map/ppermute | solution.py:226
  169.3 3.5 %collective-permute-start.31 = (bf16[64,48,128]{2,1,0:T(8,128)(2,1)S(1)}, bf16[64,48,128]{2,1,0:T(8,128)(2,1)S(1)}, u32[]{:S(2)}, u32[]{:S(2)}) collective-permute-start(bf16[64,48,128]{2,1,0:T(8,128)(2,1)S(1)} %collective-permute-done.27.refs_6_), channel_id=1, source_target_pairs={{0,96},{4,100},{8,104},{12,108},{16,112},{20,116},{24,120},{28,124... | collective-permute-start | bytes 2359304 | tf_op jit(solution)/shard_map/ppermute | solution.py:230
  172.9 19.4 %corr.2 = (bf16[512,1024]{1,0:T(8,128)(2,1)}, bf16[512,1024]{1,0:T(8,128)(2,1)}, bf16[512,1024]{1,0:T(8,128)(2,1)}, bf16[512,1024]{1,0:T(8,128)(2,1)}) custom-call(s32[8]{0:T(128)} %stack.132.place, s32[4]{0:T(128)} %pad_add_fusion.order, bf16[64,48,128]{2,1,0:T(8,128)(2,1)} %copy-done.10, bf16[64,48,128]{2,1,0:T(8,128)(2,1)} %collective-permute-done.20.refs_1_, ...), custom_call_target="tpu_custom_call" | custom-call | flops 22000001024 | bytes 40000000 | tf_op jit(solution)/shard_map/corr/pallas_call | solution.py:170
  192.4 7.5 %collective-permute-start.32 = (bf16[512,1024]{1,0:T(8,128)(2,1)}, bf16[512,1024]{1,0:T(8,128)(2,1)S(1)}, u32[]{:S(2)}, u32[]{:S(2)}) collective-permute-start(bf16[512,1024]{1,0:T(8,128)(2,1)} %get-tuple-element.236), channel_id=1, source_target_pairs={{0,1},{1,0},{2,3},{3,2},{4,5},{5,4},{6,7},{7,6},{8,9},{9,8},{10,11... | collective-permute-start | bytes 3145736 | tf_op jit(solution)/shard_map/ppermute | solution.py:338
  199.9 2.5 collective-permute-done.32
  206.0 19.4 %corr.3 = (bf16[512,1024]{1,0:T(8,128)(2,1)}, bf16[512,1024]{1,0:T(8,128)(2,1)}, bf16[512,1024]{1,0:T(8,128)(2,1)}, bf16[512,1024]{1,0:T(8,128)(2,1)}) custom-call(s32[8]{0:T(128)} %stack.132.place, s32[4]{0:T(128)} %pad_add_fusion.order, bf16[64,48,128]{2,1,0:T(8,128)(2,1)} %copy-done.11, bf16[64,48,128]{2,1,0:T(8,128)(2,1)} %copy-done.23, ...), custom_call_target="tpu_custom_call" | custom-call | flops 22000001024 | bytes 40000000 | tf_op jit(solution)/shard_map/corr/pallas_call | solution.py:170
  225.5 3.0 %collective-permute-done.33.c = bf16[512,1024]{1,0:T(8,128)(2,1)S(1)} collective-permute-done((bf16[512,1024]{1,0:T(8,128)(2,1)S(1)}, bf16[512,1024]{1,0:T(8,128)(2,1)S(1)}, u32[]{:S(2)}, u32[]{:S(2)}) %collective-permute-start.33) | collective-permute-done | bytes 1048608 | tf_op jit(solution)/shard_map/ppermute | solution.py:342
  229.7 2.5 collective-permute-done.35
  235.9 2.9 %finish.2.refs_0_ = bf16[2,1024,512]{2,1,0:T(8,128)(2,1)} custom-call(bf16[512,1024]{1,0:T(8,128)(2,1)} %get-tuple-element.269.a, bf16[512,1024]{1,0:T(8,128)(2,1)} %copy-done.1, bf16[512,1024]{1,0:T(8,128)(2,1)} %copy-done), custom_call_target="tpu_custom_call" | custom-call | tf_op jit(solution)/shard_map/finish/pallas_call | solution.py:204
  238.8 19.5 %collective-permute-done.36.c = bf16[512,1024]{1,0:T(8,128)(2,1)S(1)} collective-permute-done((bf16[512,1024]{1,0:T(8,128)(2,1)S(1)}, bf16[512,1024]{1,0:T(8,128)(2,1)S(1)}, u32[]{:S(2)}, u32[]{:S(2)}) %collective-permute-start.36) | collective-permute-done | bytes 1048608 | tf_op jit(solution)/shard_map/ppermute | solution.py:342
  260.3 2.9 %finish.3 = bf16[2,1024,512]{2,1,0:T(8,128)(2,1)} custom-call(bf16[512,1024]{1,0:T(8,128)(2,1)} %get-tuple-element.260.a, bf16[512,1024]{1,0:T(8,128)(2,1)} %copy-done.3, bf16[512,1024]{1,0:T(8,128)(2,1)} %copy-done.2, bf16[2,1024,512]{2,1,0:T(8,128)(2,1)} %finish.2.refs_0_), custom_call_target="tpu_custom_call", output_to_operand_aliasing={{}: (3, {})} | custom-call | tf_op jit(solution)/shard_map/finish/pallas_call | solution.py:204
  (140 shorter events, 51.7 us)
Async XLA Ops:
  12.4 21.9 %collective-permute-start.1 = (bf16[64,48,128]{2,1,0:T(8,128)(2,1)}, bf16[64,48,128]{2,1,0:T(8,128)(2,1)S(1)}, u32[]{:S(2)}, u32[]{:S(2)}) collective-permute-start(bf16[64,48,128]{2,1,0:T(8,128)(2,1)} %get-tuple-element.148), channel_id=1, source_target_pairs={{0,64},{4,68},{8,72},{12,76},{16,80},{20,84},{24,88},{28,92},{32,9... | collective-permute-start | bytes 2359304 | tf_op jit(solution)/shard_map/ppermute | solution.py:230
  16.8 35.9 %collective-permute-start = (bf16[65,48,128]{2,1,0:T(8,128)(2,1)}, bf16[65,48,128]{2,1,0:T(8,128)(2,1)S(1)}, u32[]{:S(2)}, u32[]{:S(2)}) collective-permute-start(bf16[65,48,128]{2,1,0:T(8,128)(2,1)} %get-tuple-element.147.refs_2_), channel_id=1, source_target_pairs={{0,8},{4,12},{8,0},{12,4},{16,24},{20,28},{24,16},{28,20},{32,40},... | collective-permute-start | bytes 2396168 | tf_op jit(solution)/shard_map/ppermute | solution.py:226
  19.5 35.8 %collective-permute-start.2 = (bf16[65,48,128]{2,1,0:T(8,128)(2,1)}, bf16[65,48,128]{2,1,0:T(8,128)(2,1)S(1)}, u32[]{:S(2)}, u32[]{:S(2)}) collective-permute-start(bf16[65,48,128]{2,1,0:T(8,128)(2,1)} %get-tuple-element.149), channel_id=1, source_target_pairs={{0,4},{4,8},{8,12},{12,0},{16,20},{20,24},{24,28},{28,16},{32,36},... | collective-permute-start | bytes 2396168 | tf_op jit(solution)/shard_map/ppermute | solution.py:226
  19.9 35.5 %collective-permute-start.4 = (bf16[65,48,128]{2,1,0:T(8,128)(2,1)}, bf16[65,48,128]{2,1,0:T(8,128)(2,1)S(1)}, u32[]{:S(2)}, u32[]{:S(2)}) collective-permute-start(bf16[65,48,128]{2,1,0:T(8,128)(2,1)} %get-tuple-element.151), channel_id=1, source_target_pairs={{0,12},{4,0},{8,4},{12,8},{16,28},{20,16},{24,20},{28,24},{32,44},... | collective-permute-start | bytes 2396168 | tf_op jit(solution)/shard_map/ppermute | solution.py:226
  22.2 29.7 %collective-permute-start.3 = (bf16[64,48,128]{2,1,0:T(8,128)(2,1)}, bf16[64,48,128]{2,1,0:T(8,128)(2,1)}, u32[]{:S(2)}, u32[]{:S(2)}) collective-permute-start(bf16[64,48,128]{2,1,0:T(8,128)(2,1)} %get-tuple-element.150), channel_id=1, source_target_pairs={{0,32},{4,36},{8,40},{12,44},{16,48},{20,52},{24,56},{28,60},{32,6... | collective-permute-start | bytes 2359304 | tf_op jit(solution)/shard_map/ppermute | solution.py:230
  34.3 18.4 %collective-permute-start.5 = (bf16[64,48,128]{2,1,0:T(8,128)(2,1)}, bf16[64,48,128]{2,1,0:T(8,128)(2,1)}, u32[]{:S(2)}, u32[]{:S(2)}) collective-permute-start(bf16[64,48,128]{2,1,0:T(8,128)(2,1)} %get-tuple-element.152), channel_id=1, source_target_pairs={{0,96},{4,100},{8,104},{12,108},{16,112},{20,116},{24,120},{28,124... | collective-permute-start | bytes 2359304 | tf_op jit(solution)/shard_map/ppermute | solution.py:230
  62.3 21.3 %collective-permute-start.6 = (bf16[2,17,48,128]{3,2,1,0:T(8,128)(2,1)}, bf16[2,17,48,128]{3,2,1,0:T(8,128)(2,1)S(1)}, u32[]{:S(2)}, u32[]{:S(2)}) collective-permute-start(bf16[2,17,48,128]{3,2,1,0:T(8,128)(2,1)} %get-tuple-element.165), channel_id=1, source_target_pairs={{0,32},{4,36},{8,40},{12,44},{16,48},{20,52},{24,56},{28,60},{32,6... | collective-permute-start | bytes 1253384 | tf_op jit(solution)/shard_map/ppermute | solution.py:230
  63.1 20.6 %collective-permute-start.7 = (bf16[2,17,48,128]{3,2,1,0:T(8,128)(2,1)}, bf16[2,17,48,128]{3,2,1,0:T(8,128)(2,1)S(1)}, u32[]{:S(2)}, u32[]{:S(2)}) collective-permute-start(bf16[2,17,48,128]{3,2,1,0:T(8,128)(2,1)} %get-tuple-element.166), channel_id=1, source_target_pairs={{0,64},{4,68},{8,72},{12,76},{16,80},{20,84},{24,88},{28,92},{32,9... | collective-permute-start | bytes 1253384 | tf_op jit(solution)/shard_map/ppermute | solution.py:230
  66.2 17.7 %collective-permute-start.8 = (bf16[2,17,48,128]{3,2,1,0:T(8,128)(2,1)}, bf16[2,17,48,128]{3,2,1,0:T(8,128)(2,1)S(1)}, u32[]{:S(2)}, u32[]{:S(2)}) collective-permute-start(bf16[2,17,48,128]{3,2,1,0:T(8,128)(2,1)} %get-tuple-element.167), channel_id=1, source_target_pairs={{0,96},{4,100},{8,104},{12,108},{16,112},{20,116},{24,120},{28,124... | collective-permute-start | bytes 1253384 | tf_op jit(solution)/shard_map/ppermute | solution.py:230
  66.2 15.3 %collective-permute-start.11 = (bf16[2,16,48,128]{3,2,1,0:T(8,128)(2,1)}, bf16[2,16,48,128]{3,2,1,0:T(8,128)(2,1)S(1)}, u32[]{:S(2)}, u32[]{:S(2)}) collective-permute-start(bf16[2,16,48,128]{3,2,1,0:T(8,128)(2,1)} %get-tuple-element.170), channel_id=1, source_target_pairs={{0,12},{4,0},{8,4},{12,8},{16,28},{20,16},{24,20},{28,24},{32,44},... | collective-permute-start | bytes 1179656 | tf_op jit(solution)/shard_map/ppermute | solution.py:226
  85.2 18.9 %collective-permute-start.12 = (bf16[2,17,48,128]{3,2,1,0:T(8,128)(2,1)S(1)}, bf16[2,17,48,128]{3,2,1,0:T(8,128)(2,1)S(1)}, u32[]{:S(2)}, u32[]{:S(2)}) collective-permute-start(bf16[2,17,48,128]{3,2,1,0:T(8,128)(2,1)S(1)} %pad_maximum_fusion.4), channel_id=1, source_target_pairs={{0,16},{4,20},{8,24},{12,28},{16,0},{20,4},{24,8},{28,12},{32,48},... | collective-permute-start | bytes 1253384 | tf_op jit(solution)/shard_map/ppermute | solution.py:234
  88.2 15.9 %collective-permute-start.13 = (bf16[2,16,48,128]{3,2,1,0:T(8,128)(2,1)S(1)}, bf16[2,16,48,128]{3,2,1,0:T(8,128)(2,1)S(1)}, u32[]{:S(2)}, u32[]{:S(2)}) collective-permute-start(bf16[2,16,48,128]{3,2,1,0:T(8,128)(2,1)S(1)} %pad_maximum_fusion.5), channel_id=1, source_target_pairs={{0,16},{4,20},{8,24},{12,28},{16,0},{20,4},{24,8},{28,12},{32,48},... | collective-permute-start | bytes 1179656 | tf_op jit(solution)/shard_map/ppermute | solution.py:234
  107.4 19.7 %collective-permute-start.15 = (bf16[2,16,48,128]{3,2,1,0:T(8,128)(2,1)S(1)}, bf16[2,16,48,128]{3,2,1,0:T(8,128)(2,1)S(1)}, u32[]{:S(2)}, u32[]{:S(2)}) collective-permute-start(bf16[2,16,48,128]{3,2,1,0:T(8,128)(2,1)S(1)} %pad_maximum_fusion.7), channel_id=1, source_target_pairs={{0,8},{4,12},{8,0},{12,4},{16,24},{20,28},{24,16},{28,20},{32,40},... | collective-permute-start | bytes 1179656 | tf_op jit(solution)/shard_map/ppermute | solution.py:226
  108.9 18.3 %collective-permute-start.16 = (bf16[2,16,48,128]{3,2,1,0:T(8,128)(2,1)}, bf16[2,16,48,128]{3,2,1,0:T(8,128)(2,1)S(1)}, u32[]{:S(2)}, u32[]{:S(2)}) collective-permute-start(bf16[2,16,48,128]{3,2,1,0:T(8,128)(2,1)} %pad_maximum_fusion.6), channel_id=1, source_target_pairs={{0,32},{4,36},{8,40},{12,44},{16,48},{20,52},{24,56},{28,60},{32,6... | collective-permute-start | bytes 1179656 | tf_op jit(solution)/shard_map/ppermute | solution.py:230
  112.7 14.8 %collective-permute-start.17 = (bf16[2,16,48,128]{3,2,1,0:T(8,128)(2,1)S(1)}, bf16[2,16,48,128]{3,2,1,0:T(8,128)(2,1)S(1)}, u32[]{:S(2)}, u32[]{:S(2)}) collective-permute-start(bf16[2,16,48,128]{3,2,1,0:T(8,128)(2,1)S(1)} %pad_maximum_fusion.7), channel_id=1, source_target_pairs={{0,4},{4,8},{8,12},{12,0},{16,20},{20,24},{24,28},{28,16},{32,36},... | collective-permute-start | bytes 1179656 | tf_op jit(solution)/shard_map/ppermute | solution.py:226
  113.7 14.4 %collective-permute-start.18 = (bf16[2,16,48,128]{3,2,1,0:T(8,128)(2,1)}, bf16[2,16,48,128]{3,2,1,0:T(8,128)(2,1)S(1)}, u32[]{:S(2)}, u32[]{:S(2)}) collective-permute-start(bf16[2,16,48,128]{3,2,1,0:T(8,128)(2,1)} %pad_maximum_fusion.6), channel_id=1, source_target_pairs={{0,96},{4,100},{8,104},{12,108},{16,112},{20,116},{24,120},{28,124... | collective-permute-start | bytes 1179656 | tf_op jit(solution)/shard_map/ppermute | solution.py:230
  114.3 13.8 %collective-permute-start.19 = (bf16[2,16,48,128]{3,2,1,0:T(8,128)(2,1)S(1)}, bf16[2,16,48,128]{3,2,1,0:T(8,128)(2,1)S(1)}, u32[]{:S(2)}, u32[]{:S(2)}) collective-permute-start(bf16[2,16,48,128]{3,2,1,0:T(8,128)(2,1)S(1)} %pad_maximum_fusion.7), channel_id=1, source_target_pairs={{0,12},{4,0},{8,4},{12,8},{16,28},{20,16},{24,20},{28,24},{32,44},... | collective-permute-start | bytes 1179656 | tf_op jit(solution)/shard_map/ppermute | solution.py:226
  128.7 16.6 %collective-permute-start.20 = (bf16[64,48,128]{2,1,0:T(8,128)(2,1)S(1)}, bf16[64,48,128]{2,1,0:T(8,128)(2,1)}, u32[]{:S(2)}, u32[]{:S(2)}) collective-permute-start(bf16[64,48,128]{2,1,0:T(8,128)(2,1)S(1)} %pad_maximum_fusion.2.refs_0_), channel_id=1, source_target_pairs={{0,4},{4,8},{8,12},{12,0},{16,20},{20,24},{24,28},{28,16},{32,36},... | collective-permute-start | bytes 2359304 | tf_op jit(solution)/shard_map/ppermute | solution.py:226
  130.5 17.4 %collective-permute-start.21 = (bf16[64,48,128]{2,1,0:T(8,128)(2,1)S(1)}, bf16[64,48,128]{2,1,0:T(8,128)(2,1)}, u32[]{:S(2)}, u32[]{:S(2)}) collective-permute-start(bf16[64,48,128]{2,1,0:T(8,128)(2,1)S(1)} %pad_maximum_fusion.3.refs_4_), channel_id=1, source_target_pairs={{0,32},{4,36},{8,40},{12,44},{16,48},{20,52},{24,56},{28,60},{32,6... | collective-permute-start | bytes 2359304 | tf_op jit(solution)/shard_map/ppermute | solution.py:230
  132.5 15.6 %collective-permute-start.22 = (bf16[64,48,128]{2,1,0:T(8,128)(2,1)S(1)}, bf16[64,48,128]{2,1,0:T(8,128)(2,1)S(1)}, u32[]{:S(2)}, u32[]{:S(2)}) collective-permute-start(bf16[64,48,128]{2,1,0:T(8,128)(2,1)S(1)} %pad_maximum_fusion.2.refs_0_), channel_id=1, source_target_pairs={{0,12},{4,0},{8,4},{12,8},{16,28},{20,16},{24,20},{28,24},{32,44},... | collective-permute-start | bytes 2359304 | tf_op jit(solution)/shard_map/ppermute | solution.py:226
  135.1 15.1 %collective-permute-start.23 = (bf16[64,48,128]{2,1,0:T(8,128)(2,1)S(1)}, bf16[64,48,128]{2,1,0:T(8,128)(2,1)S(1)}, u32[]{:S(2)}, u32[]{:S(2)}) collective-permute-start(bf16[64,48,128]{2,1,0:T(8,128)(2,1)S(1)} %pad_maximum_fusion.3.refs_4_), channel_id=1, source_target_pairs={{0,96},{4,100},{8,104},{12,108},{16,112},{20,116},{24,120},{28,124... | collective-permute-start | bytes 2359304 | tf_op jit(solution)/shard_map/ppermute | solution.py:230
  150.2 15.7 %collective-permute-start.24 = (bf16[64,48,128]{2,1,0:T(8,128)(2,1)}, bf16[64,48,128]{2,1,0:T(8,128)(2,1)}, u32[]{:S(2)}, u32[]{:S(2)}) collective-permute-start(bf16[64,48,128]{2,1,0:T(8,128)(2,1)} %collective-permute-done.20.refs_1_), channel_id=1, source_target_pairs={{0,4},{4,8},{8,12},{12,0},{16,20},{20,24},{24,28},{28,16},{32,36},... | collective-permute-start | bytes 2359304 | tf_op jit(solution)/shard_map/ppermute | solution.py:226
  150.2 15.7 %collective-permute-start.25 = (bf16[64,48,128]{2,1,0:T(8,128)(2,1)}, bf16[64,48,128]{2,1,0:T(8,128)(2,1)}, u32[]{:S(2)}, u32[]{:S(2)}) collective-permute-start(bf16[64,48,128]{2,1,0:T(8,128)(2,1)} %collective-permute-done.21.refs_5_), channel_id=1, source_target_pairs={{0,32},{4,36},{8,40},{12,44},{16,48},{20,52},{24,56},{28,60},{32,6... | collective-permute-start | bytes 2359304 | tf_op jit(solution)/shard_map/ppermute | solution.py:230
  150.2 15.7 %collective-permute-start.26 = (bf16[64,48,128]{2,1,0:T(8,128)(2,1)S(1)}, bf16[64,48,128]{2,1,0:T(8,128)(2,1)S(1)}, u32[]{:S(2)}, u32[]{:S(2)}) collective-permute-start(bf16[64,48,128]{2,1,0:T(8,128)(2,1)S(1)} %pad_maximum_fusion.refs_0_), channel_id=1, source_target_pairs={{0,12},{4,0},{8,4},{12,8},{16,28},{20,16},{24,20},{28,24},{32,44},... | collective-permute-start | bytes 2359304 | tf_op jit(solution)/shard_map/ppermute | solution.py:226
  166.7 25.7 %collective-permute-start.28 = (bf16[64,48,128]{2,1,0:T(8,128)(2,1)S(1)}, bf16[64,48,128]{2,1,0:T(8,128)(2,1)S(1)}, u32[]{:S(2)}, u32[]{:S(2)}) collective-permute-start(bf16[64,48,128]{2,1,0:T(8,128)(2,1)S(1)} %pad_maximum_fusion.refs_0_), channel_id=1, source_target_pairs={{0,4},{4,8},{8,12},{12,0},{16,20},{20,24},{24,28},{28,16},{32,36},... | collective-permute-start | bytes 2359304 | tf_op jit(solution)/shard_map/ppermute | solution.py:226
  166.7 25.7 %collective-permute-start.29 = (bf16[64,48,128]{2,1,0:T(8,128)(2,1)S(1)}, bf16[64,48,128]{2,1,0:T(8,128)(2,1)S(1)}, u32[]{:S(2)}, u32[]{:S(2)}) collective-permute-start(bf16[64,48,128]{2,1,0:T(8,128)(2,1)S(1)} %pad_maximum_fusion.1.refs_4_), channel_id=1, source_target_pairs={{0,32},{4,36},{8,40},{12,44},{16,48},{20,52},{24,56},{28,60},{32,6... | collective-permute-start | bytes 2359304 | tf_op jit(solution)/shard_map/ppermute | solution.py:230
  166.7 25.7 %collective-permute-start.30 = (bf16[64,48,128]{2,1,0:T(8,128)(2,1)S(1)}, bf16[64,48,128]{2,1,0:T(8,128)(2,1)S(1)}, u32[]{:S(2)}, u32[]{:S(2)}) collective-permute-start(bf16[64,48,128]{2,1,0:T(8,128)(2,1)S(1)} %collective-permute-done.26.refs_2_), channel_id=1, source_target_pairs={{0,12},{4,0},{8,4},{12,8},{16,28},{20,16},{24,20},{28,24},{32,44},... | collective-permute-start | bytes 2359304 | tf_op jit(solution)/shard_map/ppermute | solution.py:226
  169.3 23.1 %collective-permute-start.31 = (bf16[64,48,128]{2,1,0:T(8,128)(2,1)S(1)}, bf16[64,48,128]{2,1,0:T(8,128)(2,1)S(1)}, u32[]{:S(2)}, u32[]{:S(2)}) collective-permute-start(bf16[64,48,128]{2,1,0:T(8,128)(2,1)S(1)} %collective-permute-done.27.refs_6_), channel_id=1, source_target_pairs={{0,96},{4,100},{8,104},{12,108},{16,112},{20,116},{24,120},{28,124... | collective-permute-start | bytes 2359304 | tf_op jit(solution)/shard_map/ppermute | solution.py:230
  204.0 24.5 %collective-permute-start.33 = (bf16[512,1024]{1,0:T(8,128)(2,1)S(1)}, bf16[512,1024]{1,0:T(8,128)(2,1)S(1)}, u32[]{:S(2)}, u32[]{:S(2)}) collective-permute-start(bf16[512,1024]{1,0:T(8,128)(2,1)S(1)} %add_convert_fusion.1), channel_id=1, source_target_pairs={{0,2},{1,3},{2,0},{3,1},{4,6},{5,7},{6,4},{7,5},{8,10},{9,11},{10,... | collective-permute-start | bytes 3145736 | tf_op jit(solution)/shard_map/ppermute | solution.py:342
  205.4 23.1 %collective-permute-start.34 = (bf16[512,1024]{1,0:T(8,128)(2,1)S(1)}, bf16[512,1024]{1,0:T(8,128)(2,1)S(1)}, u32[]{:S(2)}, u32[]{:S(2)}) collective-permute-start(bf16[512,1024]{1,0:T(8,128)(2,1)S(1)} %copy-done.17), channel_id=1, source_target_pairs={{0,1},{1,0},{2,3},{3,2},{4,5},{5,4},{6,7},{7,6},{8,9},{9,8},{10,11... | collective-permute-start | bytes 3145736 | tf_op jit(solution)/shard_map/ppermute | solution.py:338
  233.9 24.5 %collective-permute-start.36 = (bf16[512,1024]{1,0:T(8,128)(2,1)S(1)}, bf16[512,1024]{1,0:T(8,128)(2,1)S(1)}, u32[]{:S(2)}, u32[]{:S(2)}) collective-permute-start(bf16[512,1024]{1,0:T(8,128)(2,1)S(1)} %add_convert_fusion), channel_id=1, source_target_pairs={{0,2},{1,3},{2,0},{3,1},{4,6},{5,7},{6,4},{7,5},{8,10},{9,11},{10,... | collective-permute-start | bytes 3145736 | tf_op jit(solution)/shard_map/ppermute | solution.py:342
  235.2 23.1 %collective-permute-start.37 = (bf16[512,1024]{1,0:T(8,128)(2,1)S(1)}, bf16[512,1024]{1,0:T(8,128)(2,1)S(1)}, u32[]{:S(2)}, u32[]{:S(2)}) collective-permute-start(bf16[512,1024]{1,0:T(8,128)(2,1)S(1)} %copy-done.18), channel_id=1, source_target_pairs={{0,1},{1,0},{2,3},{3,2},{4,5},{5,4},{6,7},{7,6},{8,9},{9,8},{10,11... | collective-permute-start | bytes 3145736 | tf_op jit(solution)/shard_map/ppermute | solution.py:338
  (33 other events, 450.1 us)

commit v6 on v5

--- a/solution.py
+++ b/solution.py
@@ -199,7 +199,7 @@
 
 
 def finish(step, near, near_got, far_sum, base=None):
-    cols = 512
+    cols = 256
     extra = [] if base is None else [base]
     return pl.pallas_call(
         finish_kernel,

time: 264 us -> 265 us (level)
  transfers between devices with their start and end apart: 38 -> 38, of which waited for: 21 -> 21; matrix products, arithmetic and copies ran while one was open for 4% -> 4% of each run, Pallas kernels for 19% -> 20%
where the time goes in v6:
time: 265 us; the launch traced here: 264 us
  waiting for transfers between devices  99.1 us (37%)
  Pallas kernels  72.3 us (27%)
  starting transfers between devices  67.4 us (25%)
  local copies, waits for them, and re-layouts  12.1 us (5%)
  other arithmetic  9.48 us (4%)
  between operations  4.02 us (2%)
    pallas_call x2, Pallas kernels, corr(): pl.pallas_call(corr_kernel, grid_spec=pltpu.PrefetchScalarGridSpec(num_sc...  38.8 us
    ppermute x15, waiting for transfers between devices, along_z(): lax.ppermute(a, 'station', [(s, (s + 8 * d) % 32) for s in range(32)])  30.3 us
    ppermute x15, waiting for transfers between devices, along_x(): lax.ppermute(a, 'station', [(s, s - s % 4 + (s + d) % 4) for s in range(3...  27.8 us
    ppermute x15, starting transfers between devices, along_z(): lax.ppermute(a, 'station', [(s, (s + 8 * d) % 32) for s in range(32)])  26.9 us
    ppermute x15, starting transfers between devices, along_x(): lax.ppermute(a, 'station', [(s, s - s % 4 + (s + d) % 4) for s in range(3...  24.6 us
    ppermute x2, waiting for transfers between devices, other_chip(): return lax.ppermute(a, 'tm', [(t, t ^ 2) for t in range(4)])  21.4 us
    ppermute x2, waiting for transfers between devices, swap_y(): return lax.ppermute(a, 'station', [(s, s ^ 4) for s in range(32)])  14.7 us
    pallas_call x1, Pallas kernels, whiten(): pl.pallas_call(whiten_kernel, grid_spec=pltpu.PrefetchScalarGridSpec(num_...  11.7 us
  transfers between devices with their start and end apart: 38, of which 21 were waited for; matrix products, arithmetic and copies ran while one was open for 4% of the time, Pallas kernels for 20%

profile of v6, /device:TPU:1, one launch (start us, length us, event | category | flops | bytes accessed | tf_op | source)
XLA Modules:
  0.0 264.4 jit_solution(10851048988797493891)
XLA Ops:
  0.6 11.7 %whiten.1 = (bf16[512,48,128]{2,1,0:T(8,128)(2,1)}, bf16[65,48,128]{2,1,0:T(8,128)(2,1)}, bf16[64,48,128]{2,1,0:T(8,128)(2,1)}, bf16[65,48,128]{2,1,0:T(8,128)(2...) custom-call(s32[6]{0:T(128)} %stack.126.place, ...), custom_call_target="tpu_custom_call" | custom-call | flops 100000000 | bytes 18000000 | tf_op jit(solution)/shard_map/whiten/pallas_call | solution.py:40
  12.4 4.4 %collective-permute-start.1 = (bf16[64,48,128]{2,1,0:T(8,128)(2,1)}, bf16[64,48,128]{2,1,0:T(8,128)(2,1)S(1)}, u32[]{:S(2)}, u32[]{:S(2)}) collective-permute-start(bf16[64,48,128]{2,1,0:T(8,128)(2,1)} %get-tuple-element.148), channel_id=1, source_target_pairs={{0,64},{4,68},{8,72},{12,76},{16,80},{20,84},{24,88},{28,92},{32,9... | collective-permute-start | bytes 2359304 | tf_op jit(solution)/shard_map/ppermute | solution.py:230
  16.8 2.7 %collective-permute-start = (bf16[65,48,128]{2,1,0:T(8,128)(2,1)}, bf16[65,48,128]{2,1,0:T(8,128)(2,1)S(1)}, u32[]{:S(2)}, u32[]{:S(2)}) collective-permute-start(bf16[65,48,128]{2,1,0:T(8,128)(2,1)} %get-tuple-element.147.refs_2_), channel_id=1, source_target_pairs={{0,8},{4,12},{8,0},{12,4},{16,24},{20,28},{24,16},{28,20},{32,40},... | collective-permute-start | bytes 2396168 | tf_op jit(solution)/shard_map/ppermute | solution.py:226
  23.0 11.4 %collective-permute-done.1.refs_7_ = bf16[64,48,128]{2,1,0:T(8,128)(2,1)S(1)} collective-permute-done((bf16[64,48,128]{2,1,0:T(8,128)(2,1)}, bf16[64,48,128]{2,1,0:T(8,128)(2,1)S(1)}, u32[]{:S(2)}, u32[]{:S(2)}) %collective-permute-start.1) | collective-permute-done | bytes 786464 | tf_op jit(solution)/shard_map/ppermute | solution.py:230
  34.3 2.8 %collective-permute-start.5 = (bf16[64,48,128]{2,1,0:T(8,128)(2,1)}, bf16[64,48,128]{2,1,0:T(8,128)(2,1)}, u32[]{:S(2)}, u32[]{:S(2)}) collective-permute-start(bf16[64,48,128]{2,1,0:T(8,128)(2,1)} %get-tuple-element.152), channel_id=1, source_target_pairs={{0,96},{4,100},{8,104},{12,108},{16,112},{20,116},{24,120},{28,124... | collective-permute-start | bytes 2359304 | tf_op jit(solution)/shard_map/ppermute | solution.py:230
  40.8 11.2 %collective-permute-done.3.refs_6_ = bf16[64,48,128]{2,1,0:T(8,128)(2,1)} collective-permute-done((bf16[64,48,128]{2,1,0:T(8,128)(2,1)}, bf16[64,48,128]{2,1,0:T(8,128)(2,1)}, u32[]{:S(2)}, u32[]{:S(2)}) %collective-permute-start.3) | collective-permute-done | bytes 786464 | tf_op jit(solution)/shard_map/ppermute | solution.py:230
  52.7 2.7 %collective-permute-done.2.refs_3_ = bf16[65,48,128]{2,1,0:T(8,128)(2,1)S(1)} collective-permute-done((bf16[65,48,128]{2,1,0:T(8,128)(2,1)}, bf16[65,48,128]{2,1,0:T(8,128)(2,1)S(1)}, u32[]{:S(2)}, u32[]{:S(2)}) %collective-permute-start.2) | collective-permute-done | bytes 798752 | tf_op jit(solution)/shard_map/ppermute | solution.py:226
  56.5 4.6 %choose.1 = (bf16[2,17,48,128]{3,2,1,0:T(8,128)(2,1)}, bf16[2,17,48,128]{3,2,1,0:T(8,128)(2,1)}, bf16[2,17,48,128]{3,2,1,0:T(8,128)(2,1)}, bf16[2,17,48,128]{3,2...) custom-call(s32[14]{0:T(128)} %stack.122.refs_0_, ...), custom_call_target="tpu_custom_call" | custom-call | flops 1000000 | bytes 6000000 | tf_op jit(solution)/shard_map/choose/pallas_call | solution.py:78
  63.1 3.1 %collective-permute-start.7 = (bf16[2,17,48,128]{3,2,1,0:T(8,128)(2,1)}, bf16[2,17,48,128]{3,2,1,0:T(8,128)(2,1)S(1)}, u32[]{:S(2)}, u32[]{:S(2)}) collective-permute-start(bf16[2,17,48,128]{3,2,1,0:T(8,128)(2,1)} %get-tuple-element.166), channel_id=1, source_target_pairs={{0,64},{4,68},{8,72},{12,76},{16,80},{20,84},{24,88},{28,92},{32,9... | collective-permute-start | bytes 1253384 | tf_op jit(solution)/shard_map/ppermute | solution.py:230
  67.7 5.4 %collective-permute-done.10 = bf16[2,16,48,128]{3,2,1,0:T(8,128)(2,1)S(1)} collective-permute-done((bf16[2,16,48,128]{3,2,1,0:T(8,128)(2,1)}, bf16[2,16,48,128]{3,2,1,0:T(8,128)(2,1)S(1)}, u32[]{:S(2)}, u32[]{:S(2)}) %collective-permute-start.10) | collective-permute-done | bytes 393248 | tf_op jit(solution)/shard_map/ppermute | solution.py:226
  73.8 7.7 %collective-permute-done.11 = bf16[2,16,48,128]{3,2,1,0:T(8,128)(2,1)S(1)} collective-permute-done((bf16[2,16,48,128]{3,2,1,0:T(8,128)(2,1)}, bf16[2,16,48,128]{3,2,1,0:T(8,128)(2,1)S(1)}, u32[]{:S(2)}, u32[]{:S(2)}) %collective-permute-start.11) | collective-permute-done | bytes 393248 | tf_op jit(solution)/shard_map/ppermute | solution.py:226
  85.3 3.0 %collective-permute-start.12 = (bf16[2,17,48,128]{3,2,1,0:T(8,128)(2,1)S(1)}, bf16[2,17,48,128]{3,2,1,0:T(8,128)(2,1)S(1)}, u32[]{:S(2)}, u32[]{:S(2)}) collective-permute-start(bf16[2,17,48,128]{3,2,1,0:T(8,128)(2,1)S(1)} %pad_maximum_fusion.4), channel_id=1, source_target_pairs={{0,16},{4,20},{8,24},{12,28},{16,0},{20,4},{24,8},{28,12},{32,48},... | collective-permute-start | bytes 1253384 | tf_op jit(solution)/shard_map/ppermute | solution.py:234
  89.6 14.7 %collective-permute-done.13 = bf16[2,16,48,128]{3,2,1,0:T(8,128)(2,1)S(1)} collective-permute-done((bf16[2,16,48,128]{3,2,1,0:T(8,128)(2,1)S(1)}, bf16[2,16,48,128]{3,2,1,0:T(8,128)(2,1)S(1)}, u32[]{:S(2)}, u32[]{:S(2)}) %collective-permute-start.13) | collective-permute-done | bytes 393248 | tf_op jit(solution)/shard_map/ppermute | solution.py:234
  108.9 3.9 %collective-permute-start.16 = (bf16[2,16,48,128]{3,2,1,0:T(8,128)(2,1)}, bf16[2,16,48,128]{3,2,1,0:T(8,128)(2,1)S(1)}, u32[]{:S(2)}, u32[]{:S(2)}) collective-permute-start(bf16[2,16,48,128]{3,2,1,0:T(8,128)(2,1)} %pad_maximum_fusion.6), channel_id=1, source_target_pairs={{0,32},{4,36},{8,40},{12,44},{16,48},{20,52},{24,56},{28,60},{32,6... | collective-permute-start | bytes 1179656 | tf_op jit(solution)/shard_map/ppermute | solution.py:230
  114.4 3.8 %collective-permute-start.19 = (bf16[2,16,48,128]{3,2,1,0:T(8,128)(2,1)S(1)}, bf16[2,16,48,128]{3,2,1,0:T(8,128)(2,1)S(1)}, u32[]{:S(2)}, u32[]{:S(2)}) collective-permute-start(bf16[2,16,48,128]{3,2,1,0:T(8,128)(2,1)S(1)} %pad_maximum_fusion.7), channel_id=1, source_target_pairs={{0,12},{4,0},{8,4},{12,8},{16,28},{20,16},{24,20},{28,24},{32,44},... | collective-permute-start | bytes 1179656 | tf_op jit(solution)/shard_map/ppermute | solution.py:226
  132.5 2.6 collective-permute-start.22
  135.9 9.0 %turn.1.refs_10_.refs_11_ = bf16[512,48,128]{2,1,0:T(8,128)(2,1)} custom-call(bf16[512,48,128]{2,1,0:T(8,128)(2,1)} %get-tuple-element.253.refs_1_.own.refs_8_.refs_9_), custom_call_target="tpu_custom_call" | custom-call | flops 1000000 | bytes 25000000 | tf_op jit(solution)/shard_map/turn/pallas_call | solution.py:101
  145.3 2.6 collective-permute-done.21.refs_5_
  150.2 2.7 %collective-permute-start.26 = (bf16[64,48,128]{2,1,0:T(8,128)(2,1)S(1)}, bf16[64,48,128]{2,1,0:T(8,128)(2,1)S(1)}, u32[]{:S(2)}, u32[]{:S(2)}) collective-permute-start(bf16[64,48,128]{2,1,0:T(8,128)(2,1)S(1)} %pad_maximum_fusion.refs_0_), channel_id=1, source_target_pairs={{0,12},{4,0},{8,4},{12,8},{16,28},{20,16},{24,20},{28,24},{32,44},... | collective-permute-start | bytes 2359304 | tf_op jit(solution)/shard_map/ppermute | solution.py:226
  152.9 2.7 %collective-permute-start.27 = (bf16[64,48,128]{2,1,0:T(8,128)(2,1)S(1)}, bf16[64,48,128]{2,1,0:T(8,128)(2,1)S(1)}, u32[]{:S(2)}, u32[]{:S(2)}) collective-permute-start(bf16[64,48,128]{2,1,0:T(8,128)(2,1)S(1)} %pad_maximum_fusion.1.refs_4_), channel_id=1, source_target_pairs={{0,96},{4,100},{8,104},{12,108},{16,112},{20,116},{24,120},{28,124... | collective-permute-start | bytes 2359304 | tf_op jit(solution)/shard_map/ppermute | solution.py:230
  156.8 9.1 %collective-permute-done.24.refs_3_ = bf16[64,48,128]{2,1,0:T(8,128)(2,1)} collective-permute-done((bf16[64,48,128]{2,1,0:T(8,128)(2,1)}, bf16[64,48,128]{2,1,0:T(8,128)(2,1)}, u32[]{:S(2)}, u32[]{:S(2)}) %collective-permute-start.24) | collective-permute-done | bytes 786464 | tf_op jit(solution)/shard_map/ppermute | solution.py:226
  166.7 2.7 %collective-permute-start.30 = (bf16[64,48,128]{2,1,0:T(8,128)(2,1)S(1)}, bf16[64,48,128]{2,1,0:T(8,128)(2,1)S(1)}, u32[]{:S(2)}, u32[]{:S(2)}) collective-permute-start(bf16[64,48,128]{2,1,0:T(8,128)(2,1)S(1)} %collective-permute-done.26.refs_2_), channel_id=1, source_target_pairs={{0,12},{4,0},{8,4},{12,8},{16,28},{20,16},{24,20},{28,24},{32,44},... | collective-permute-start | bytes 2359304 | tf_op jit(solution)/shard_map/ppermute | solution.py:226
  169.4 3.5 %collective-permute-start.31 = (bf16[64,48,128]{2,1,0:T(8,128)(2,1)S(1)}, bf16[64,48,128]{2,1,0:T(8,128)(2,1)S(1)}, u32[]{:S(2)}, u32[]{:S(2)}) collective-permute-start(bf16[64,48,128]{2,1,0:T(8,128)(2,1)S(1)} %collective-permute-done.27.refs_6_), channel_id=1, source_target_pairs={{0,96},{4,100},{8,104},{12,108},{16,112},{20,116},{24,120},{28,124... | collective-permute-start | bytes 2359304 | tf_op jit(solution)/shard_map/ppermute | solution.py:230
  172.9 19.4 %corr.2 = (bf16[512,1024]{1,0:T(8,128)(2,1)}, bf16[512,1024]{1,0:T(8,128)(2,1)}, bf16[512,1024]{1,0:T(8,128)(2,1)}, bf16[512,1024]{1,0:T(8,128)(2,1)}) custom-call(s32[8]{0:T(128)} %stack.132.place, s32[4]{0:T(128)} %pad_add_fusion.order, bf16[64,48,128]{2,1,0:T(8,128)(2,1)} %copy-done.10, bf16[64,48,128]{2,1,0:T(8,128)(2,1)} %collective-permute-done.20.refs_1_, ...), custom_call_target="tpu_custom_call" | custom-call | flops 22000001024 | bytes 40000000 | tf_op jit(solution)/shard_map/corr/pallas_call | solution.py:170
  192.5 7.4 %collective-permute-start.32 = (bf16[512,1024]{1,0:T(8,128)(2,1)}, bf16[512,1024]{1,0:T(8,128)(2,1)S(1)}, u32[]{:S(2)}, u32[]{:S(2)}) collective-permute-start(bf16[512,1024]{1,0:T(8,128)(2,1)} %get-tuple-element.236), channel_id=1, source_target_pairs={{0,1},{1,0},{2,3},{3,2},{4,5},{5,4},{6,7},{7,6},{8,9},{9,8},{10,11... | collective-permute-start | bytes 3145736 | tf_op jit(solution)/shard_map/ppermute | solution.py:338
  199.9 2.5 collective-permute-done.32
  206.1 19.4 %corr.3 = (bf16[512,1024]{1,0:T(8,128)(2,1)}, bf16[512,1024]{1,0:T(8,128)(2,1)}, bf16[512,1024]{1,0:T(8,128)(2,1)}, bf16[512,1024]{1,0:T(8,128)(2,1)}) custom-call(s32[8]{0:T(128)} %stack.132.place, s32[4]{0:T(128)} %pad_add_fusion.order, bf16[64,48,128]{2,1,0:T(8,128)(2,1)} %copy-done.11, bf16[64,48,128]{2,1,0:T(8,128)(2,1)} %copy-done.23, ...), custom_call_target="tpu_custom_call" | custom-call | flops 22000001024 | bytes 40000000 | tf_op jit(solution)/shard_map/corr/pallas_call | solution.py:170
  225.5 3.0 %collective-permute-done.33.c = bf16[512,1024]{1,0:T(8,128)(2,1)S(1)} collective-permute-done((bf16[512,1024]{1,0:T(8,128)(2,1)S(1)}, bf16[512,1024]{1,0:T(8,128)(2,1)S(1)}, u32[]{:S(2)}, u32[]{:S(2)}) %collective-permute-start.33) | collective-permute-done | bytes 1048608 | tf_op jit(solution)/shard_map/ppermute | solution.py:342
  229.8 2.5 collective-permute-done.35
  235.9 4.0 %finish.2.refs_0_ = bf16[2,1024,512]{2,1,0:T(8,128)(2,1)} custom-call(bf16[512,1024]{1,0:T(8,128)(2,1)} %get-tuple-element.269.a, bf16[512,1024]{1,0:T(8,128)(2,1)} %copy-done.1, bf16[512,1024]{1,0:T(8,128)(2,1)} %copy-done), custom_call_target="tpu_custom_call" | custom-call | tf_op jit(solution)/shard_map/finish/pallas_call | solution.py:204
  240.0 18.4 %collective-permute-done.36.c = bf16[512,1024]{1,0:T(8,128)(2,1)S(1)} collective-permute-done((bf16[512,1024]{1,0:T(8,128)(2,1)S(1)}, bf16[512,1024]{1,0:T(8,128)(2,1)S(1)}, u32[]{:S(2)}, u32[]{:S(2)}) %collective-permute-start.36) | collective-permute-done | bytes 1048608 | tf_op jit(solution)/shard_map/ppermute | solution.py:342
  260.3 4.0 %finish.3 = bf16[2,1024,512]{2,1,0:T(8,128)(2,1)} custom-call(bf16[512,1024]{1,0:T(8,128)(2,1)} %get-tuple-element.260.a, bf16[512,1024]{1,0:T(8,128)(2,1)} %copy-done.3, bf16[512,1024]{1,0:T(8,128)(2,1)} %copy-done.2, bf16[2,1024,512]{2,1,0:T(8,128)(2,1)} %finish.2.refs_0_), custom_call_target="tpu_custom_call", output_to_operand_aliasing={{}: (3, {})} | custom-call | tf_op jit(solution)/shard_map/finish/pallas_call | solution.py:204
  (140 shorter events, 51.8 us)
Async XLA Ops:
  12.4 21.9 %collective-permute-start.1 = (bf16[64,48,128]{2,1,0:T(8,128)(2,1)}, bf16[64,48,128]{2,1,0:T(8,128)(2,1)S(1)}, u32[]{:S(2)}, u32[]{:S(2)}) collective-permute-start(bf16[64,48,128]{2,1,0:T(8,128)(2,1)} %get-tuple-element.148), channel_id=1, source_target_pairs={{0,64},{4,68},{8,72},{12,76},{16,80},{20,84},{24,88},{28,92},{32,9... | collective-permute-start | bytes 2359304 | tf_op jit(solution)/shard_map/ppermute | solution.py:230
  16.8 35.9 %collective-permute-start = (bf16[65,48,128]{2,1,0:T(8,128)(2,1)}, bf16[65,48,128]{2,1,0:T(8,128)(2,1)S(1)}, u32[]{:S(2)}, u32[]{:S(2)}) collective-permute-start(bf16[65,48,128]{2,1,0:T(8,128)(2,1)} %get-tuple-element.147.refs_2_), channel_id=1, source_target_pairs={{0,8},{4,12},{8,0},{12,4},{16,24},{20,28},{24,16},{28,20},{32,40},... | collective-permute-start | bytes 2396168 | tf_op jit(solution)/shard_map/ppermute | solution.py:226
  19.5 35.8 %collective-permute-start.2 = (bf16[65,48,128]{2,1,0:T(8,128)(2,1)}, bf16[65,48,128]{2,1,0:T(8,128)(2,1)S(1)}, u32[]{:S(2)}, u32[]{:S(2)}) collective-permute-start(bf16[65,48,128]{2,1,0:T(8,128)(2,1)} %get-tuple-element.149), channel_id=1, source_target_pairs={{0,4},{4,8},{8,12},{12,0},{16,20},{20,24},{24,28},{28,16},{32,36},... | collective-permute-start | bytes 2396168 | tf_op jit(solution)/shard_map/ppermute | solution.py:226
  19.9 35.5 %collective-permute-start.4 = (bf16[65,48,128]{2,1,0:T(8,128)(2,1)}, bf16[65,48,128]{2,1,0:T(8,128)(2,1)S(1)}, u32[]{:S(2)}, u32[]{:S(2)}) collective-permute-start(bf16[65,48,128]{2,1,0:T(8,128)(2,1)} %get-tuple-element.151), channel_id=1, source_target_pairs={{0,12},{4,0},{8,4},{12,8},{16,28},{20,16},{24,20},{28,24},{32,44},... | collective-permute-start | bytes 2396168 | tf_op jit(solution)/shard_map/ppermute | solution.py:226
  22.2 29.7 %collective-permute-start.3 = (bf16[64,48,128]{2,1,0:T(8,128)(2,1)}, bf16[64,48,128]{2,1,0:T(8,128)(2,1)}, u32[]{:S(2)}, u32[]{:S(2)}) collective-permute-start(bf16[64,48,128]{2,1,0:T(8,128)(2,1)} %get-tuple-element.150), channel_id=1, source_target_pairs={{0,32},{4,36},{8,40},{12,44},{16,48},{20,52},{24,56},{28,60},{32,6... | collective-permute-start | bytes 2359304 | tf_op jit(solution)/shard_map/ppermute | solution.py:230
  34.3 18.4 %collective-permute-start.5 = (bf16[64,48,128]{2,1,0:T(8,128)(2,1)}, bf16[64,48,128]{2,1,0:T(8,128)(2,1)}, u32[]{:S(2)}, u32[]{:S(2)}) collective-permute-start(bf16[64,48,128]{2,1,0:T(8,128)(2,1)} %get-tuple-element.152), channel_id=1, source_target_pairs={{0,96},{4,100},{8,104},{12,108},{16,112},{20,116},{24,120},{28,124... | collective-permute-start | bytes 2359304 | tf_op jit(solution)/shard_map/ppermute | solution.py:230
  62.3 21.3 %collective-permute-start.6 = (bf16[2,17,48,128]{3,2,1,0:T(8,128)(2,1)}, bf16[2,17,48,128]{3,2,1,0:T(8,128)(2,1)S(1)}, u32[]{:S(2)}, u32[]{:S(2)}) collective-permute-start(bf16[2,17,48,128]{3,2,1,0:T(8,128)(2,1)} %get-tuple-element.165), channel_id=1, source_target_pairs={{0,32},{4,36},{8,40},{12,44},{16,48},{20,52},{24,56},{28,60},{32,6... | collective-permute-start | bytes 1253384 | tf_op jit(solution)/shard_map/ppermute | solution.py:230
  63.1 20.6 %collective-permute-start.7 = (bf16[2,17,48,128]{3,2,1,0:T(8,128)(2,1)}, bf16[2,17,48,128]{3,2,1,0:T(8,128)(2,1)S(1)}, u32[]{:S(2)}, u32[]{:S(2)}) collective-permute-start(bf16[2,17,48,128]{3,2,1,0:T(8,128)(2,1)} %get-tuple-element.166), channel_id=1, source_target_pairs={{0,64},{4,68},{8,72},{12,76},{16,80},{20,84},{24,88},{28,92},{32,9... | collective-permute-start | bytes 1253384 | tf_op jit(solution)/shard_map/ppermute | solution.py:230
  66.2 17.7 %collective-permute-start.8 = (bf16[2,17,48,128]{3,2,1,0:T(8,128)(2,1)}, bf16[2,17,48,128]{3,2,1,0:T(8,128)(2,1)S(1)}, u32[]{:S(2)}, u32[]{:S(2)}) collective-permute-start(bf16[2,17,48,128]{3,2,1,0:T(8,128)(2,1)} %get-tuple-element.167), channel_id=1, source_target_pairs={{0,96},{4,100},{8,104},{12,108},{16,112},{20,116},{24,120},{28,124... | collective-permute-start | bytes 1253384 | tf_op jit(solution)/shard_map/ppermute | solution.py:230
  66.2 15.3 %collective-permute-start.11 = (bf16[2,16,48,128]{3,2,1,0:T(8,128)(2,1)}, bf16[2,16,48,128]{3,2,1,0:T(8,128)(2,1)S(1)}, u32[]{:S(2)}, u32[]{:S(2)}) collective-permute-start(bf16[2,16,48,128]{3,2,1,0:T(8,128)(2,1)} %get-tuple-element.170), channel_id=1, source_target_pairs={{0,12},{4,0},{8,4},{12,8},{16,28},{20,16},{24,20},{28,24},{32,44},... | collective-permute-start | bytes 1179656 | tf_op jit(solution)/shard_map/ppermute | solution.py:226
  85.3 18.9 %collective-permute-start.12 = (bf16[2,17,48,128]{3,2,1,0:T(8,128)(2,1)S(1)}, bf16[2,17,48,128]{3,2,1,0:T(8,128)(2,1)S(1)}, u32[]{:S(2)}, u32[]{:S(2)}) collective-permute-start(bf16[2,17,48,128]{3,2,1,0:T(8,128)(2,1)S(1)} %pad_maximum_fusion.4), channel_id=1, source_target_pairs={{0,16},{4,20},{8,24},{12,28},{16,0},{20,4},{24,8},{28,12},{32,48},... | collective-permute-start | bytes 1253384 | tf_op jit(solution)/shard_map/ppermute | solution.py:234
  88.3 15.9 %collective-permute-start.13 = (bf16[2,16,48,128]{3,2,1,0:T(8,128)(2,1)S(1)}, bf16[2,16,48,128]{3,2,1,0:T(8,128)(2,1)S(1)}, u32[]{:S(2)}, u32[]{:S(2)}) collective-permute-start(bf16[2,16,48,128]{3,2,1,0:T(8,128)(2,1)S(1)} %pad_maximum_fusion.5), channel_id=1, source_target_pairs={{0,16},{4,20},{8,24},{12,28},{16,0},{20,4},{24,8},{28,12},{32,48},... | collective-permute-start | bytes 1179656 | tf_op jit(solution)/shard_map/ppermute | solution.py:234
  107.4 19.7 %collective-permute-start.15 = (bf16[2,16,48,128]{3,2,1,0:T(8,128)(2,1)S(1)}, bf16[2,16,48,128]{3,2,1,0:T(8,128)(2,1)S(1)}, u32[]{:S(2)}, u32[]{:S(2)}) collective-permute-start(bf16[2,16,48,128]{3,2,1,0:T(8,128)(2,1)S(1)} %pad_maximum_fusion.7), channel_id=1, source_target_pairs={{0,8},{4,12},{8,0},{12,4},{16,24},{20,28},{24,16},{28,20},{32,40},... | collective-permute-start | bytes 1179656 | tf_op jit(solution)/shard_map/ppermute | solution.py:226
  108.9 18.3 %collective-permute-start.16 = (bf16[2,16,48,128]{3,2,1,0:T(8,128)(2,1)}, bf16[2,16,48,128]{3,2,1,0:T(8,128)(2,1)S(1)}, u32[]{:S(2)}, u32[]{:S(2)}) collective-permute-start(bf16[2,16,48,128]{3,2,1,0:T(8,128)(2,1)} %pad_maximum_fusion.6), channel_id=1, source_target_pairs={{0,32},{4,36},{8,40},{12,44},{16,48},{20,52},{24,56},{28,60},{32,6... | collective-permute-start | bytes 1179656 | tf_op jit(solution)/shard_map/ppermute | solution.py:230
  112.7 14.8 %collective-permute-start.17 = (bf16[2,16,48,128]{3,2,1,0:T(8,128)(2,1)S(1)}, bf16[2,16,48,128]{3,2,1,0:T(8,128)(2,1)S(1)}, u32[]{:S(2)}, u32[]{:S(2)}) collective-permute-start(bf16[2,16,48,128]{3,2,1,0:T(8,128)(2,1)S(1)} %pad_maximum_fusion.7), channel_id=1, source_target_pairs={{0,4},{4,8},{8,12},{12,0},{16,20},{20,24},{24,28},{28,16},{32,36},... | collective-permute-start | bytes 1179656 | tf_op jit(solution)/shard_map/ppermute | solution.py:226
  113.7 14.4 %collective-permute-start.18 = (bf16[2,16,48,128]{3,2,1,0:T(8,128)(2,1)}, bf16[2,16,48,128]{3,2,1,0:T(8,128)(2,1)S(1)}, u32[]{:S(2)}, u32[]{:S(2)}) collective-permute-start(bf16[2,16,48,128]{3,2,1,0:T(8,128)(2,1)} %pad_maximum_fusion.6), channel_id=1, source_target_pairs={{0,96},{4,100},{8,104},{12,108},{16,112},{20,116},{24,120},{28,124... | collective-permute-start | bytes 1179656 | tf_op jit(solution)/shard_map/ppermute | solution.py:230
  128.7 16.6 %collective-permute-start.20 = (bf16[64,48,128]{2,1,0:T(8,128)(2,1)S(1)}, bf16[64,48,128]{2,1,0:T(8,128)(2,1)}, u32[]{:S(2)}, u32[]{:S(2)}) collective-permute-start(bf16[64,48,128]{2,1,0:T(8,128)(2,1)S(1)} %pad_maximum_fusion.2.refs_0_), channel_id=1, source_target_pairs={{0,4},{4,8},{8,12},{12,0},{16,20},{20,24},{24,28},{28,16},{32,36},... | collective-permute-start | bytes 2359304 | tf_op jit(solution)/shard_map/ppermute | solution.py:226
  130.5 17.4 %collective-permute-start.21 = (bf16[64,48,128]{2,1,0:T(8,128)(2,1)S(1)}, bf16[64,48,128]{2,1,0:T(8,128)(2,1)}, u32[]{:S(2)}, u32[]{:S(2)}) collective-permute-start(bf16[64,48,128]{2,1,0:T(8,128)(2,1)S(1)} %pad_maximum_fusion.3.refs_4_), channel_id=1, source_target_pairs={{0,32},{4,36},{8,40},{12,44},{16,48},{20,52},{24,56},{28,60},{32,6... | collective-permute-start | bytes 2359304 | tf_op jit(solution)/shard_map/ppermute | solution.py:230
  132.5 15.7 %collective-permute-start.22 = (bf16[64,48,128]{2,1,0:T(8,128)(2,1)S(1)}, bf16[64,48,128]{2,1,0:T(8,128)(2,1)S(1)}, u32[]{:S(2)}, u32[]{:S(2)}) collective-permute-start(bf16[64,48,128]{2,1,0:T(8,128)(2,1)S(1)} %pad_maximum_fusion.2.refs_0_), channel_id=1, source_target_pairs={{0,12},{4,0},{8,4},{12,8},{16,28},{20,16},{24,20},{28,24},{32,44},... | collective-permute-start | bytes 2359304 | tf_op jit(solution)/shard_map/ppermute | solution.py:226
  135.1 15.1 %collective-permute-start.23 = (bf16[64,48,128]{2,1,0:T(8,128)(2,1)S(1)}, bf16[64,48,128]{2,1,0:T(8,128)(2,1)S(1)}, u32[]{:S(2)}, u32[]{:S(2)}) collective-permute-start(bf16[64,48,128]{2,1,0:T(8,128)(2,1)S(1)} %pad_maximum_fusion.3.refs_4_), channel_id=1, source_target_pairs={{0,96},{4,100},{8,104},{12,108},{16,112},{20,116},{24,120},{28,124... | collective-permute-start | bytes 2359304 | tf_op jit(solution)/shard_map/ppermute | solution.py:230
  150.2 15.7 %collective-permute-start.24 = (bf16[64,48,128]{2,1,0:T(8,128)(2,1)}, bf16[64,48,128]{2,1,0:T(8,128)(2,1)}, u32[]{:S(2)}, u32[]{:S(2)}) collective-permute-start(bf16[64,48,128]{2,1,0:T(8,128)(2,1)} %collective-permute-done.20.refs_1_), channel_id=1, source_target_pairs={{0,4},{4,8},{8,12},{12,0},{16,20},{20,24},{24,28},{28,16},{32,36},... | collective-permute-start | bytes 2359304 | tf_op jit(solution)/shard_map/ppermute | solution.py:226
  150.2 15.7 %collective-permute-start.25 = (bf16[64,48,128]{2,1,0:T(8,128)(2,1)}, bf16[64,48,128]{2,1,0:T(8,128)(2,1)}, u32[]{:S(2)}, u32[]{:S(2)}) collective-permute-start(bf16[64,48,128]{2,1,0:T(8,128)(2,1)} %collective-permute-done.21.refs_5_), channel_id=1, source_target_pairs={{0,32},{4,36},{8,40},{12,44},{16,48},{20,52},{24,56},{28,60},{32,6... | collective-permute-start | bytes 2359304 | tf_op jit(solution)/shard_map/ppermute | solution.py:230
  150.2 15.7 %collective-permute-start.26 = (bf16[64,48,128]{2,1,0:T(8,128)(2,1)S(1)}, bf16[64,48,128]{2,1,0:T(8,128)(2,1)S(1)}, u32[]{:S(2)}, u32[]{:S(2)}) collective-permute-start(bf16[64,48,128]{2,1,0:T(8,128)(2,1)S(1)} %pad_maximum_fusion.refs_0_), channel_id=1, source_target_pairs={{0,12},{4,0},{8,4},{12,8},{16,28},{20,16},{24,20},{28,24},{32,44},... | collective-permute-start | bytes 2359304 | tf_op jit(solution)/shard_map/ppermute | solution.py:226
  152.9 13.8 %collective-permute-start.27 = (bf16[64,48,128]{2,1,0:T(8,128)(2,1)S(1)}, bf16[64,48,128]{2,1,0:T(8,128)(2,1)S(1)}, u32[]{:S(2)}, u32[]{:S(2)}) collective-permute-start(bf16[64,48,128]{2,1,0:T(8,128)(2,1)S(1)} %pad_maximum_fusion.1.refs_4_), channel_id=1, source_target_pairs={{0,96},{4,100},{8,104},{12,108},{16,112},{20,116},{24,120},{28,124... | collective-permute-start | bytes 2359304 | tf_op jit(solution)/shard_map/ppermute | solution.py:230
  166.7 25.7 %collective-permute-start.28 = (bf16[64,48,128]{2,1,0:T(8,128)(2,1)S(1)}, bf16[64,48,128]{2,1,0:T(8,128)(2,1)S(1)}, u32[]{:S(2)}, u32[]{:S(2)}) collective-permute-start(bf16[64,48,128]{2,1,0:T(8,128)(2,1)S(1)} %pad_maximum_fusion.refs_0_), channel_id=1, source_target_pairs={{0,4},{4,8},{8,12},{12,0},{16,20},{20,24},{24,28},{28,16},{32,36},... | collective-permute-start | bytes 2359304 | tf_op jit(solution)/shard_map/ppermute | solution.py:226
  166.7 25.7 %collective-permute-start.29 = (bf16[64,48,128]{2,1,0:T(8,128)(2,1)S(1)}, bf16[64,48,128]{2,1,0:T(8,128)(2,1)S(1)}, u32[]{:S(2)}, u32[]{:S(2)}) collective-permute-start(bf16[64,48,128]{2,1,0:T(8,128)(2,1)S(1)} %pad_maximum_fusion.1.refs_4_), channel_id=1, source_target_pairs={{0,32},{4,36},{8,40},{12,44},{16,48},{20,52},{24,56},{28,60},{32,6... | collective-permute-start | bytes 2359304 | tf_op jit(solution)/shard_map/ppermute | solution.py:230
  166.7 25.7 %collective-permute-start.30 = (bf16[64,48,128]{2,1,0:T(8,128)(2,1)S(1)}, bf16[64,48,128]{2,1,0:T(8,128)(2,1)S(1)}, u32[]{:S(2)}, u32[]{:S(2)}) collective-permute-start(bf16[64,48,128]{2,1,0:T(8,128)(2,1)S(1)} %collective-permute-done.26.refs_2_), channel_id=1, source_target_pairs={{0,12},{4,0},{8,4},{12,8},{16,28},{20,16},{24,20},{28,24},{32,44},... | collective-permute-start | bytes 2359304 | tf_op jit(solution)/shard_map/ppermute | solution.py:226
  169.4 23.1 %collective-permute-start.31 = (bf16[64,48,128]{2,1,0:T(8,128)(2,1)S(1)}, bf16[64,48,128]{2,1,0:T(8,128)(2,1)S(1)}, u32[]{:S(2)}, u32[]{:S(2)}) collective-permute-start(bf16[64,48,128]{2,1,0:T(8,128)(2,1)S(1)} %collective-permute-done.27.refs_6_), channel_id=1, source_target_pairs={{0,96},{4,100},{8,104},{12,108},{16,112},{20,116},{24,120},{28,124... | collective-permute-start | bytes 2359304 | tf_op jit(solution)/shard_map/ppermute | solution.py:230
  204.0 24.5 %collective-permute-start.33 = (bf16[512,1024]{1,0:T(8,128)(2,1)S(1)}, bf16[512,1024]{1,0:T(8,128)(2,1)S(1)}, u32[]{:S(2)}, u32[]{:S(2)}) collective-permute-start(bf16[512,1024]{1,0:T(8,128)(2,1)S(1)} %add_convert_fusion.1), channel_id=1, source_target_pairs={{0,2},{1,3},{2,0},{3,1},{4,6},{5,7},{6,4},{7,5},{8,10},{9,11},{10,... | collective-permute-start | bytes 3145736 | tf_op jit(solution)/shard_map/ppermute | solution.py:342
  205.4 23.1 %collective-permute-start.34 = (bf16[512,1024]{1,0:T(8,128)(2,1)S(1)}, bf16[512,1024]{1,0:T(8,128)(2,1)S(1)}, u32[]{:S(2)}, u32[]{:S(2)}) collective-permute-start(bf16[512,1024]{1,0:T(8,128)(2,1)S(1)} %copy-done.17), channel_id=1, source_target_pairs={{0,1},{1,0},{2,3},{3,2},{4,5},{5,4},{6,7},{7,6},{8,9},{9,8},{10,11... | collective-permute-start | bytes 3145736 | tf_op jit(solution)/shard_map/ppermute | solution.py:338
  233.9 24.5 %collective-permute-start.36 = (bf16[512,1024]{1,0:T(8,128)(2,1)S(1)}, bf16[512,1024]{1,0:T(8,128)(2,1)S(1)}, u32[]{:S(2)}, u32[]{:S(2)}) collective-permute-start(bf16[512,1024]{1,0:T(8,128)(2,1)S(1)} %add_convert_fusion), channel_id=1, source_target_pairs={{0,2},{1,3},{2,0},{3,1},{4,6},{5,7},{6,4},{7,5},{8,10},{9,11},{10,... | collective-permute-start | bytes 3145736 | tf_op jit(solution)/shard_map/ppermute | solution.py:342
  235.3 23.1 %collective-permute-start.37 = (bf16[512,1024]{1,0:T(8,128)(2,1)S(1)}, bf16[512,1024]{1,0:T(8,128)(2,1)S(1)}, u32[]{:S(2)}, u32[]{:S(2)}) collective-permute-start(bf16[512,1024]{1,0:T(8,128)(2,1)S(1)} %copy-done.18), channel_id=1, source_target_pairs={{0,1},{1,0},{2,3},{3,2},{4,5},{5,4},{6,7},{7,6},{8,9},{9,8},{10,11... | collective-permute-start | bytes 3145736 | tf_op jit(solution)/shard_map/ppermute | solution.py:338
  (33 other events, 450.1 us)
